TPU v7x, 32 devices: a whole 2x2x4 slice. The times are simulated.
32 devices in a mesh: blk: 16 (over z, x, core), rep: 2 (over y).
Axes of the slice: x: 2, y: 2, z: 4, core: 2. Of those that a mesh axis runs over, the one named last changes fastest.
Arguments:
- features: float32 [16384, 256], P(('blk', 'rep')), may hold values from -6 to 6
- degrees: int32 [16384], P(('blk', 'rep')), may hold values from 8 to 120, as said below
- root_weight: float32 [256, 256], replicated, may hold values from -0.375 to 0.375
- neighbor_weight: float32 [256, 256], replicated, may hold values from -0.375 to 0.375
- bias: float32 [256], replicated, may hold values from -3 to 3
- tile_rows: int32 [16, 16, 16], P('blk', 'rep'), may hold values from 0 to 7
- tile_cols: int32 [16, 16, 16], P('blk', 'rep'), may hold values from 0 to 7
- tile_count: int32 [16, 16], P('blk', 'rep'), may hold values from 1 to 16, as said below
- edge_row: int32 [16, 16, 16, 256], P('blk', 'rep'), may hold values from 0 to 127
- edge_col: int32 [16, 16, 16, 256], P('blk', 'rep'), may hold values from 0 to 127
- edge_weight: int32 [16, 16, 16, 256], P('blk', 'rep'), may hold values from 1 to 4
Outputs:
- activated: float32 [16384, 256], P(('blk', 'rep'))
Inputs may be any that keep to these rules, and one draw needn't show every extreme that they name: `degrees`: degrees are whole numbers spread roughly evenly in the logarithm. `tile_count`: every row block and source offset has at least one used slot; some have all 16 used.
All inputs are finite; a program needn't handle non-finite values.
Results may differ from a plain program's by a relative error of at most 0.0003.
Values sent between devices are 32-bit elements; how exact they have to be, the bound alone decides.
No kernel may reach another device: no remote copies, remote signals or barrier semaphores. Data moves between devices by JAX's collectives and lax.ppermute only.
A program may use at most 64 MiB of HBM per device.

v0:
```python
import functools

import jax
import jax.numpy as jnp
from jax import lax
from jax.experimental import pallas as pl
from jax.experimental.pallas import tpu as pltpu
from jax.sharding import PartitionSpec as P

TILE = 128
UNROLL = 4
SMEM = pl.BlockSpec(memory_space=pltpu.SMEM)
VMEM = pl.BlockSpec(memory_space=pltpu.VMEM)


def bf16_pair(value):
    high = value.astype(jnp.bfloat16)
    low = (value - high.astype(jnp.float32)).astype(jnp.bfloat16)
    return high, low


def tile_matrix(edges, pair, slot, slots, live):
    rows = edges[pair, pl.ds(slot, 1), :]
    cols = edges[pair, pl.ds(slot + slots, 1), :]
    weights = edges[pair, pl.ds(slot + 2 * slots, 1), :]
    weights = jnp.where(live, weights, 0).astype(jnp.float32)
    index = lax.broadcasted_iota(jnp.int32, (TILE, rows.shape[1]), 0)
    row_hot = jnp.where(index == rows, 1.0, 0.0).astype(jnp.bfloat16)
    col_hot = jnp.where(index == cols, weights, 0.0).astype(jnp.bfloat16)
    matrix = lax.dot_general(
        row_hot, col_hot, (((1,), (1,)), ((), ())), preferred_element_type=jnp.float32
    )
    return jnp.concatenate(bf16_pair(matrix), axis=1)


def sum_kernel(sources, chunks, pieces, slots, first, split_out, *refs):
    pairs, place, meta = refs[:3]
    refs = refs[3:]
    blocks, refs = refs[: 2 * sources], refs[2 * sources :]
    count_x = sources * chunks * pieces
    parts, refs = refs[:count_x], refs[count_x:]
    if not first:
        before, refs = refs[:chunks], refs[chunks:]
    if split_out:
        count_out = 4 * chunks
        outs, refs = refs[:count_out], refs[count_out:]
        edges, sides, entries = refs[:3]
        sums = refs[3:]
    else:
        sums, refs = refs[:chunks], refs[chunks:]
        edges, sides, entries = refs
    tiles_here = sides.shape[1]
    tiles_per = sums[0].shape[1] // TILE

    for chunk in range(chunks):
        sums[chunk][...] = jnp.zeros_like(sums[chunk]) if first else before[chunk][...]

    used = jnp.int32(0)
    for number in range(2 * sources):
        edges[number] = blocks[number][0, : 3 * slots]
        pair = pairs[number]
        for slot in range(slots):
            column = meta[pair, slots + slot] - place[0]
            row = lax.rem(meta[pair, slot] + place[1], tiles_per)
            wanted = (slot < meta[pair, 2 * slots]) & (column >= 0) & (column < tiles_here)
            code = ((number * slots + slot) * tiles_here + column) * tiles_per + row
            entries[used] = jnp.where(wanted, code, 0)
            used = used + wanted.astype(jnp.int32)
    for extra in range(UNROLL - 1):
        entries[used + extra] = 0

    for source in range(sources):
        for chunk in range(chunks):
            for piece in range(pieces):
                part = parts[(source * chunks + chunk) * pieces + piece]
                size = min(part.shape[0], TILE)
                for start in range(0, part.shape[0], size):
                    at = piece * part.shape[0] + start
                    high, low = bf16_pair(part[start : start + size, :])
                    for half in range(2):
                        below = half * TILE + at % TILE
                        left = 2 * TILE * chunk
                        sides[source, at // TILE, below : below + size, left : left + TILE] = high
                        sides[source, at // TILE, below : below + size, left + TILE : left + 2 * TILE] = low

    def group(step, carry):
        for lane in range(UNROLL):
            entry = step * UNROLL + lane
            code = entries[entry]
            row = lax.rem(code, tiles_per)
            code = lax.div(code, tiles_per)
            column = lax.rem(code, tiles_here)
            code = lax.div(code, tiles_here)
            slot = lax.rem(code, slots)
            number = lax.div(code, slots)
            matrix = tile_matrix(edges, number, slot, slots, entry < used)
            result = jnp.dot(
                matrix, sides[lax.div(number, 2), column], preferred_element_type=jnp.float32
            )
            at = (lax.rem(number, 2), pl.ds(pl.multiple_of(row * TILE, TILE), TILE), slice(None))
            for chunk in range(chunks):
                left = 2 * TILE * chunk
                sums[chunk][at] += result[:, left : left + TILE] + result[:, left + TILE : left + 2 * TILE]
        return carry

    lax.fori_loop(0, lax.div(used + UNROLL - 1, UNROLL), group, 0)
    if split_out:
        half = sums[0].shape[1] // 2
        for chunk in range(chunks):
            for block in range(2):
                outs[4 * chunk + 2 * block][...] = sums[chunk][block, :half]
                outs[4 * chunk + 2 * block + 1][...] = sums[chunk][block, half:]


def add_sources(pairs, place, meta, edges, parts, before, rows, slots, split_out=False):
    sources, chunks, pieces = len(parts), len(parts[0]), len(parts[0][0])
    flat = [piece for source in parts for chunk in source for piece in chunk]
    width = flat[0].shape[1]
    tiles_here = pieces * flat[0].shape[0] // TILE
    first = before is None
    whole = jax.ShapeDtypeStruct((2, rows, width), jnp.float32)
    quarter = jax.ShapeDtypeStruct((rows // 2, width), jnp.float32)

    def picked(number):
        return pl.BlockSpec(
            (1,) + edges.shape[1:], lambda step, pair_ref, number=number: (pair_ref[number], 0, 0)
        )

    def full(shape):
        return pl.BlockSpec(shape, lambda step, pair_ref: (0,) * len(shape))

    olds = [] if first else list(before)
    outs = [quarter] * (4 * chunks) if split_out else [whole] * chunks
    scratch = [
        pltpu.VMEM((2 * sources, 3 * slots, edges.shape[2]), jnp.int32),
        pltpu.VMEM((sources, tiles_here, 2 * TILE, 2 * TILE * chunks), jnp.bfloat16),
        pltpu.SMEM((2 * sources * slots + UNROLL,), jnp.int32),
    ]
    if split_out:
        scratch += [pltpu.VMEM(whole.shape, jnp.float32)] * chunks
    flops = 2 * sources * 8 * 2 * TILE * TILE * (256 + 4 * TILE * chunks)
    return pl.pallas_call(
        functools.partial(sum_kernel, sources, chunks, pieces, slots, first, split_out),
        grid_spec=pltpu.PrefetchScalarGridSpec(
            num_scalar_prefetch=1,
            grid=(1,),
            in_specs=[SMEM, SMEM]
            + [picked(number) for number in range(2 * sources)]
            + [full(part.shape) for part in flat]
            + [full(old.shape) for old in olds],
            out_specs=[full(out.shape) for out in outs],
            scratch_shapes=scratch,
        ),
        out_shape=outs,
        compiler_params=pltpu.CompilerParams(vmem_limit_bytes=24 << 20),
        cost_estimate=pl.CostEstimate(flops=flops, bytes_accessed=4 << 20, transcendentals=0),
    )(pairs, place, meta, *([edges] * (2 * sources)), *flat, *olds)


def on_device(
    features,
    degrees,
    root_weight,
    neighbor_weight,
    bias,
    tile_rows,
    tile_cols,
    tile_count,
    edge_row,
    edge_col,
    edge_weight,
):
    highest = lax.Precision.HIGHEST
    groups, blocks = lax.axis_size("rep"), lax.axis_size("blk")
    lanes = blocks // 2
    layers = lanes // 2
    arc, slots, listed = edge_row.shape[1:]
    per = arc // 2
    shard, width = features.shape
    rows = shard * groups
    chunks, pieces = width // TILE, 2
    block, replica = lax.axis_index("blk"), lax.axis_index("rep")
    chip, core = block // 2, block % 2

    def chip_at(position):
        return 2 * position if position < layers else 2 * (lanes - 1 - position) + 1

    def ring(value, step):
        pairs = [
            (2 * chip_at(p) + c, 2 * chip_at((p + step) % lanes) + c) for p in range(lanes) for c in range(2)
        ]
        return lax.ppermute(value, "blk", pairs)

    def core_swap(value):
        return lax.ppermute(value, "blk", [(b, b ^ 1) for b in range(blocks)])

    def rep_swap(value):
        return lax.ppermute(value, "rep", [(0, 1), (1, 0)])

    scale = lax.rsqrt(degrees.astype(jnp.float32))
    scaled = features * scale[:, None]
    cut = shard // pieces
    own = [
        [scaled[h * cut : (h + 1) * cut, f * TILE : (f + 1) * TILE] for h in range(pieces)] for f in range(chunks)
    ]

    def bundle(start):
        lists = [array[0, start::2] for array in (edge_row, edge_col, edge_weight)]
        head = jnp.concatenate(
            [tile_rows[0, start::2], tile_cols[0, start::2], tile_count[0, start::2, None]], axis=1
        )
        head = jnp.pad(head, ((0, 0), (0, listed - head.shape[1])))[:, None]
        head = jnp.pad(head, ((0, 0), (0, 7), (0, 0)))
        return jnp.concatenate(lists + [head], axis=1)

    own_lists = bundle(0)
    sibling_lists = core_swap(bundle(1))
    if groups == 2:
        gathered = [own_lists, rep_swap(own_lists), sibling_lists, rep_swap(sibling_lists)]
    else:
        gathered = [lax.all_gather(lists, "rep", axis=0, tiled=True) for lists in (own_lists, sibling_lists)]
    edges = jnp.concatenate(gathered, axis=0)
    meta = edges[:, 3 * slots, :TILE]

    def list_place(offset):
        group = offset // per
        group = group ^ replica if groups == 2 else group
        return group * per + offset % per

    position = jnp.where(chip % 2 == 0, chip // 2, lanes - 1 - chip // 2)

    def pairs_of(distances):
        places = []
        for distance in distances:
            there = (position + distance + lanes) % lanes
            source = jnp.where(there < layers, 2 * there, 2 * (lanes - 1 - there) + 1)
            places.append(list_place((chip - source + lanes) % lanes))
            places.append(groups * per + list_place((chip - source - core + lanes) % lanes))
        return jnp.stack(places).astype(jnp.int32)

    tiles_per = rows // TILE
    tiles_here = shard // TILE
    rotation = (tiles_per - replica * tiles_here) if groups == 2 else 0 * replica
    place = jnp.stack([replica * tiles_here, rotation]).astype(jnp.int32)
    add = functools.partial(add_sources, rows=rows, slots=slots)

    root = jnp.dot(features, root_weight, precision=highest) + bias

    up, down = own, own
    totals = None
    for step in range(1, lanes // 2 + 1):
        last = step == lanes // 2
        up = [[ring(v, 1) if h == 0 or not last else None for h, v in enumerate(f)] for f in up]
        down = [[ring(v, -1) if h == 1 or not last else None for h, v in enumerate(f)] for f in down]
        if step == 1:
            totals = add(pairs_of([0]), place, meta, edges, [own], None)
        if not last:
            totals = add(pairs_of([-step, step]), place, meta, edges, [up, down], totals)
    pairs = pairs_of([lanes // 2])
    hidden = root
    for f in range(chunks):
        ends = add(pairs, place, meta, edges, [[[up[f][0], down[f][1]]]], [totals[f]], split_out=True)
        own_mine, own_other, sibling_mine, sibling_other = ends
        if groups == 2:
            other = rep_swap(own_other + core_swap(sibling_other))
            share = own_mine + core_swap(sibling_mine) + other
        else:
            mine = jnp.concatenate([own_mine, own_other], 0) + core_swap(
                jnp.concatenate([sibling_mine, sibling_other], 0)
            )
            share = lax.psum_scatter(mine, "rep", scatter_dimension=0, tiled=True)
        mixed = share * scale[:, None]
        hidden = hidden + jnp.dot(mixed, neighbor_weight[f * TILE : (f + 1) * TILE], precision=highest)
    return jax.nn.relu(hidden)


def solution(mesh):
    placed = (
        P(("blk", "rep"), None),
        P(("blk", "rep")),
        P(),
        P(),
        P(),
        P("blk", "rep", None),
        P("blk", "rep", None),
        P("blk", "rep"),
        P("blk", "rep", None, None),
        P("blk", "rep", None, None),
        P("blk", "rep", None, None),
    )
    return jax.shard_map(
        on_device, mesh=mesh, in_specs=placed, out_specs=P(("blk", "rep"), None), check_vma=False
    )
```

profile of v0, /device:TPU:14, one launch (start us, length us, event | category | flops | bytes accessed | tf_op | source)
XLA Modules:
  0.0 105.4 jit_solution(15604590883648929502)
XLA Ops:
  0.7 1.2 %broadcast_multiply_fusion = f32[512,256]{1,0:T(8,128)S(1)} fusion(f32[512,256]{1,0:T(8,128)} %param.11, f32[512]{0:T(512)S(1)} %convert_rsqrt_fusion), kind=kLoop, calls=%fused_computation.12 | loop fusion | flops 131072 | bytes 1050624 | tf_op jit(solution)/shard_map/mul | solution.py:201
  2.5 1.6 %collective-permute-start.23 = (f32[256,128]{1,0:T(8,128)S(1)}, f32[256,128]{1,0:T(8,128)S(1)}, u32[]{:S(2)}, u32[]{:S(2)}) collective-permute-start(f32[256,128]{1,0:T(8,128)S(1)} %get-tuple-element.39.refs_7_), channel_id=1, source_target_pairs={{0,4},{2,6},{8,0},{10,2},{16,8},{18,10},{24,16},{26,18},{28,24},{3... | collective-permute-start | bytes 393224 | tf_op jit(solution)/shard_map/ppermute | solution.py:192
  4.5 1.6 %collective-permute-start.26 = (f32[256,128]{1,0:T(8,128)S(1)}, f32[256,128]{1,0:T(8,128)S(1)}, u32[]{:S(2)}, u32[]{:S(2)}) collective-permute-start(f32[256,128]{1,0:T(8,128)S(1)} %get-tuple-element.38.refs_8_), channel_id=1, source_target_pairs={{0,4},{2,6},{8,0},{10,2},{16,8},{18,10},{24,16},{26,18},{28,24},{3... | collective-permute-start | bytes 393224 | tf_op jit(solution)/shard_map/ppermute | solution.py:192
  9.5 3.4 %collective-permute-done.11.refs_8_ = f32[256,128]{1,0:T(8,128)S(1)} collective-permute-done((f32[256,128]{1,0:T(8,128)S(1)}, f32[256,128]{1,0:T(8,128)S(1)}, u32[]{:S(2)}, u32[]{:S(2)}) %collective-permute-start.11) | collective-permute-done | bytes 131104 | tf_op jit(solution)/shard_map/ppermute | solution.py:192
  12.9 1.6 %collective-permute-start.20 = (f32[256,128]{1,0:T(8,128)S(1)}, f32[256,128]{1,0:T(8,128)S(1)}, u32[]{:S(2)}, u32[]{:S(2)}) collective-permute-start(f32[256,128]{1,0:T(8,128)S(1)} %get-tuple-element.40.refs_5_), channel_id=1, source_target_pairs={{0,4},{2,6},{8,0},{10,2},{16,8},{18,10},{24,16},{26,18},{28,24},{3... | collective-permute-start | bytes 393224 | tf_op jit(solution)/shard_map/ppermute | solution.py:192
  15.8 1.6 %collective-permute-start.7 = (f32[256,128]{1,0:T(8,128)S(1)}, f32[256,128]{1,0:T(8,128)S(1)}, u32[]{:S(2)}, u32[]{:S(2)}) collective-permute-start(f32[256,128]{1,0:T(8,128)S(1)} %get-tuple-element.37.refs_6_), channel_id=1, source_target_pairs={{0,4},{2,6},{8,0},{10,2},{16,8},{18,10},{24,16},{26,18},{28,24},{3... | collective-permute-start | bytes 393224 | tf_op jit(solution)/shard_map/ppermute | solution.py:192
  17.3 1.6 %collective-permute-done.20.refs_11_ = f32[256,128]{1,0:T(8,128)S(1)} collective-permute-done((f32[256,128]{1,0:T(8,128)S(1)}, f32[256,128]{1,0:T(8,128)S(1)}, u32[]{:S(2)}, u32[]{:S(2)}) %collective-permute-start.20) | collective-permute-done | bytes 131104 | tf_op jit(solution)/shard_map/ppermute | solution.py:192
  20.7 1.5 %collective-permute-start.18 = (f32[256,128]{1,0:T(8,128)S(1)}, f32[256,128]{1,0:T(8,128)S(1)}, u32[]{:S(2)}, u32[]{:S(2)}) collective-permute-start(f32[256,128]{1,0:T(8,128)S(1)} %collective-permute-done.17.refs_10_), channel_id=1, source_target_pairs={{0,8},{2,10},{8,16},{10,18},{16,24},{18,26},{24,28},{26,30},{28,20... | collective-permute-start | bytes 393224 | tf_op jit(solution)/shard_map/ppermute | solution.py:192
  22.2 2.7 %collective-permute-done = s32[4,56,256]{2,1,0:T(8,128)S(1)} collective-permute-done((s32[4,56,256]{2,1,0:T(8,128)S(1)}, s32[4,56,256]{2,1,0:T(8,128)S(1)}, u32[]{:S(2)}, u32[]{:S(2)}) %collective-permute-start) | collective-permute-done | bytes 229408 | tf_op jit(solution)/shard_map/ppermute | solution.py:198
  24.9 1.6 %collective-permute-start.21 = (f32[256,128]{1,0:T(8,128)S(1)}, f32[256,128]{1,0:T(8,128)S(1)}, u32[]{:S(2)}, u32[]{:S(2)}) collective-permute-start(f32[256,128]{1,0:T(8,128)S(1)} %collective-permute-done.20.refs_11_), channel_id=1, source_target_pairs={{0,4},{2,6},{8,0},{10,2},{16,8},{18,10},{24,16},{26,18},{28,24},{3... | collective-permute-start | bytes 393224 | tf_op jit(solution)/shard_map/ppermute | solution.py:192
  26.5 1.6 %collective-permute-start.27 = (f32[256,128]{1,0:T(8,128)S(1)}, f32[256,128]{1,0:T(8,128)S(1)}, u32[]{:S(2)}, u32[]{:S(2)}) collective-permute-start(f32[256,128]{1,0:T(8,128)S(1)} %collective-permute-done.26.refs_14_), channel_id=1, source_target_pairs={{0,4},{2,6},{8,0},{10,2},{16,8},{18,10},{24,16},{26,18},{28,24},{3... | collective-permute-start | bytes 393224 | tf_op jit(solution)/shard_map/ppermute | solution.py:192
  28.6 1.5 %collective-permute-start.2 = (s32[4,56,256]{2,1,0:T(8,128)S(1)}, s32[4,56,256]{2,1,0:T(8,128)}, u32[]{:S(2)}, u32[]{:S(2)}) collective-permute-start(s32[4,56,256]{2,1,0:T(8,128)S(1)} %collective-permute-done.1), channel_id=1, source_target_pairs={{0,1},{1,0},{2,3},{3,2},{4,5},{5,4},{6,7},{7,6},{8,9},{9,8},{10,11... | collective-permute-start | bytes 688136 | tf_op jit(solution)/shard_map/ppermute | solution.py:198
  31.4 1.6 %collective-permute-start.24 = (f32[256,128]{1,0:T(8,128)S(1)}, f32[256,128]{1,0:T(8,128)S(1)}, u32[]{:S(2)}, u32[]{:S(2)}) collective-permute-start(f32[256,128]{1,0:T(8,128)S(1)} %collective-permute-done.23.refs_13_), channel_id=1, source_target_pairs={{0,4},{2,6},{8,0},{10,2},{16,8},{18,10},{24,16},{26,18},{28,24},{3... | collective-permute-start | bytes 393224 | tf_op jit(solution)/shard_map/ppermute | solution.py:192
  33.0 1.6 %collective-permute-start.8 = (f32[256,128]{1,0:T(8,128)S(1)}, f32[256,128]{1,0:T(8,128)S(1)}, u32[]{:S(2)}, u32[]{:S(2)}) collective-permute-start(f32[256,128]{1,0:T(8,128)S(1)} %collective-permute-done.7.refs_12_), channel_id=1, source_target_pairs={{0,4},{2,6},{8,0},{10,2},{16,8},{18,10},{24,16},{26,18},{28,24},{3... | collective-permute-start | bytes 393224 | tf_op jit(solution)/shard_map/ppermute | solution.py:192
  35.0 1.6 %collective-permute-start.28 = (f32[256,128]{1,0:T(8,128)S(1)}, f32[256,128]{1,0:T(8,128)S(1)}, u32[]{:S(2)}, u32[]{:S(2)}) collective-permute-start(f32[256,128]{1,0:T(8,128)S(1)} %collective-permute-done.27.refs_14_), channel_id=1, source_target_pairs={{0,4},{2,6},{8,0},{10,2},{16,8},{18,10},{24,16},{26,18},{28,24},{3... | collective-permute-start | bytes 393224 | tf_op jit(solution)/shard_map/ppermute | solution.py:192
  37.0 1.0 pad_add_fusion.refs_3_.refs_4_.refs_5_.refs_6_
  38.1 2.6 %collective-permute-done.8.refs_12_ = f32[256,128]{1,0:T(8,128)S(1)} collective-permute-done((f32[256,128]{1,0:T(8,128)S(1)}, f32[256,128]{1,0:T(8,128)S(1)}, u32[]{:S(2)}, u32[]{:S(2)}) %collective-permute-start.8) | collective-permute-done | bytes 131104 | tf_op jit(solution)/shard_map/ppermute | solution.py:192
  40.6 1.6 %collective-permute-start.9 = (f32[256,128]{1,0:T(8,128)S(1)}, f32[256,128]{1,0:T(8,128)S(1)}, u32[]{:S(2)}, u32[]{:S(2)}) collective-permute-start(f32[256,128]{1,0:T(8,128)S(1)} %collective-permute-done.8.refs_12_), channel_id=1, source_target_pairs={{0,4},{2,6},{8,0},{10,2},{16,8},{18,10},{24,16},{26,18},{28,24},{3... | collective-permute-start | bytes 393224 | tf_op jit(solution)/shard_map/ppermute | solution.py:192
  42.7 4.9 %shard_map.109 = (f32[2,1024,128]{2,1,0:T(8,128)S(1)}, f32[2,1024,128]{2,1,0:T(8,128)S(1)}) custom-call(s32[2]{0:T(128)S(1)} %pad_add_fusion.10.refs_0_, s32[2]{0:T(128)S(1)} %pad_add_fusion.6.refs_1_, s32[16,128]{1,0:T(8,128)S(1)} %bitcast.39, s32[16,56,256]{2,1,0:T(8,128)S(1)} %pad_add_fusion.refs_3_.refs_4_.refs_5_.refs_6_, ...), custom_call_target="tpu_custom_call" | custom-call | flops 671088640 | bytes 4194304 | tf_op jit(solution)/shard_map/pallas_call | solution.py:142
  47.6 2.0 %collective-permute-start.22 = (f32[256,128]{1,0:T(8,128)S(1)}, f32[256,128]{1,0:T(8,128)S(1)}, u32[]{:S(2)}, u32[]{:S(2)}) collective-permute-start(f32[256,128]{1,0:T(8,128)S(1)} %collective-permute-done.21.refs_11_), channel_id=1, source_target_pairs={{0,4},{2,6},{8,0},{10,2},{16,8},{18,10},{24,16},{26,18},{28,24},{3... | collective-permute-start | bytes 393224 | tf_op jit(solution)/shard_map/ppermute | solution.py:192
  50.0 10.4 %shard_map.110 = (f32[2,1024,128]{2,1,0:T(8,128)S(1)}, f32[2,1024,128]{2,1,0:T(8,128)S(1)}) custom-call(s32[4]{0:T(128)S(1)} %pad_add_fusion.9.refs_0_, s32[2]{0:T(128)S(1)} %pad_add_fusion.6.refs_1_, s32[16,128]{1,0:T(8,128)S(1)} %bitcast.40, s32[16,56,256]{2,1,0:T(8,128)S(1)} %pad_add_fusion.refs_3_.refs_4_.refs_5_.refs_6_, ...), custom_call_target="tpu_custom_call" | custom-call | flops 1342177280 | bytes 4194304 | tf_op jit(solution)/shard_map/pallas_call | solution.py:142
  60.4 1.7 %collective-permute-start.32 = (f32[256,128]{1,0:T(8,128)S(1)}, f32[256,128]{1,0:T(8,128)S(1)}, u32[]{:S(2)}, u32[]{:S(2)}) collective-permute-start(f32[256,128]{1,0:T(8,128)S(1)} %collective-permute-done.16.refs_9_), channel_id=1, source_target_pairs={{0,8},{2,10},{8,16},{10,18},{16,24},{18,26},{24,28},{26,30},{28,20... | collective-permute-start | bytes 393224 | tf_op jit(solution)/shard_map/ppermute | solution.py:192
  62.5 10.4 %shard_map.111 = (f32[2,1024,128]{2,1,0:T(8,128)S(1)}, f32[2,1024,128]{2,1,0:T(8,128)S(1)}) custom-call(s32[4]{0:T(128)S(1)} %pad_add_fusion.8.refs_0_, s32[2]{0:T(128)S(1)} %pad_add_fusion.6.refs_1_, s32[16,128]{1,0:T(8,128)S(1)} %bitcast.41, s32[16,56,256]{2,1,0:T(8,128)S(1)} %pad_add_fusion.refs_3_.refs_4_.refs_5_.refs_6_, ...), custom_call_target="tpu_custom_call" | custom-call | flops 1342177280 | bytes 4194304 | tf_op jit(solution)/shard_map/pallas_call | solution.py:142
  72.9 2.0 %collective-permute-start.6 = (f32[256,128]{1,0:T(8,128)S(1)}, f32[256,128]{1,0:T(8,128)S(1)}, u32[]{:S(2)}, u32[]{:S(2)}) collective-permute-start(f32[256,128]{1,0:T(8,128)S(1)} %collective-permute-done.5.refs_7_), channel_id=1, source_target_pairs={{0,8},{2,10},{8,16},{10,18},{16,24},{18,26},{24,28},{26,30},{28,20... | collective-permute-start | bytes 393224 | tf_op jit(solution)/shard_map/ppermute | solution.py:192
  74.9 7.0 %shard_map.112 = (f32[2,1024,128]{2,1,0:T(8,128)S(1)}, f32[2,1024,128]{2,1,0:T(8,128)S(1)}) custom-call(s32[4]{0:T(128)S(1)} %pad_add_fusion.7.refs_0_, s32[2]{0:T(128)S(1)} %pad_add_fusion.6.refs_1_, s32[16,128]{1,0:T(8,128)S(1)} %bitcast.42, s32[16,56,256]{2,1,0:T(8,128)S(1)} %pad_add_fusion.refs_3_.refs_4_.refs_5_.refs_6_, ...), custom_call_target="tpu_custom_call" | custom-call | flops 1342177280 | bytes 4194304 | tf_op jit(solution)/shard_map/pallas_call | solution.py:142
  82.0 2.8 %shard_map.114 = (f32[512,128]{1,0:T(8,128)S(1)}, f32[512,128]{1,0:T(8,128)S(1)}, f32[512,128]{1,0:T(8,128)S(1)}, f32[512,128]{1,0:T(8,128)S(1)}) custom-call(s32[2]{0:T(128)S(1)} %pad_add_fusion.5.refs_0_, s32[2]{0:T(128)S(1)} %pad_add_fusion.6.refs_1_, s32[16,128]{1,0:T(8,128)S(1)} %bitcast.43, ...), custom_call_target="tpu_custom_call" | custom-call | flops 402653184 | bytes 4194304 | tf_op jit(solution)/shard_map/pallas_call | solution.py:142
  84.9 2.8 %shard_map.113 = (f32[512,128]{1,0:T(8,128)S(1)}, f32[512,128]{1,0:T(8,128)S(1)}, f32[512,128]{1,0:T(8,128)S(1)}, f32[512,128]{1,0:T(8,128)S(1)}) custom-call(s32[2]{0:T(128)S(1)} %pad_add_fusion.5.refs_0_, s32[2]{0:T(128)S(1)} %pad_add_fusion.6.refs_1_, s32[16,128]{1,0:T(8,128)S(1)} %bitcast.44, ...), custom_call_target="tpu_custom_call" | custom-call | flops 402653184 | bytes 4194304 | tf_op jit(solution)/shard_map/pallas_call | solution.py:142
  87.7 1.8 %collective-permute-start.30 = (f32[512,128]{1,0:T(8,128)S(1)}, f32[512,128]{1,0:T(8,128)S(1)}, u32[]{:S(2)}, u32[]{:S(2)}) collective-permute-start(f32[512,128]{1,0:T(8,128)S(1)} %get-tuple-element.31), channel_id=1, source_target_pairs={{0,2},{2,0},{4,6},{6,4},{8,10},{10,8},{12,14},{14,12},{16,18},{18,... | collective-permute-start | bytes 786440 | tf_op jit(solution)/shard_map/ppermute | solution.py:195
  90.8 1.3 %collective-permute-start.31 = (f32[512,128]{1,0:T(8,128)S(1)}, f32[512,128]{1,0:T(8,128)S(1)}, u32[]{:S(2)}, u32[]{:S(2)}) collective-permute-start(f32[512,128]{1,0:T(8,128)S(1)} %add.475), channel_id=1, source_target_pairs={{0,1},{1,0},{2,3},{3,2},{4,5},{5,4},{6,7},{7,6},{8,9},{9,8},{10,11... | collective-permute-start | bytes 786440 | tf_op jit(solution)/shard_map/ppermute | solution.py:198
  92.7 6.2 %collective-permute-done.36 = f32[512,128]{1,0:T(8,128)S(1)} collective-permute-done((f32[512,128]{1,0:T(8,128)S(1)}, f32[512,128]{1,0:T(8,128)S(1)}, u32[]{:S(2)}, u32[]{:S(2)}) %collective-permute-start.36) | collective-permute-done | bytes 262176 | tf_op jit(solution)/shard_map/ppermute | solution.py:198
  99.5 4.5 %collective-permute-done.31 = f32[512,128]{1,0:T(8,128)S(1)} collective-permute-done((f32[512,128]{1,0:T(8,128)S(1)}, f32[512,128]{1,0:T(8,128)S(1)}, u32[]{:S(2)}, u32[]{:S(2)}) %collective-permute-start.31) | collective-permute-done | bytes 262176 | tf_op jit(solution)/shard_map/ppermute | solution.py:198
  104.0 1.4 %fusion.1 = f32[512,256]{1,0:T(8,128)} fusion(f32[512,256]{1,0:T(8,128)S(1)} %fusion.2, f32[512,256]{1,0:T(8,128)S(1)} %convolution_add_fusion.1, f32[512,128]{1,0:T(8,128)S(1)} %collective-permute-done.31, f32[512,128]{1,0:T(8,128)S(1)} %get-tuple-element.28, f32[512,128]{1,0:T(8,128)S(1)} %collective-permute-done.29, f32[256,256]{1,0:T(8,128)S(1)} %copy-done.2, ...), kind=kOutput, calls=%fused_computation.2 | convolution fusion | flops 201916416 | bytes 2492416 | tf_op jit(solution)/shard_map/dot_general | solution.py:273
  (103 shorter events, 13.9 us)
Async XLA Ops:
  2.0 12.5 %collective-permute-start.14 = (f32[256,128]{1,0:T(8,128)S(1)}, f32[256,128]{1,0:T(8,128)S(1)}, u32[]{:S(2)}, u32[]{:S(2)}) collective-permute-start(f32[256,128]{1,0:T(8,128)S(1)} %get-tuple-element.39.refs_7_), channel_id=1, source_target_pairs={{0,8},{2,10},{8,16},{10,18},{16,24},{18,26},{24,28},{26,30},{28,20... | collective-permute-start | bytes 393224 | tf_op jit(solution)/shard_map/ppermute | solution.py:192
  2.5 17.0 %collective-permute-start.23 = (f32[256,128]{1,0:T(8,128)S(1)}, f32[256,128]{1,0:T(8,128)S(1)}, u32[]{:S(2)}, u32[]{:S(2)}) collective-permute-start(f32[256,128]{1,0:T(8,128)S(1)} %get-tuple-element.39.refs_7_), channel_id=1, source_target_pairs={{0,4},{2,6},{8,0},{10,2},{16,8},{18,10},{24,16},{26,18},{28,24},{3... | collective-permute-start | bytes 393224 | tf_op jit(solution)/shard_map/ppermute | solution.py:192
  4.0 11.7 %collective-permute-start.17 = (f32[256,128]{1,0:T(8,128)S(1)}, f32[256,128]{1,0:T(8,128)S(1)}, u32[]{:S(2)}, u32[]{:S(2)}) collective-permute-start(f32[256,128]{1,0:T(8,128)S(1)} %get-tuple-element.38.refs_8_), channel_id=1, source_target_pairs={{0,8},{2,10},{8,16},{10,18},{16,24},{18,26},{24,28},{26,30},{28,20... | collective-permute-start | bytes 393224 | tf_op jit(solution)/shard_map/ppermute | solution.py:192
  4.5 14.9 %collective-permute-start.26 = (f32[256,128]{1,0:T(8,128)S(1)}, f32[256,128]{1,0:T(8,128)S(1)}, u32[]{:S(2)}, u32[]{:S(2)}) collective-permute-start(f32[256,128]{1,0:T(8,128)S(1)} %get-tuple-element.38.refs_8_), channel_id=1, source_target_pairs={{0,4},{2,6},{8,0},{10,2},{16,8},{18,10},{24,16},{26,18},{28,24},{3... | collective-permute-start | bytes 393224 | tf_op jit(solution)/shard_map/ppermute | solution.py:192
  6.1 6.8 %collective-permute-start.11 = (f32[256,128]{1,0:T(8,128)S(1)}, f32[256,128]{1,0:T(8,128)S(1)}, u32[]{:S(2)}, u32[]{:S(2)}) collective-permute-start(f32[256,128]{1,0:T(8,128)S(1)} %get-tuple-element.37.refs_6_), channel_id=1, source_target_pairs={{0,8},{2,10},{8,16},{10,18},{16,24},{18,26},{24,28},{26,30},{28,20... | collective-permute-start | bytes 393224 | tf_op jit(solution)/shard_map/ppermute | solution.py:192
  12.9 6.0 %collective-permute-start.20 = (f32[256,128]{1,0:T(8,128)S(1)}, f32[256,128]{1,0:T(8,128)S(1)}, u32[]{:S(2)}, u32[]{:S(2)}) collective-permute-start(f32[256,128]{1,0:T(8,128)S(1)} %get-tuple-element.40.refs_5_), channel_id=1, source_target_pairs={{0,4},{2,6},{8,0},{10,2},{16,8},{18,10},{24,16},{26,18},{28,24},{3... | collective-permute-start | bytes 393224 | tf_op jit(solution)/shard_map/ppermute | solution.py:192
  18.9 6.0 %collective-permute-start = (s32[4,56,256]{2,1,0:T(8,128)S(1)}, s32[4,56,256]{2,1,0:T(8,128)S(1)}, u32[]{:S(2)}, u32[]{:S(2)}) collective-permute-start(s32[4,56,256]{2,1,0:T(8,128)S(1)} %pad_add_fusion.2), channel_id=1, source_target_pairs={{0,1},{1,0},{2,3},{3,2},{4,5},{5,4},{6,7},{7,6},{8,9},{9,8},{10,11... | collective-permute-start | bytes 688136 | tf_op jit(solution)/shard_map/ppermute | solution.py:198
  19.4 7.1 %collective-permute-start.1 = (s32[4,56,256]{2,1,0:T(8,128)}, s32[4,56,256]{2,1,0:T(8,128)S(1)}, u32[]{:S(2)}, u32[]{:S(2)}) collective-permute-start(s32[4,56,256]{2,1,0:T(8,128)} %pad_add_fusion.1), channel_id=1, source_target_pairs={{0,2},{2,0},{4,6},{6,4},{8,10},{10,8},{12,14},{14,12},{16,18},{18,... | collective-permute-start | bytes 688136 | tf_op jit(solution)/shard_map/ppermute | solution.py:195
  19.4 8.7 %collective-permute-start.12 = (f32[256,128]{1,0:T(8,128)S(1)}, f32[256,128]{1,0:T(8,128)S(1)}, u32[]{:S(2)}, u32[]{:S(2)}) collective-permute-start(f32[256,128]{1,0:T(8,128)S(1)} %collective-permute-done.11.refs_8_), channel_id=1, source_target_pairs={{0,8},{2,10},{8,16},{10,18},{16,24},{18,26},{24,28},{26,30},{28,20... | collective-permute-start | bytes 393224 | tf_op jit(solution)/shard_map/ppermute | solution.py:192
  19.9 8.7 %collective-permute-start.15 = (f32[256,128]{1,0:T(8,128)S(1)}, f32[256,128]{1,0:T(8,128)S(1)}, u32[]{:S(2)}, u32[]{:S(2)}) collective-permute-start(f32[256,128]{1,0:T(8,128)S(1)} %collective-permute-done.14.refs_9_), channel_id=1, source_target_pairs={{0,8},{2,10},{8,16},{10,18},{16,24},{18,26},{24,28},{26,30},{28,20... | collective-permute-start | bytes 393224 | tf_op jit(solution)/shard_map/ppermute | solution.py:192
  20.7 10.7 %collective-permute-start.18 = (f32[256,128]{1,0:T(8,128)S(1)}, f32[256,128]{1,0:T(8,128)S(1)}, u32[]{:S(2)}, u32[]{:S(2)}) collective-permute-start(f32[256,128]{1,0:T(8,128)S(1)} %collective-permute-done.17.refs_10_), channel_id=1, source_target_pairs={{0,8},{2,10},{8,16},{10,18},{16,24},{18,26},{24,28},{26,30},{28,20... | collective-permute-start | bytes 393224 | tf_op jit(solution)/shard_map/ppermute | solution.py:192
  24.9 8.0 %collective-permute-start.21 = (f32[256,128]{1,0:T(8,128)S(1)}, f32[256,128]{1,0:T(8,128)S(1)}, u32[]{:S(2)}, u32[]{:S(2)}) collective-permute-start(f32[256,128]{1,0:T(8,128)S(1)} %collective-permute-done.20.refs_11_), channel_id=1, source_target_pairs={{0,4},{2,6},{8,0},{10,2},{16,8},{18,10},{24,16},{26,18},{28,24},{3... | collective-permute-start | bytes 393224 | tf_op jit(solution)/shard_map/ppermute | solution.py:192
  26.5 8.0 %collective-permute-start.27 = (f32[256,128]{1,0:T(8,128)S(1)}, f32[256,128]{1,0:T(8,128)S(1)}, u32[]{:S(2)}, u32[]{:S(2)}) collective-permute-start(f32[256,128]{1,0:T(8,128)S(1)} %collective-permute-done.26.refs_14_), channel_id=1, source_target_pairs={{0,4},{2,6},{8,0},{10,2},{16,8},{18,10},{24,16},{26,18},{28,24},{3... | collective-permute-start | bytes 393224 | tf_op jit(solution)/shard_map/ppermute | solution.py:192
  28.1 6.9 %collective-permute-start.4 = (f32[256,128]{1,0:T(8,128)S(1)}, f32[256,128]{1,0:T(8,128)S(1)}, u32[]{:S(2)}, u32[]{:S(2)}) collective-permute-start(f32[256,128]{1,0:T(8,128)S(1)} %collective-permute-done.3.refs_7_), channel_id=1, source_target_pairs={{0,8},{2,10},{8,16},{10,18},{16,24},{18,26},{24,28},{26,30},{28,20... | collective-permute-start | bytes 393224 | tf_op jit(solution)/shard_map/ppermute | solution.py:192
  28.6 8.0 %collective-permute-start.2 = (s32[4,56,256]{2,1,0:T(8,128)S(1)}, s32[4,56,256]{2,1,0:T(8,128)}, u32[]{:S(2)}, u32[]{:S(2)}) collective-permute-start(s32[4,56,256]{2,1,0:T(8,128)S(1)} %collective-permute-done.1), channel_id=1, source_target_pairs={{0,1},{1,0},{2,3},{3,2},{4,5},{5,4},{6,7},{7,6},{8,9},{9,8},{10,11... | collective-permute-start | bytes 688136 | tf_op jit(solution)/shard_map/ppermute | solution.py:198
  31.4 10.8 %collective-permute-start.24 = (f32[256,128]{1,0:T(8,128)S(1)}, f32[256,128]{1,0:T(8,128)S(1)}, u32[]{:S(2)}, u32[]{:S(2)}) collective-permute-start(f32[256,128]{1,0:T(8,128)S(1)} %collective-permute-done.23.refs_13_), channel_id=1, source_target_pairs={{0,4},{2,6},{8,0},{10,2},{16,8},{18,10},{24,16},{26,18},{28,24},{3... | collective-permute-start | bytes 393224 | tf_op jit(solution)/shard_map/ppermute | solution.py:192
  33.0 7.7 %collective-permute-start.8 = (f32[256,128]{1,0:T(8,128)S(1)}, f32[256,128]{1,0:T(8,128)S(1)}, u32[]{:S(2)}, u32[]{:S(2)}) collective-permute-start(f32[256,128]{1,0:T(8,128)S(1)} %collective-permute-done.7.refs_12_), channel_id=1, source_target_pairs={{0,4},{2,6},{8,0},{10,2},{16,8},{18,10},{24,16},{26,18},{28,24},{3... | collective-permute-start | bytes 393224 | tf_op jit(solution)/shard_map/ppermute | solution.py:192
  34.6 13.0 %collective-permute-start.16 = (f32[256,128]{1,0:T(8,128)S(1)}, f32[256,128]{1,0:T(8,128)S(1)}, u32[]{:S(2)}, u32[]{:S(2)}) collective-permute-start(f32[256,128]{1,0:T(8,128)S(1)} %collective-permute-done.15.refs_9_), channel_id=1, source_target_pairs={{0,8},{2,10},{8,16},{10,18},{16,24},{18,26},{24,28},{26,30},{28,20... | collective-permute-start | bytes 393224 | tf_op jit(solution)/shard_map/ppermute | solution.py:192
  35.0 12.6 %collective-permute-start.28 = (f32[256,128]{1,0:T(8,128)S(1)}, f32[256,128]{1,0:T(8,128)S(1)}, u32[]{:S(2)}, u32[]{:S(2)}) collective-permute-start(f32[256,128]{1,0:T(8,128)S(1)} %collective-permute-done.27.refs_14_), channel_id=1, source_target_pairs={{0,4},{2,6},{8,0},{10,2},{16,8},{18,10},{24,16},{26,18},{28,24},{3... | collective-permute-start | bytes 393224 | tf_op jit(solution)/shard_map/ppermute | solution.py:192
  36.6 13.0 %collective-permute-start.5 = (f32[256,128]{1,0:T(8,128)S(1)}, f32[256,128]{1,0:T(8,128)S(1)}, u32[]{:S(2)}, u32[]{:S(2)}) collective-permute-start(f32[256,128]{1,0:T(8,128)S(1)} %collective-permute-done.4.refs_7_), channel_id=1, source_target_pairs={{0,8},{2,10},{8,16},{10,18},{16,24},{18,26},{24,28},{26,30},{28,20... | collective-permute-start | bytes 393224 | tf_op jit(solution)/shard_map/ppermute | solution.py:192
  40.6 19.7 %collective-permute-start.9 = (f32[256,128]{1,0:T(8,128)S(1)}, f32[256,128]{1,0:T(8,128)S(1)}, u32[]{:S(2)}, u32[]{:S(2)}) collective-permute-start(f32[256,128]{1,0:T(8,128)S(1)} %collective-permute-done.8.refs_12_), channel_id=1, source_target_pairs={{0,4},{2,6},{8,0},{10,2},{16,8},{18,10},{24,16},{26,18},{28,24},{3... | collective-permute-start | bytes 393224 | tf_op jit(solution)/shard_map/ppermute | solution.py:192
  42.2 19.9 %collective-permute-start.13 = (f32[256,128]{1,0:T(8,128)S(1)}, f32[256,128]{1,0:T(8,128)S(1)}, u32[]{:S(2)}, u32[]{:S(2)}) collective-permute-start(f32[256,128]{1,0:T(8,128)S(1)} %collective-permute-done.12.refs_8_), channel_id=1, source_target_pairs={{0,8},{2,10},{8,16},{10,18},{16,24},{18,26},{24,28},{26,30},{28,20... | collective-permute-start | bytes 393224 | tf_op jit(solution)/shard_map/ppermute | solution.py:192
  47.5 25.3 %collective-permute-start.19 = (f32[256,128]{1,0:T(8,128)S(1)}, f32[256,128]{1,0:T(8,128)S(1)}, u32[]{:S(2)}, u32[]{:S(2)}) collective-permute-start(f32[256,128]{1,0:T(8,128)S(1)} %collective-permute-done.18.refs_10_), channel_id=1, source_target_pairs={{0,8},{2,10},{8,16},{10,18},{16,24},{18,26},{24,28},{26,30},{28,20... | collective-permute-start | bytes 393224 | tf_op jit(solution)/shard_map/ppermute | solution.py:192
  47.6 25.3 %collective-permute-start.22 = (f32[256,128]{1,0:T(8,128)S(1)}, f32[256,128]{1,0:T(8,128)S(1)}, u32[]{:S(2)}, u32[]{:S(2)}) collective-permute-start(f32[256,128]{1,0:T(8,128)S(1)} %collective-permute-done.21.refs_11_), channel_id=1, source_target_pairs={{0,4},{2,6},{8,0},{10,2},{16,8},{18,10},{24,16},{26,18},{28,24},{3... | collective-permute-start | bytes 393224 | tf_op jit(solution)/shard_map/ppermute | solution.py:192
  49.6 25.3 %collective-permute-start.25 = (f32[256,128]{1,0:T(8,128)S(1)}, f32[256,128]{1,0:T(8,128)S(1)}, u32[]{:S(2)}, u32[]{:S(2)}) collective-permute-start(f32[256,128]{1,0:T(8,128)S(1)} %collective-permute-done.24.refs_13_), channel_id=1, source_target_pairs={{0,4},{2,6},{8,0},{10,2},{16,8},{18,10},{24,16},{26,18},{28,24},{3... | collective-permute-start | bytes 393224 | tf_op jit(solution)/shard_map/ppermute | solution.py:192
  60.4 21.6 %collective-permute-start.32 = (f32[256,128]{1,0:T(8,128)S(1)}, f32[256,128]{1,0:T(8,128)S(1)}, u32[]{:S(2)}, u32[]{:S(2)}) collective-permute-start(f32[256,128]{1,0:T(8,128)S(1)} %collective-permute-done.16.refs_9_), channel_id=1, source_target_pairs={{0,8},{2,10},{8,16},{10,18},{16,24},{18,26},{24,28},{26,30},{28,20... | collective-permute-start | bytes 393224 | tf_op jit(solution)/shard_map/ppermute | solution.py:192
  62.1 19.8 %collective-permute-start.33 = (f32[256,128]{1,0:T(8,128)S(1)}, f32[256,128]{1,0:T(8,128)S(1)}, u32[]{:S(2)}, u32[]{:S(2)}) collective-permute-start(f32[256,128]{1,0:T(8,128)S(1)} %collective-permute-done.28.refs_14_), channel_id=1, source_target_pairs={{0,4},{2,6},{8,0},{10,2},{16,8},{18,10},{24,16},{26,18},{28,24},{3... | collective-permute-start | bytes 393224 | tf_op jit(solution)/shard_map/ppermute | solution.py:192
  72.8 12.0 %collective-permute-start.10 = (f32[256,128]{1,0:T(8,128)S(1)}, f32[256,128]{1,0:T(8,128)S(1)}, u32[]{:S(2)}, u32[]{:S(2)}) collective-permute-start(f32[256,128]{1,0:T(8,128)S(1)} %collective-permute-done.9.refs_12_), channel_id=1, source_target_pairs={{0,4},{2,6},{8,0},{10,2},{16,8},{18,10},{24,16},{26,18},{28,24},{3... | collective-permute-start | bytes 393224 | tf_op jit(solution)/shard_map/ppermute | solution.py:192
  72.9 12.0 %collective-permute-start.6 = (f32[256,128]{1,0:T(8,128)S(1)}, f32[256,128]{1,0:T(8,128)S(1)}, u32[]{:S(2)}, u32[]{:S(2)}) collective-permute-start(f32[256,128]{1,0:T(8,128)S(1)} %collective-permute-done.5.refs_7_), channel_id=1, source_target_pairs={{0,8},{2,10},{8,16},{10,18},{16,24},{18,26},{24,28},{26,30},{28,20... | collective-permute-start | bytes 393224 | tf_op jit(solution)/shard_map/ppermute | solution.py:192
  89.7 9.2 %collective-permute-start.36 = (f32[512,128]{1,0:T(8,128)S(1)}, f32[512,128]{1,0:T(8,128)S(1)}, u32[]{:S(2)}, u32[]{:S(2)}) collective-permute-start(f32[512,128]{1,0:T(8,128)S(1)} %add.479), channel_id=1, source_target_pairs={{0,1},{1,0},{2,3},{3,2},{4,5},{5,4},{6,7},{7,6},{8,9},{9,8},{10,11... | collective-permute-start | bytes 786440 | tf_op jit(solution)/shard_map/ppermute | solution.py:198
  89.7 9.7 %collective-permute-start.29 = (f32[512,128]{1,0:T(8,128)S(1)}, f32[512,128]{1,0:T(8,128)S(1)}, u32[]{:S(2)}, u32[]{:S(2)}) collective-permute-start(f32[512,128]{1,0:T(8,128)S(1)} %get-tuple-element.29), channel_id=1, source_target_pairs={{0,2},{2,0},{4,6},{6,4},{8,10},{10,8},{12,14},{14,12},{16,18},{18,... | collective-permute-start | bytes 786440 | tf_op jit(solution)/shard_map/ppermute | solution.py:195
  90.8 13.3 %collective-permute-start.31 = (f32[512,128]{1,0:T(8,128)S(1)}, f32[512,128]{1,0:T(8,128)S(1)}, u32[]{:S(2)}, u32[]{:S(2)}) collective-permute-start(f32[512,128]{1,0:T(8,128)S(1)} %add.475), channel_id=1, source_target_pairs={{0,1},{1,0},{2,3},{3,2},{4,5},{5,4},{6,7},{7,6},{8,9},{9,8},{10,11... | collective-permute-start | bytes 786440 | tf_op jit(solution)/shard_map/ppermute | solution.py:198
  (15 other events, 131.1 us)
where the time goes:
time: 107 us; the launch traced here: 105 us
  Pallas kernels  38.2 us (36%)
  starting transfers between devices  33.9 us (32%)
  waiting for transfers between devices  22.7 us (21%)
  other arithmetic  4.3 us (4%)
  local copies, waits for them, and re-layouts  2.67 us (2%)
  matrix products  2.61 us (2%)
    pallas_call x6, Pallas kernels, add_sources(): pl.pallas_call(functools.partial(sum_kernel, sources, chunks, pieces, slo...  38.2 us
    ppermute x28, starting transfers between devices, ring(): return lax.ppermute(value, 'blk', pairs)  28 us
    ppermute x4, waiting for transfers between devices, rep_swap(): return lax.ppermute(value, 'rep', [(0, 1), (1, 0)])  13.4 us
    ppermute x28, waiting for transfers between devices, ring(): return lax.ppermute(value, 'blk', pairs)  8.75 us
    ppermute x4, starting transfers between devices, rep_swap(): return lax.ppermute(value, 'rep', [(0, 1), (1, 0)])  3.39 us
    ppermute x5, starting transfers between devices, core_swap(): return lax.ppermute(value, 'blk', [(b, b ^ 1) for b in range(blocks)])  2.46 us
  transfers between devices with their start and end apart: 37, of which 9 were waited for; matrix products, arithmetic and copies ran while one was open for 4% of the time, Pallas kernels for 36%

commit v1 on v0

v1 whole, which is shorter than its diff:
```python
import functools

import jax
import jax.numpy as jnp
from jax import lax
from jax.experimental import pallas as pl
from jax.experimental.pallas import tpu as pltpu
from jax.sharding import PartitionSpec as P

TILE = 128
UNROLL = 8
SMEM = pl.BlockSpec(memory_space=pltpu.SMEM)
VMEM = pl.BlockSpec(memory_space=pltpu.VMEM)


def bf16_pair(value):
    high = value.astype(jnp.bfloat16)
    low = (value - high.astype(jnp.float32)).astype(jnp.bfloat16)
    return high, low


def tile_matrix(edges, pair, slot, slots, live):
    rows = edges[pair, pl.ds(slot, 1), :]
    cols = edges[pair, pl.ds(slot + slots, 1), :]
    weights = edges[pair, pl.ds(slot + 2 * slots, 1), :]
    weights = jnp.where(live, weights, 0).astype(jnp.float32)
    index = lax.broadcasted_iota(jnp.int32, (TILE, rows.shape[1]), 0)
    row_hot = jnp.where(index == rows, 1.0, 0.0).astype(jnp.bfloat16)
    col_hot = jnp.where(index == cols, weights, 0.0).astype(jnp.bfloat16)
    matrix = lax.dot_general(
        row_hot, col_hot, (((1,), (1,)), ((), ())), preferred_element_type=jnp.float32
    )
    return jnp.concatenate(bf16_pair(matrix), axis=1)


def sum_kernel(sources, chunks, slots, first, last, *refs):
    pairs, place, meta, edges = refs[:4]
    refs = refs[4:]
    parts, refs = refs[: sources * chunks], refs[sources * chunks :]
    if not first:
        before, refs = refs[:chunks], refs[chunks:]
    if last:
        outs, sides, entries = refs[: 2 * chunks], refs[2 * chunks], refs[2 * chunks + 1]
        sums = refs[2 * chunks + 2 :]
    else:
        sums, sides, entries = refs[:chunks], refs[chunks], refs[chunks + 1]
    tiles_here = sides.shape[1]
    tiles_per = sums[0].shape[1] // TILE

    for chunk in range(chunks):
        if first:
            sums[chunk][...] = jnp.zeros_like(sums[chunk])
        else:
            sums[chunk][...] = before[chunk][...]

    used = jnp.int32(0)
    for number in range(2 * sources):
        pair = pairs[number]
        for slot in range(slots):
            column = meta[pair, slots + slot] - place[0]
            row = (meta[pair, slot] + place[1]) & (tiles_per - 1)
            wanted = (slot < meta[pair, 2 * slots]) & (column >= 0) & (column < tiles_here)
            code = ((number * slots + slot) * tiles_here + column) * tiles_per + row
            entries[used] = jnp.where(wanted, code, 0)
            used = used + wanted.astype(jnp.int32)
    for extra in range(UNROLL - 1):
        entries[used + extra] = 0

    for source in range(sources):
        for chunk in range(chunks):
            part = parts[source * chunks + chunk]
            left = 2 * TILE * chunk
            for tile in range(tiles_here):
                high, low = bf16_pair(part[tile * TILE : (tile + 1) * TILE, :])
                for half in range(2):
                    below = half * TILE
                    sides[source, tile, below : below + TILE, left : left + TILE] = high
                    sides[source, tile, below : below + TILE, left + TILE : left + 2 * TILE] = low

    def group(step, carry):
        todo = []
        for lane in range(UNROLL):
            entry = step * UNROLL + lane
            code = entries[entry]
            row = code & (tiles_per - 1)
            code = lax.div(code, tiles_per)
            column = lax.rem(code, tiles_here)
            code = lax.div(code, tiles_here)
            slot = lax.rem(code, slots)
            number = lax.div(code, slots)
            matrix = tile_matrix(edges, pairs[number], slot, slots, entry < used)
            todo.append((matrix, number, column, row))
        results = [
            jnp.dot(matrix, sides[lax.div(number, 2), column], preferred_element_type=jnp.float32)
            for matrix, number, column, _ in todo
        ]
        for (_, number, _, row), result in zip(todo, results):
            at = (lax.rem(number, 2), pl.ds(pl.multiple_of(row * TILE, TILE), TILE), slice(None))
            for chunk in range(chunks):
                left = 2 * TILE * chunk
                sums[chunk][at] += result[:, left : left + TILE] + result[:, left + TILE : left + 2 * TILE]
        return carry

    lax.fori_loop(0, lax.div(used + UNROLL - 1, UNROLL), group, 0)
    if last:
        for chunk in range(chunks):
            for block in range(2):
                outs[2 * chunk + block][...] = sums[chunk][block]


def add_sources(pairs, place, meta, edges, parts, before, rows, slots, last=False):
    sources, chunks = len(parts), len(parts[0])
    flat = [chunk for source in parts for chunk in source]
    here, width = flat[0].shape
    first = before is None
    whole = jax.ShapeDtypeStruct((2, rows, width), jnp.float32)
    block = jax.ShapeDtypeStruct((rows, width), jnp.float32)
    olds = [] if first else list(before)
    outs = [block] * (2 * chunks) if last else [whole] * chunks
    scratch = [
        pltpu.VMEM((sources, here // TILE, 2 * TILE, 2 * TILE * chunks), jnp.bfloat16),
        pltpu.SMEM((2 * sources * slots + UNROLL,), jnp.int32),
    ]
    if last:
        scratch += [pltpu.VMEM(whole.shape, jnp.float32)] * chunks
    flops = 2 * sources * 8 * 2 * TILE * TILE * (256 + 4 * TILE * chunks)
    return pl.pallas_call(
        functools.partial(sum_kernel, sources, chunks, slots, first, last),
        in_specs=[SMEM] * 3 + [VMEM] * (1 + len(flat) + len(olds)),
        out_specs=[VMEM] * len(outs),
        out_shape=outs,
        scratch_shapes=scratch,
        compiler_params=pltpu.CompilerParams(vmem_limit_bytes=24 << 20),
        cost_estimate=pl.CostEstimate(flops=flops, bytes_accessed=4 << 20, transcendentals=0),
    )(pairs, place, meta, edges, *flat, *olds)


def on_device(
    features,
    degrees,
    root_weight,
    neighbor_weight,
    bias,
    tile_rows,
    tile_cols,
    tile_count,
    edge_row,
    edge_col,
    edge_weight,
):
    highest = lax.Precision.HIGHEST
    groups, blocks = lax.axis_size("rep"), lax.axis_size("blk")
    lanes = blocks // 2
    layers = lanes // 2
    arc, slots, listed = edge_row.shape[1:]
    per = arc // 2
    shard, width = features.shape
    rows = shard * groups
    chunks = width // TILE
    block, replica = lax.axis_index("blk"), lax.axis_index("rep")
    chip, core = block // 2, block % 2

    def chip_at(position):
        return 2 * position if position < layers else 2 * (lanes - 1 - position) + 1

    def ring(value, step):
        pairs = [
            (2 * chip_at(p) + c, 2 * chip_at((p + step) % lanes) + c) for p in range(lanes) for c in range(2)
        ]
        return lax.ppermute(value, "blk", pairs)

    def core_swap(value):
        return lax.ppermute(value, "blk", [(b, b ^ 1) for b in range(blocks)])

    def rep_swap(value):
        return lax.ppermute(value, "rep", [(0, 1), (1, 0)])

    scale = lax.rsqrt(degrees.astype(jnp.float32))
    scaled = features * scale[:, None]
    own = [scaled[:, f * TILE : (f + 1) * TILE] for f in range(chunks)]

    def bundle(start):
        lists = [array[0, start::2] for array in (edge_row, edge_col, edge_weight)]
        head = jnp.concatenate(
            [tile_rows[0, start::2], tile_cols[0, start::2], tile_count[0, start::2, None]], axis=1
        )
        head = jnp.pad(head, ((0, 0), (0, listed - head.shape[1])))[:, None]
        head = jnp.pad(head, ((0, 0), (0, 7), (0, 0)))
        return jnp.concatenate(lists + [head], axis=1)

    own_lists = bundle(0)
    sibling_lists = core_swap(bundle(1))
    lists = jnp.concatenate([own_lists, sibling_lists], axis=0)
    if groups == 2:
        edges = jnp.concatenate([lists, rep_swap(lists)], axis=0)
    else:
        edges = lax.all_gather(lists, "rep", axis=0, tiled=True)
    meta = edges[:, 3 * slots, :TILE]

    def list_place(offset, which):
        group = offset // per
        group = group ^ replica if groups == 2 else group
        return (2 * group + which) * per + offset % per

    position = jnp.where(chip % 2 == 0, chip // 2, lanes - 1 - chip // 2)

    def pairs_of(distances):
        places = []
        for distance in distances:
            there = (position + distance + lanes) % lanes
            source = jnp.where(there < layers, 2 * there, 2 * (lanes - 1 - there) + 1)
            places.append(list_place((chip - source + lanes) % lanes, 0))
            places.append(list_place((chip - source - core + lanes) % lanes, 1))
        return jnp.stack(places).astype(jnp.int32)

    tiles_per = rows // TILE
    tiles_here = shard // TILE
    rotation = (tiles_per - replica * tiles_here) if groups == 2 else 0 * replica
    place = jnp.stack([replica * tiles_here, rotation]).astype(jnp.int32)
    add = functools.partial(add_sources, rows=rows, slots=slots)

    root = jnp.dot(features, root_weight, precision=highest) + bias

    up, down = own, own
    totals = None
    for step in range(1, lanes // 2 + 1):
        last = step == lanes // 2
        up = [ring(v, 1) if f % 2 == 0 or not last else None for f, v in enumerate(up)]
        down = [ring(v, -1) if f % 2 == 1 or not last else None for f, v in enumerate(down)]
        if step == 1:
            totals = add(pairs_of([0]), place, meta, edges, [own], None)
        if not last:
            totals = add(pairs_of([-step, step]), place, meta, edges, [up, down], totals)
    pairs = pairs_of([lanes // 2])
    hidden = root
    for f in range(chunks):
        end = up[f] if f % 2 == 0 else down[f]
        own_sum, sibling_sum = add(pairs, place, meta, edges, [[end]], [totals[f]], last=True)
        swapped = core_swap(sibling_sum)
        if groups == 2:
            other = rep_swap(own_sum[shard:] + swapped[shard:])
            share = own_sum[:shard] + swapped[:shard] + other
        else:
            share = lax.psum_scatter(own_sum + swapped, "rep", scatter_dimension=0, tiled=True)
        mixed = share * scale[:, None]
        hidden = hidden + jnp.dot(mixed, neighbor_weight[f * TILE : (f + 1) * TILE], precision=highest)
    return jax.nn.relu(hidden)


def solution(mesh):
    placed = (
        P(("blk", "rep"), None),
        P(("blk", "rep")),
        P(),
        P(),
        P(),
        P("blk", "rep", None),
        P("blk", "rep", None),
        P("blk", "rep"),
        P("blk", "rep", None, None),
        P("blk", "rep", None, None),
        P("blk", "rep", None, None),
    )
    return jax.shard_map(
        on_device, mesh=mesh, in_specs=placed, out_specs=P(("blk", "rep"), None), check_vma=False
    )
```

time: 107 us -> 71.9 us (0.67)
  the two profiles are of different devices: /device:TPU:14 before, /device:TPU:0 now
where the time goes in v1:
time: 71.9 us; the launch traced here: 72 us
  waiting for transfers between devices  24.3 us (34%)
  starting transfers between devices  20.5 us (29%)
  Pallas kernels  18 us (25%)
  other arithmetic  4.48 us (6%)
  matrix products  2.61 us (4%)
  local copies, waits for them, and re-layouts  1.23 us (2%)
  between operations  0.99 us (1%)
    pallas_call x6, Pallas kernels, add_sources(): pl.pallas_call(functools.partial(sum_kernel, sources, chunks, slots, firs...  18 us
    ppermute x14, starting transfers between devices, ring(): return lax.ppermute(value, 'blk', pairs)  17.2 us
    ppermute x14, waiting for transfers between devices, ring(): return lax.ppermute(value, 'blk', pairs)  11.7 us
    ppermute x3, waiting for transfers between devices, rep_swap(): return lax.ppermute(value, 'rep', [(0, 1), (1, 0)])  10.7 us
    ppermute x3, starting transfers between devices, rep_swap(): return lax.ppermute(value, 'rep', [(0, 1), (1, 0)])  3.04 us
    dot_general x2, matrix products, on_device(): jnp.dot(mixed, neighbor_weight[f * TILE:(f + 1) * TILE], precision=highest)  2.03 us
    ppermute x3, waiting for transfers between devices, core_swap(): return lax.ppermute(value, 'blk', [(b, b ^ 1) for b in range(blocks)])  2 us
  transfers between devices with their start and end apart: 20, of which 8 were waited for; matrix products, arithmetic and copies ran while one was open for 6% of the time, Pallas kernels for 25%

profile of v1, /device:TPU:0, one launch (start us, length us, event | category | flops | bytes accessed | tf_op | source)
XLA Modules:
  0.0 72.0 jit_solution(1460704625189396428)
XLA Ops:
  0.0 0.7 %convert_rsqrt_fusion = f32[512]{0:T(512)S(1)} fusion(s32[512]{0:T(512)} %param.12), kind=kLoop, calls=%fused_computation.31 | loop fusion | flops 512 | bytes 4096 | tf_op jit(solution)/shard_map/rsqrt | solution.py:178
  0.7 1.2 %broadcast_multiply_fusion = f32[512,256]{1,0:T(8,128)S(1)} fusion(f32[512,256]{1,0:T(8,128)} %param.11, f32[512]{0:T(512)S(1)} %convert_rsqrt_fusion), kind=kLoop, calls=%fused_computation.17 | loop fusion | flops 131072 | bytes 1050624 | tf_op jit(solution)/shard_map/mul | solution.py:179
  2.0 3.0 %collective-permute-start.12 = (f32[512,128]{1,0:T(8,128)S(1)}, f32[512,128]{1,0:T(8,128)S(1)}, u32[]{:S(2)}, u32[]{:S(2)}) collective-permute-start(f32[512,128]{1,0:T(8,128)S(1)} %get-tuple-element.30.refs_5_), channel_id=1, source_target_pairs={{0,4},{2,6},{8,0},{10,2},{16,8},{18,10},{24,16},{26,18},{28,24},{3... | collective-permute-start | bytes 786440 | tf_op jit(solution)/shard_map/ppermute | solution.py:170
  5.1 2.0 %collective-permute-start.2 = (f32[512,128]{1,0:T(8,128)S(1)}, f32[512,128]{1,0:T(8,128)S(1)}, u32[]{:S(2)}, u32[]{:S(2)}) collective-permute-start(f32[512,128]{1,0:T(8,128)S(1)} %get-tuple-element.29.refs_4_), channel_id=1, source_target_pairs={{0,8},{2,10},{8,16},{10,18},{16,24},{18,26},{24,28},{26,30},{28,20... | collective-permute-start | bytes 786440 | tf_op jit(solution)/shard_map/ppermute | solution.py:170
  9.0 0.7 %collective-permute-done = s32[4,56,256]{2,1,0:T(8,128)S(1)} collective-permute-done((s32[4,56,256]{2,1,0:T(8,128)S(1)}, s32[4,56,256]{2,1,0:T(8,128)S(1)}, u32[]{:S(2)}, u32[]{:S(2)}) %collective-permute-start) | collective-permute-done | bytes 229408 | tf_op jit(solution)/shard_map/ppermute | solution.py:173
  9.7 0.8 %pad_add_fusion.1 = s32[8,56,256]{2,1,0:T(8,128)} fusion(s32[4,56,256]{2,1,0:T(8,128)S(1)} %collective-permute-done, s32[4,8,256]{2,1,0:T(8,128)S(1)} %pad.15, s32[4,16,256]{2,1,0:T(8,128)S(1)} %get-tuple-element.35, s32[4,16,256]{2,1,0:T(8,128)S(1)} %get-tuple-element.38, s32[4,16,256]{2,1,0:T(8,128)S(1)} %get-tuple-element.31), kind=kLoop, calls=%fused_computation.5 | loop fusion | flops 458752 | bytes 917504 | tf_op jit(solution)/shard_map/concatenate | solution.py:193
  10.5 1.9 %collective-permute-start.1 = (s32[8,56,256]{2,1,0:T(8,128)}, s32[8,56,256]{2,1,0:T(8,128)}, u32[]{:S(2)}, u32[]{:S(2)}) collective-permute-start(s32[8,56,256]{2,1,0:T(8,128)} %pad_add_fusion.1), channel_id=1, source_target_pairs={{0,1},{1,0},{2,3},{3,2},{4,5},{5,4},{6,7},{7,6},{8,9},{9,8},{10,11... | collective-permute-start | bytes 1376264 | tf_op jit(solution)/shard_map/ppermute | solution.py:176
  12.4 1.7 %collective-permute-start.13 = (f32[512,128]{1,0:T(8,128)S(1)}, f32[512,128]{1,0:T(8,128)S(1)}, u32[]{:S(2)}, u32[]{:S(2)}) collective-permute-start(f32[512,128]{1,0:T(8,128)S(1)} %collective-permute-done.12.refs_7_), channel_id=1, source_target_pairs={{0,4},{2,6},{8,0},{10,2},{16,8},{18,10},{24,16},{26,18},{28,24},{3... | collective-permute-start | bytes 786440 | tf_op jit(solution)/shard_map/ppermute | solution.py:170
  14.2 3.6 %collective-permute-done.9.refs_6_ = f32[512,128]{1,0:T(8,128)S(1)} collective-permute-done((f32[512,128]{1,0:T(8,128)S(1)}, f32[512,128]{1,0:T(8,128)S(1)}, u32[]{:S(2)}, u32[]{:S(2)}) %collective-permute-start.9) | collective-permute-done | bytes 262176 | tf_op jit(solution)/shard_map/ppermute | solution.py:170
  17.8 2.0 %collective-permute-start.10 = (f32[512,128]{1,0:T(8,128)S(1)}, f32[512,128]{1,0:T(8,128)S(1)}, u32[]{:S(2)}, u32[]{:S(2)}) collective-permute-start(f32[512,128]{1,0:T(8,128)S(1)} %collective-permute-done.9.refs_6_), channel_id=1, source_target_pairs={{0,4},{2,6},{8,0},{10,2},{16,8},{18,10},{24,16},{26,18},{28,24},{3... | collective-permute-start | bytes 786440 | tf_op jit(solution)/shard_map/ppermute | solution.py:170
  19.9 2.0 %collective-permute-start.7 = (f32[512,128]{1,0:T(8,128)S(1)}, f32[512,128]{1,0:T(8,128)S(1)}, u32[]{:S(2)}, u32[]{:S(2)}) collective-permute-start(f32[512,128]{1,0:T(8,128)S(1)} %collective-permute-done.6.refs_5_), channel_id=1, source_target_pairs={{0,8},{2,10},{8,16},{10,18},{16,24},{18,26},{24,28},{26,30},{28,20... | collective-permute-start | bytes 786440 | tf_op jit(solution)/shard_map/ppermute | solution.py:170
  22.5 0.9 %collective-permute-done.13.refs_7_ = f32[512,128]{1,0:T(8,128)S(1)} collective-permute-done((f32[512,128]{1,0:T(8,128)S(1)}, f32[512,128]{1,0:T(8,128)S(1)}, u32[]{:S(2)}, u32[]{:S(2)}) %collective-permute-start.13) | collective-permute-done | bytes 262176 | tf_op jit(solution)/shard_map/ppermute | solution.py:170
  23.4 2.0 %collective-permute-start.14 = (f32[512,128]{1,0:T(8,128)S(1)}, f32[512,128]{1,0:T(8,128)S(1)}, u32[]{:S(2)}, u32[]{:S(2)}) collective-permute-start(f32[512,128]{1,0:T(8,128)S(1)} %collective-permute-done.13.refs_7_), channel_id=1, source_target_pairs={{0,4},{2,6},{8,0},{10,2},{16,8},{18,10},{24,16},{26,18},{28,24},{3... | collective-permute-start | bytes 786440 | tf_op jit(solution)/shard_map/ppermute | solution.py:170
  25.5 3.6 %collective-permute-done.3.refs_4_ = f32[512,128]{1,0:T(8,128)S(1)} collective-permute-done((f32[512,128]{1,0:T(8,128)S(1)}, f32[512,128]{1,0:T(8,128)S(1)}, u32[]{:S(2)}, u32[]{:S(2)}) %collective-permute-start.3) | collective-permute-done | bytes 262176 | tf_op jit(solution)/shard_map/ppermute | solution.py:170
  29.1 1.9 %collective-permute-start.11 = (f32[512,128]{1,0:T(8,128)S(1)}, f32[512,128]{1,0:T(8,128)S(1)}, u32[]{:S(2)}, u32[]{:S(2)}) collective-permute-start(f32[512,128]{1,0:T(8,128)S(1)} %collective-permute-done.10.refs_6_), channel_id=1, source_target_pairs={{0,4},{2,6},{8,0},{10,2},{16,8},{18,10},{24,16},{26,18},{28,24},{3... | collective-permute-start | bytes 786440 | tf_op jit(solution)/shard_map/ppermute | solution.py:170
  31.0 3.6 %collective-permute-done.7.refs_5_ = f32[512,128]{1,0:T(8,128)S(1)} collective-permute-done((f32[512,128]{1,0:T(8,128)S(1)}, f32[512,128]{1,0:T(8,128)S(1)}, u32[]{:S(2)}, u32[]{:S(2)}) %collective-permute-start.7) | collective-permute-done | bytes 262176 | tf_op jit(solution)/shard_map/ppermute | solution.py:170
  34.7 1.1 %pad_add_fusion.refs_3_ = s32[16,56,256]{2,1,0:T(8,128)S(1)} fusion(s32[8,56,256]{2,1,0:T(8,128)} %collective-permute-done.1, s32[4,56,256]{2,1,0:T(8,128)S(1)} %collective-permute-done, s32[4,8,256]{2,1,0:T(8,128)S(1)} %pad.15, s32[4,16,256]{2,1,0:T(8,128)S(1)} %get-tuple-element.35, s32[4,16,256]{2,1,0:T(8,128)S(1)} %get-tuple-element.38, ...), kind=kLoop, calls=%fused_computation.4 | loop fusion | flops 1146880 | bytes 1835008 | tf_op jit(solution)/shard_map/concatenate | solution.py:195
  35.8 2.9 %shard_map.109 = (f32[2,1024,128]{2,1,0:T(8,128)S(1)}, f32[2,1024,128]{2,1,0:T(8,128)S(1)}) custom-call(s32[2]{0:T(128)S(1)} %pad_add_fusion.10.refs_0_, s32[2]{0:T(128)S(1)} %pad_add_fusion.6.refs_1_, s32[16,128]{1,0:T(8,128)S(1)} %bitcast.39, s32[16,56,256]{2,1,0:T(8,128)S(1)} %pad_add_fusion.refs_3_, f32[512,128]{1,0:T(8,128)S(1)} %get-tuple-element.29.refs_4_, ...), custom_call_target="tpu_custom_call" | custom-call | flops 671088640 | bytes 4194304 | tf_op jit(solution)/shard_map/pallas_call | solution.py:127
  38.8 1.3 %collective-permute-start.17 = (f32[512,128]{1,0:T(8,128)S(1)}, f32[512,128]{1,0:T(8,128)S(1)}, u32[]{:S(2)}, u32[]{:S(2)}) collective-permute-start(f32[512,128]{1,0:T(8,128)S(1)} %collective-permute-done.14.refs_7_), channel_id=1, source_target_pairs={{0,4},{2,6},{8,0},{10,2},{16,8},{18,10},{24,16},{26,18},{28,24},{3... | collective-permute-start | bytes 786440 | tf_op jit(solution)/shard_map/ppermute | solution.py:170
  40.1 3.8 %shard_map.110 = (f32[2,1024,128]{2,1,0:T(8,128)S(1)}, f32[2,1024,128]{2,1,0:T(8,128)S(1)}) custom-call(s32[4]{0:T(128)S(1)} %pad_add_fusion.9.refs_0_, s32[2]{0:T(128)S(1)} %pad_add_fusion.6.refs_1_, s32[16,128]{1,0:T(8,128)S(1)} %bitcast.40, s32[16,56,256]{2,1,0:T(8,128)S(1)} %pad_add_fusion.refs_3_, f32[512,128]{1,0:T(8,128)S(1)} %collective-permute-done.2.refs_4_, ...), custom_call_target="tpu_custom_call" | custom-call | flops 1342177280 | bytes 4194304 | tf_op jit(solution)/shard_map/pallas_call | solution.py:127
  43.9 3.2 %shard_map.111 = (f32[2,1024,128]{2,1,0:T(8,128)S(1)}, f32[2,1024,128]{2,1,0:T(8,128)S(1)}) custom-call(s32[4]{0:T(128)S(1)} %pad_add_fusion.8.refs_0_, s32[2]{0:T(128)S(1)} %pad_add_fusion.6.refs_1_, s32[16,128]{1,0:T(8,128)S(1)} %bitcast.41, s32[16,56,256]{2,1,0:T(8,128)S(1)} %pad_add_fusion.refs_3_, f32[512,128]{1,0:T(8,128)S(1)} %collective-permute-done.3.refs_4_, ...), custom_call_target="tpu_custom_call" | custom-call | flops 1342177280 | bytes 4194304 | tf_op jit(solution)/shard_map/pallas_call | solution.py:127
  47.1 0.8 %collective-permute-start.5 = (f32[512,128]{1,0:T(8,128)S(1)}, f32[512,128]{1,0:T(8,128)S(1)}, u32[]{:S(2)}, u32[]{:S(2)}) collective-permute-start(f32[512,128]{1,0:T(8,128)S(1)} %collective-permute-done.4.refs_4_), channel_id=1, source_target_pairs={{0,8},{2,10},{8,16},{10,18},{16,24},{18,26},{24,28},{26,30},{28,20... | collective-permute-start | bytes 786440 | tf_op jit(solution)/shard_map/ppermute | solution.py:170
  47.9 3.2 %shard_map.112 = (f32[2,1024,128]{2,1,0:T(8,128)S(1)}, f32[2,1024,128]{2,1,0:T(8,128)S(1)}) custom-call(s32[4]{0:T(128)S(1)} %pad_add_fusion.7.refs_0_, s32[2]{0:T(128)S(1)} %pad_add_fusion.6.refs_1_, s32[16,128]{1,0:T(8,128)S(1)} %bitcast.42, s32[16,56,256]{2,1,0:T(8,128)S(1)} %pad_add_fusion.refs_3_, f32[512,128]{1,0:T(8,128)S(1)} %collective-permute-done.4.refs_4_, ...), custom_call_target="tpu_custom_call" | custom-call | flops 1342177280 | bytes 4194304 | tf_op jit(solution)/shard_map/pallas_call | solution.py:127
  51.2 2.4 %shard_map.114 = (f32[1024,128]{1,0:T(8,128)S(1)}, f32[1024,128]{1,0:T(8,128)S(1)}) custom-call(s32[2]{0:T(128)S(1)} %pad_add_fusion.5.refs_0_, s32[2]{0:T(128)S(1)} %pad_add_fusion.6.refs_1_, s32[16,128]{1,0:T(8,128)S(1)} %bitcast.43, s32[16,56,256]{2,1,0:T(8,128)S(1)} %pad_add_fusion.refs_3_, f32[512,128]{1,0:T(8,128)S(1)} %collective-permute-done.17.refs_4_, ...), custom_call_target="tpu_custom_call" | custom-call | flops 402653184 | bytes 4194304 | tf_op jit(solution)/shard_map/pallas_call | solution.py:127
  53.7 2.4 %shard_map.113 = (f32[1024,128]{1,0:T(8,128)S(1)}, f32[1024,128]{1,0:T(8,128)S(1)}) custom-call(s32[2]{0:T(128)S(1)} %pad_add_fusion.5.refs_0_, s32[2]{0:T(128)S(1)} %pad_add_fusion.6.refs_1_, s32[16,128]{1,0:T(8,128)S(1)} %bitcast.44, s32[16,56,256]{2,1,0:T(8,128)S(1)} %pad_add_fusion.refs_3_, f32[512,128]{1,0:T(8,128)S(1)} %collective-permute-done.5.refs_4_, ...), custom_call_target="tpu_custom_call" | custom-call | flops 402653184 | bytes 4194304 | tf_op jit(solution)/shard_map/pallas_call | solution.py:127
  56.2 0.6 collective-permute-start.19
  56.8 1.3 %collective-permute-done.15 = f32[1024,128]{1,0:T(8,128)S(1)} collective-permute-done((f32[1024,128]{1,0:T(8,128)S(1)}, f32[1024,128]{1,0:T(8,128)S(1)}, u32[]{:S(2)}, u32[]{:S(2)}) %collective-permute-start.15) | collective-permute-done | bytes 524320 | tf_op jit(solution)/shard_map/ppermute | solution.py:173
  58.8 0.6 convolution_add_fusion.1
  59.3 6.1 %collective-permute-done.19 = f32[512,128]{1,0:T(8,128)S(1)} collective-permute-done((f32[512,128]{1,0:T(8,128)S(1)}, f32[512,128]{1,0:T(8,128)S(1)}, u32[]{:S(2)}, u32[]{:S(2)}) %collective-permute-start.19) | collective-permute-done | bytes 262176 | tf_op jit(solution)/shard_map/ppermute | solution.py:176
  65.4 0.6 fusion.4
  66.0 4.6 %collective-permute-done.16 = f32[512,128]{1,0:T(8,128)S(1)} collective-permute-done((f32[512,128]{1,0:T(8,128)S(1)}, f32[512,128]{1,0:T(8,128)S(1)}, u32[]{:S(2)}, u32[]{:S(2)}) %collective-permute-start.16) | collective-permute-done | bytes 262176 | tf_op jit(solution)/shard_map/ppermute | solution.py:176
  70.6 1.4 %fusion.1 = f32[512,256]{1,0:T(8,128)} fusion(f32[512,256]{1,0:T(8,128)S(1)} %fusion.4, f32[512,256]{1,0:T(8,128)S(1)} %convolution_add_fusion.1, f32[512,128]{1,0:T(8,128)S(1)} %collective-permute-done.16, f32[1024,128]{1,0:T(8,128)S(1)} %collective-permute-done.15, f32[1024,128]{1,0:T(8,128)S(1)} %get-tuple-element.24, f32[256,256]{1,0:T(8,128)S(1)} %copy-done.2, ...), kind=kOutput, calls=%fused_computation.2 | convolution fusion | flops 201916416 | bytes 2492416 | tf_op jit(solution)/shard_map/dot_general | solution.py:246
  (69 shorter events, 3.2 us)
Async XLA Ops:
  0.0 58.7 %copy-start = (f32[256,256]{1,0:T(8,128)S(1)}, f32[256,256]{1,0:T(8,128)}, u32[]{:S(2)}) copy-start(f32[256,256]{1,0:T(8,128)} %param.13) | copy-start | bytes 786436
  1.9 5.2 %copy-start.3 = (s32[1,8,16,256]{3,2,1,0:T(8,128)S(1)}, s32[1,8,16,256]{3,2,1,0:T(8,128)}, u32[]{:S(2)}) copy-start(s32[1,8,16,256]{3,2,1,0:T(8,128)} %param.19) | copy-start | bytes 393220
  2.0 10.4 %collective-permute-start.12 = (f32[512,128]{1,0:T(8,128)S(1)}, f32[512,128]{1,0:T(8,128)S(1)}, u32[]{:S(2)}, u32[]{:S(2)}) collective-permute-start(f32[512,128]{1,0:T(8,128)S(1)} %get-tuple-element.30.refs_5_), channel_id=1, source_target_pairs={{0,4},{2,6},{8,0},{10,2},{16,8},{18,10},{24,16},{26,18},{28,24},{3... | collective-permute-start | bytes 786440 | tf_op jit(solution)/shard_map/ppermute | solution.py:170
  5.0 14.9 %collective-permute-start.6 = (f32[512,128]{1,0:T(8,128)S(1)}, f32[512,128]{1,0:T(8,128)S(1)}, u32[]{:S(2)}, u32[]{:S(2)}) collective-permute-start(f32[512,128]{1,0:T(8,128)S(1)} %get-tuple-element.30.refs_5_), channel_id=1, source_target_pairs={{0,8},{2,10},{8,16},{10,18},{16,24},{18,26},{24,28},{26,30},{28,20... | collective-permute-start | bytes 786440 | tf_op jit(solution)/shard_map/ppermute | solution.py:170
  5.1 2.1 %copy-start.9 = (s32[1,8]{1,0:T(1,128)S(1)}, s32[1,8]{1,0:T(1,128)}, u32[]{:S(2)}) copy-start(s32[1,8]{1,0:T(1,128)} %param.18) | copy-start | bytes 100
  5.1 3.0 %copy-start.4 = (s32[1,8,16,256]{3,2,1,0:T(8,128)S(1)}, s32[1,8,16,256]{3,2,1,0:T(8,128)}, u32[]{:S(2)}) copy-start(s32[1,8,16,256]{3,2,1,0:T(8,128)} %param.21) | copy-start | bytes 393220
  5.1 3.0 %copy-start.5 = (s32[1,8,16,256]{3,2,1,0:T(8,128)S(1)}, s32[1,8,16,256]{3,2,1,0:T(8,128)}, u32[]{:S(2)}) copy-start(s32[1,8,16,256]{3,2,1,0:T(8,128)} %param.20) | copy-start | bytes 393220
  5.1 14.7 %collective-permute-start.2 = (f32[512,128]{1,0:T(8,128)S(1)}, f32[512,128]{1,0:T(8,128)S(1)}, u32[]{:S(2)}, u32[]{:S(2)}) collective-permute-start(f32[512,128]{1,0:T(8,128)S(1)} %get-tuple-element.29.refs_4_), channel_id=1, source_target_pairs={{0,8},{2,10},{8,16},{10,18},{16,24},{18,26},{24,28},{26,30},{28,20... | collective-permute-start | bytes 786440 | tf_op jit(solution)/shard_map/ppermute | solution.py:170
  7.1 10.7 %collective-permute-start.9 = (f32[512,128]{1,0:T(8,128)S(1)}, f32[512,128]{1,0:T(8,128)S(1)}, u32[]{:S(2)}, u32[]{:S(2)}) collective-permute-start(f32[512,128]{1,0:T(8,128)S(1)} %get-tuple-element.29.refs_4_), channel_id=1, source_target_pairs={{0,4},{2,6},{8,0},{10,2},{16,8},{18,10},{24,16},{26,18},{28,24},{3... | collective-permute-start | bytes 786440 | tf_op jit(solution)/shard_map/ppermute | solution.py:170
  7.2 0.7 copy-start.6
  7.3 0.7 copy-start.7
  8.2 1.6 %collective-permute-start = (s32[4,56,256]{2,1,0:T(8,128)S(1)}, s32[4,56,256]{2,1,0:T(8,128)S(1)}, u32[]{:S(2)}, u32[]{:S(2)}) collective-permute-start(s32[4,56,256]{2,1,0:T(8,128)S(1)} %pad_add_fusion.2), channel_id=1, source_target_pairs={{0,2},{2,0},{4,6},{6,4},{8,10},{10,8},{12,14},{14,12},{16,18},{18,... | collective-permute-start | bytes 688136 | tf_op jit(solution)/shard_map/ppermute | solution.py:173
  10.5 24.2 %collective-permute-start.1 = (s32[8,56,256]{2,1,0:T(8,128)}, s32[8,56,256]{2,1,0:T(8,128)}, u32[]{:S(2)}, u32[]{:S(2)}) collective-permute-start(s32[8,56,256]{2,1,0:T(8,128)} %pad_add_fusion.1), channel_id=1, source_target_pairs={{0,1},{1,0},{2,3},{3,2},{4,5},{5,4},{6,7},{7,6},{8,9},{9,8},{10,11... | collective-permute-start | bytes 1376264 | tf_op jit(solution)/shard_map/ppermute | solution.py:176
  12.4 11.0 %collective-permute-start.13 = (f32[512,128]{1,0:T(8,128)S(1)}, f32[512,128]{1,0:T(8,128)S(1)}, u32[]{:S(2)}, u32[]{:S(2)}) collective-permute-start(f32[512,128]{1,0:T(8,128)S(1)} %collective-permute-done.12.refs_7_), channel_id=1, source_target_pairs={{0,4},{2,6},{8,0},{10,2},{16,8},{18,10},{24,16},{26,18},{28,24},{3... | collective-permute-start | bytes 786440 | tf_op jit(solution)/shard_map/ppermute | solution.py:170
  17.8 11.3 %collective-permute-start.10 = (f32[512,128]{1,0:T(8,128)S(1)}, f32[512,128]{1,0:T(8,128)S(1)}, u32[]{:S(2)}, u32[]{:S(2)}) collective-permute-start(f32[512,128]{1,0:T(8,128)S(1)} %collective-permute-done.9.refs_6_), channel_id=1, source_target_pairs={{0,4},{2,6},{8,0},{10,2},{16,8},{18,10},{24,16},{26,18},{28,24},{3... | collective-permute-start | bytes 786440 | tf_op jit(solution)/shard_map/ppermute | solution.py:170
  19.8 9.2 %collective-permute-start.3 = (f32[512,128]{1,0:T(8,128)S(1)}, f32[512,128]{1,0:T(8,128)S(1)}, u32[]{:S(2)}, u32[]{:S(2)}) collective-permute-start(f32[512,128]{1,0:T(8,128)S(1)} %collective-permute-done.2.refs_4_), channel_id=1, source_target_pairs={{0,8},{2,10},{8,16},{10,18},{16,24},{18,26},{24,28},{26,30},{28,20... | collective-permute-start | bytes 786440 | tf_op jit(solution)/shard_map/ppermute | solution.py:170
  19.9 14.8 %collective-permute-start.7 = (f32[512,128]{1,0:T(8,128)S(1)}, f32[512,128]{1,0:T(8,128)S(1)}, u32[]{:S(2)}, u32[]{:S(2)}) collective-permute-start(f32[512,128]{1,0:T(8,128)S(1)} %collective-permute-done.6.refs_5_), channel_id=1, source_target_pairs={{0,8},{2,10},{8,16},{10,18},{16,24},{18,26},{24,28},{26,30},{28,20... | collective-permute-start | bytes 786440 | tf_op jit(solution)/shard_map/ppermute | solution.py:170
  23.4 15.3 %collective-permute-start.14 = (f32[512,128]{1,0:T(8,128)S(1)}, f32[512,128]{1,0:T(8,128)S(1)}, u32[]{:S(2)}, u32[]{:S(2)}) collective-permute-start(f32[512,128]{1,0:T(8,128)S(1)} %collective-permute-done.13.refs_7_), channel_id=1, source_target_pairs={{0,4},{2,6},{8,0},{10,2},{16,8},{18,10},{24,16},{26,18},{28,24},{3... | collective-permute-start | bytes 786440 | tf_op jit(solution)/shard_map/ppermute | solution.py:170
  29.0 18.1 %collective-permute-start.4 = (f32[512,128]{1,0:T(8,128)S(1)}, f32[512,128]{1,0:T(8,128)S(1)}, u32[]{:S(2)}, u32[]{:S(2)}) collective-permute-start(f32[512,128]{1,0:T(8,128)S(1)} %collective-permute-done.3.refs_4_), channel_id=1, source_target_pairs={{0,8},{2,10},{8,16},{10,18},{16,24},{18,26},{24,28},{26,30},{28,20... | collective-permute-start | bytes 786440 | tf_op jit(solution)/shard_map/ppermute | solution.py:170
  29.1 18.8 %collective-permute-start.11 = (f32[512,128]{1,0:T(8,128)S(1)}, f32[512,128]{1,0:T(8,128)S(1)}, u32[]{:S(2)}, u32[]{:S(2)}) collective-permute-start(f32[512,128]{1,0:T(8,128)S(1)} %collective-permute-done.10.refs_6_), channel_id=1, source_target_pairs={{0,4},{2,6},{8,0},{10,2},{16,8},{18,10},{24,16},{26,18},{28,24},{3... | collective-permute-start | bytes 786440 | tf_op jit(solution)/shard_map/ppermute | solution.py:170
  34.6 13.3 %collective-permute-start.8 = (f32[512,128]{1,0:T(8,128)S(1)}, f32[512,128]{1,0:T(8,128)S(1)}, u32[]{:S(2)}, u32[]{:S(2)}) collective-permute-start(f32[512,128]{1,0:T(8,128)S(1)} %collective-permute-done.7.refs_5_), channel_id=1, source_target_pairs={{0,8},{2,10},{8,16},{10,18},{16,24},{18,26},{24,28},{26,30},{28,20... | collective-permute-start | bytes 786440 | tf_op jit(solution)/shard_map/ppermute | solution.py:170
  38.8 12.4 %collective-permute-start.17 = (f32[512,128]{1,0:T(8,128)S(1)}, f32[512,128]{1,0:T(8,128)S(1)}, u32[]{:S(2)}, u32[]{:S(2)}) collective-permute-start(f32[512,128]{1,0:T(8,128)S(1)} %collective-permute-done.14.refs_7_), channel_id=1, source_target_pairs={{0,4},{2,6},{8,0},{10,2},{16,8},{18,10},{24,16},{26,18},{28,24},{3... | collective-permute-start | bytes 786440 | tf_op jit(solution)/shard_map/ppermute | solution.py:170
  47.1 6.5 %collective-permute-start.5 = (f32[512,128]{1,0:T(8,128)S(1)}, f32[512,128]{1,0:T(8,128)S(1)}, u32[]{:S(2)}, u32[]{:S(2)}) collective-permute-start(f32[512,128]{1,0:T(8,128)S(1)} %collective-permute-done.4.refs_4_), channel_id=1, source_target_pairs={{0,8},{2,10},{8,16},{10,18},{16,24},{18,26},{24,28},{26,30},{28,20... | collective-permute-start | bytes 786440 | tf_op jit(solution)/shard_map/ppermute | solution.py:170
  53.6 2.6 %collective-permute-start.18 = (f32[1024,128]{1,0:T(8,128)S(1)}, f32[1024,128]{1,0:T(8,128)S(1)}, u32[]{:S(2)}, u32[]{:S(2)}) collective-permute-start(f32[1024,128]{1,0:T(8,128)S(1)} %get-tuple-element.28), channel_id=1, source_target_pairs={{0,2},{2,0},{4,6},{6,4},{8,10},{10,8},{12,14},{14,12},{16,18},{18,... | collective-permute-start | bytes 1572872 | tf_op jit(solution)/shard_map/ppermute | solution.py:173
  56.1 2.0 %collective-permute-start.15 = (f32[1024,128]{1,0:T(8,128)S(1)}, f32[1024,128]{1,0:T(8,128)S(1)}, u32[]{:S(2)}, u32[]{:S(2)}) collective-permute-start(f32[1024,128]{1,0:T(8,128)S(1)} %get-tuple-element.25), channel_id=1, source_target_pairs={{0,2},{2,0},{4,6},{6,4},{8,10},{10,8},{12,14},{14,12},{16,18},{18,... | collective-permute-start | bytes 1572872 | tf_op jit(solution)/shard_map/ppermute | solution.py:173
  56.2 2.5 %copy-start.1 = (f32[512,256]{1,0:T(8,128)S(1)}, f32[512,256]{1,0:T(8,128)}, u32[]{:S(2)}) copy-start(f32[512,256]{1,0:T(8,128)} %param.11) | copy-start | bytes 1572868
  56.2 9.2 %collective-permute-start.19 = (f32[512,128]{1,0:T(8,128)S(1)}, f32[512,128]{1,0:T(8,128)S(1)}, u32[]{:S(2)}, u32[]{:S(2)}) collective-permute-start(f32[512,128]{1,0:T(8,128)S(1)} %slice_add_fusion), channel_id=1, source_target_pairs={{0,1},{1,0},{2,3},{3,2},{4,5},{5,4},{6,7},{7,6},{8,9},{9,8},{10,11... | collective-permute-start | bytes 786440 | tf_op jit(solution)/shard_map/ppermute | solution.py:176
  58.1 0.7 copy-start.8
  58.1 7.3 %copy-start.2 = (f32[256,256]{1,0:T(8,128)S(1)}, f32[256,256]{1,0:T(8,128)}, u32[]{:S(2)}) copy-start(f32[256,256]{1,0:T(8,128)} %param.14) | copy-start | bytes 786436
  58.1 12.5 %collective-permute-start.16 = (f32[512,128]{1,0:T(8,128)S(1)}, f32[512,128]{1,0:T(8,128)S(1)}, u32[]{:S(2)}, u32[]{:S(2)}) collective-permute-start(f32[512,128]{1,0:T(8,128)S(1)} %slice_add_fusion.2), channel_id=1, source_target_pairs={{0,1},{1,0},{2,3},{3,2},{4,5},{5,4},{6,7},{7,6},{8,9},{9,8},{10,11... | collective-permute-start | bytes 786440 | tf_op jit(solution)/shard_map/ppermute | solution.py:176

commit v2 on v1

--- a/solution.py
+++ b/solution.py
@@ -33,10 +33,11 @@
     return jnp.concatenate(bf16_pair(matrix), axis=1)
 
 
-def sum_kernel(sources, chunks, slots, first, last, *refs):
+def sum_kernel(sources, chunks, pieces, slots, first, last, *refs):
     pairs, place, meta, edges = refs[:4]
     refs = refs[4:]
-    parts, refs = refs[: sources * chunks], refs[sources * chunks :]
+    count = sources * chunks * pieces
+    parts, refs = refs[:count], refs[count:]
     if not first:
         before, refs = refs[:chunks], refs[chunks:]
     if last:
@@ -50,7 +51,7 @@
     for chunk in range(chunks):
         if first:
             sums[chunk][...] = jnp.zeros_like(sums[chunk])
-        else:
+        elif last:
             sums[chunk][...] = before[chunk][...]
 
     used = jnp.int32(0)
@@ -68,14 +69,17 @@
 
     for source in range(sources):
         for chunk in range(chunks):
-            part = parts[source * chunks + chunk]
             left = 2 * TILE * chunk
-            for tile in range(tiles_here):
-                high, low = bf16_pair(part[tile * TILE : (tile + 1) * TILE, :])
-                for half in range(2):
-                    below = half * TILE
-                    sides[source, tile, below : below + TILE, left : left + TILE] = high
-                    sides[source, tile, below : below + TILE, left + TILE : left + 2 * TILE] = low
+            for piece in range(pieces):
+                part = parts[(source * chunks + chunk) * pieces + piece]
+                size = min(part.shape[0], TILE)
+                for start in range(0, part.shape[0], size):
+                    at = piece * part.shape[0] + start
+                    high, low = bf16_pair(part[start : start + size, :])
+                    for half in range(2):
+                        below = half * TILE + at % TILE
+                        sides[source, at // TILE, below : below + size, left : left + TILE] = high
+                        sides[source, at // TILE, below : below + size, left + TILE : left + 2 * TILE] = low
 
     def group(step, carry):
         todo = []
@@ -109,29 +113,34 @@
 
 
 def add_sources(pairs, place, meta, edges, parts, before, rows, slots, last=False):
-    sources, chunks = len(parts), len(parts[0])
-    flat = [chunk for source in parts for chunk in source]
-    here, width = flat[0].shape
+    sources, chunks, pieces = len(parts), len(parts[0]), len(parts[0][0])
+    flat = [piece for source in parts for chunk in source for piece in chunk]
+    here, width = pieces * flat[0].shape[0], flat[0].shape[1]
     first = before is None
     whole = jax.ShapeDtypeStruct((2, rows, width), jnp.float32)
     block = jax.ShapeDtypeStruct((rows, width), jnp.float32)
     olds = [] if first else list(before)
-    outs = [block] * (2 * chunks) if last else [whole] * chunks
+    outs = [block] * (2 * chunks) if last else [pltpu.VMEM(whole.shape, whole.dtype)] * chunks
     scratch = [
         pltpu.VMEM((sources, here // TILE, 2 * TILE, 2 * TILE * chunks), jnp.bfloat16),
         pltpu.SMEM((2 * sources * slots + UNROLL,), jnp.int32),
     ]
+    aliases = {}
     if last:
         scratch += [pltpu.VMEM(whole.shape, jnp.float32)] * chunks
-    flops = 2 * sources * 8 * 2 * TILE * TILE * (256 + 4 * TILE * chunks)
+    elif not first:
+        olds = [pltpu.with_memory_space_constraint(old, pltpu.VMEM) for old in olds]
+        aliases = {4 + len(flat) + chunk: chunk for chunk in range(chunks)}
+    flops = 1_000_000_000 * (1 + sources * chunks)
     return pl.pallas_call(
-        functools.partial(sum_kernel, sources, chunks, slots, first, last),
+        functools.partial(sum_kernel, sources, chunks, pieces, slots, first, last),
         in_specs=[SMEM] * 3 + [VMEM] * (1 + len(flat) + len(olds)),
         out_specs=[VMEM] * len(outs),
         out_shape=outs,
         scratch_shapes=scratch,
+        input_output_aliases=aliases,
         compiler_params=pltpu.CompilerParams(vmem_limit_bytes=24 << 20),
-        cost_estimate=pl.CostEstimate(flops=flops, bytes_accessed=4 << 20, transcendentals=0),
+        cost_estimate=pl.CostEstimate(flops=flops, bytes_accessed=1 << 20, transcendentals=0),
     )(pairs, place, meta, edges, *flat, *olds)
 
 
@@ -188,19 +197,21 @@
         head = jnp.pad(head, ((0, 0), (0, 7), (0, 0)))
         return jnp.concatenate(lists + [head], axis=1)
 
-    own_lists = bundle(0)
-    sibling_lists = core_swap(bundle(1))
-    lists = jnp.concatenate([own_lists, sibling_lists], axis=0)
+    own_lists, others_lists = bundle(0), bundle(1)
     if groups == 2:
-        edges = jnp.concatenate([lists, rep_swap(lists)], axis=0)
+        own_far = rep_swap(own_lists)
+        sibling_lists = core_swap(others_lists)
+        edges = jnp.concatenate([own_lists, own_far, sibling_lists, rep_swap(sibling_lists)], axis=0)
     else:
-        edges = lax.all_gather(lists, "rep", axis=0, tiled=True)
+        lists = jnp.concatenate([own_lists, core_swap(others_lists)], axis=1)
+        lists = lax.all_gather(lists, "rep", axis=0, tiled=True)
+        edges = jnp.concatenate([lists[:, : own_lists.shape[1]], lists[:, own_lists.shape[1] :]], axis=0)
     meta = edges[:, 3 * slots, :TILE]
 
     def list_place(offset, which):
         group = offset // per
         group = group ^ replica if groups == 2 else group
-        return (2 * group + which) * per + offset % per
+        return (which * groups + group) * per + offset % per
 
     position = jnp.where(chip % 2 == 0, chip // 2, lanes - 1 - chip // 2)
 
@@ -221,21 +232,21 @@
 
     root = jnp.dot(features, root_weight, precision=highest) + bias
 
+    half = shard // 2
     up, down = own, own
-    totals = None
-    for step in range(1, lanes // 2 + 1):
-        last = step == lanes // 2
-        up = [ring(v, 1) if f % 2 == 0 or not last else None for f, v in enumerate(up)]
-        down = [ring(v, -1) if f % 2 == 1 or not last else None for f, v in enumerate(down)]
-        if step == 1:
-            totals = add(pairs_of([0]), place, meta, edges, [own], None)
-        if not last:
-            totals = add(pairs_of([-step, step]), place, meta, edges, [up, down], totals)
+    totals = add(pairs_of([0]), place, meta, edges, [[[v] for v in own]], None)
+    for step in range(1, lanes // 2):
+        up, down = [ring(v, 1) for v in up], [ring(v, -1) for v in down]
+        if step == lanes // 2 - 1:
+            for f in range(chunks):
+                up[f], down[f], totals = lax.optimization_barrier((up[f], down[f], totals))
+        parts = [[[v] for v in up], [[v] for v in down]]
+        totals = add(pairs_of([-step, step]), place, meta, edges, parts, totals)
+    ends = [[ring(up[f][:half], 1), ring(down[f][half:], -1)] for f in range(chunks)]
     pairs = pairs_of([lanes // 2])
     hidden = root
     for f in range(chunks):
-        end = up[f] if f % 2 == 0 else down[f]
-        own_sum, sibling_sum = add(pairs, place, meta, edges, [[end]], [totals[f]], last=True)
+        own_sum, sibling_sum = add(pairs, place, meta, edges, [[ends[f]]], [totals[f]], last=True)
         swapped = core_swap(sibling_sum)
         if groups == 2:
             other = rep_swap(own_sum[shard:] + swapped[shard:])

time: 71.9 us -> 73.7 us (1.025)
  starting transfers between devices: 20.5 us -> 26.1 us
  Pallas kernels: 18 us -> 14.9 us
  other arithmetic: 4.48 us -> 2.67 us
    ppermute x3 -> x4, starting transfers between devices: 3.04 us -> 6.7 us  [rep_swap(): return lax.ppermute(value, 'rep', [(0, 1), (1, 0)])]
    pallas_call x6, Pallas kernels: 18 us -> 14.9 us  [add_sources(): pl.pallas_call(functools.partial(sum_kernel, sources, chunks, pieces, slo...]
    ppermute x3, waiting for transfers between devices: 2 us -> 0.01 us  [core_swap(): return lax.ppermute(value, 'blk', [(b, b ^ 1) for b in range(blocks)])]
    concatenate x2 -> x1, other arithmetic: 1.89 us -> 0.07 us  [on_device(): jnp.concatenate([own_lists, own_far, sibling_lists, rep_swap(sibling_list...]
    ppermute x3 -> x4, waiting for transfers between devices: 10.7 us -> 12.5 us  [rep_swap(): return lax.ppermute(value, 'rep', [(0, 1), (1, 0)])]
    ppermute x14 -> x16, starting transfers between devices: 17.2 us -> 18.7 us  [ring(): return lax.ppermute(value, 'blk', pairs)]
    ppermute x14 -> x16, waiting for transfers between devices: 11.7 us -> 12.5 us  [ring(): return lax.ppermute(value, 'blk', pairs)]
  transfers between devices with their start and end apart: 20 -> 23, of which waited for: 8 -> 10; matrix products, arithmetic and copies ran while one was open for 6% -> 3% of each run, Pallas kernels for 25% -> 20%
where the time goes in v2:
time: 73.7 us; the launch traced here: 73.1 us
  starting transfers between devices  26.1 us (35%)
  waiting for transfers between devices  25 us (34%)
  Pallas kernels  14.9 us (20%)
  other arithmetic  2.67 us (4%)
  matrix products  2.61 us (4%)
  local copies, waits for them, and re-layouts  1.22 us (2%)
    ppermute x16, starting transfers between devices, ring(): return lax.ppermute(value, 'blk', pairs)  18.7 us
    pallas_call x6, Pallas kernels, add_sources(): pl.pallas_call(functools.partial(sum_kernel, sources, chunks, pieces, slo...  14.9 us
    ppermute x16, waiting for transfers between devices, ring(): return lax.ppermute(value, 'blk', pairs)  12.5 us
    ppermute x4, waiting for transfers between devices, rep_swap(): return lax.ppermute(value, 'rep', [(0, 1), (1, 0)])  12.5 us
    ppermute x4, starting transfers between devices, rep_swap(): return lax.ppermute(value, 'rep', [(0, 1), (1, 0)])  6.7 us
    dot_general x2, matrix products, on_device(): jnp.dot(mixed, neighbor_weight[f * TILE:(f + 1) * TILE], precision=highest)  2.03 us
  transfers between devices with their start and end apart: 23, of which 10 were waited for; matrix products, arithmetic and copies ran while one was open for 3% of the time, Pallas kernels for 20%

profile of v2, /device:TPU:0, one launch (start us, length us, event | category | flops | bytes accessed | tf_op | source)
XLA Modules:
  0.0 73.1 jit_solution(14040977518920501313)
XLA Ops:
  0.0 0.7 convert_rsqrt_fusion
  0.7 1.2 %broadcast_multiply_fusion = f32[512,256]{1,0:T(8,128)S(1)} fusion(f32[512,256]{1,0:T(8,128)} %param.11, f32[512]{0:T(512)S(1)} %convert_rsqrt_fusion), kind=kLoop, calls=%fused_computation.16 | loop fusion | flops 131072 | bytes 1050624 | tf_op jit(solution)/shard_map/mul | solution.py:188
  2.0 3.1 %collective-permute-start.3 = (f32[512,128]{1,0:T(8,128)S(1)}, f32[512,128]{1,0:T(8,128)S(1)}, u32[]{:S(2)}, u32[]{:S(2)}) collective-permute-start(f32[512,128]{1,0:T(8,128)S(1)} %get-tuple-element.45.refs_4_), channel_id=1, source_target_pairs={{0,8},{2,10},{8,16},{10,18},{16,24},{18,26},{24,28},{26,30},{28,20... | collective-permute-start | bytes 786440 | tf_op jit(solution)/shard_map/ppermute | solution.py:179
  6.1 2.0 %collective-permute-start = (s32[4,56,256]{2,1,0:T(8,128)S(1)}, s32[4,56,256]{2,1,0:T(8,128)S(1)}, u32[]{:S(2)}, u32[]{:S(2)}) collective-permute-start(s32[4,56,256]{2,1,0:T(8,128)S(1)} %pad_add_fusion.2), channel_id=1, source_target_pairs={{0,1},{1,0},{2,3},{3,2},{4,5},{5,4},{6,7},{7,6},{8,9},{9,8},{10,11... | collective-permute-start | bytes 688136 | tf_op jit(solution)/shard_map/ppermute | solution.py:185
  8.6 1.5 %collective-permute-start.11 = (f32[512,128]{1,0:T(8,128)S(1)}, f32[512,128]{1,0:T(8,128)S(1)}, u32[]{:S(2)}, u32[]{:S(2)}) collective-permute-start(f32[512,128]{1,0:T(8,128)S(1)} %get-tuple-element.46.refs_5_), channel_id=1, source_target_pairs={{0,4},{2,6},{8,0},{10,2},{16,8},{18,10},{24,16},{26,18},{28,24},{3... | collective-permute-start | bytes 786440 | tf_op jit(solution)/shard_map/ppermute | solution.py:179
  10.3 2.9 %collective-permute-done = s32[4,56,256]{2,1,0:T(8,128)S(1)} collective-permute-done((s32[4,56,256]{2,1,0:T(8,128)S(1)}, s32[4,56,256]{2,1,0:T(8,128)S(1)}, u32[]{:S(2)}, u32[]{:S(2)}) %collective-permute-start) | collective-permute-done | bytes 229408 | tf_op jit(solution)/shard_map/ppermute | solution.py:185
  13.2 1.7 %collective-permute-start.9 = (f32[512,128]{1,0:T(8,128)S(1)}, f32[512,128]{1,0:T(8,128)S(1)}, u32[]{:S(2)}, u32[]{:S(2)}) collective-permute-start(f32[512,128]{1,0:T(8,128)S(1)} %get-tuple-element.46.refs_5_), channel_id=1, source_target_pairs={{0,8},{2,10},{8,16},{10,18},{16,24},{18,26},{24,28},{26,30},{28,20... | collective-permute-start | bytes 786440 | tf_op jit(solution)/shard_map/ppermute | solution.py:179
  15.3 1.6 %collective-permute-start.2 = (s32[4,56,256]{2,1,0:T(8,128)S(1)}, s32[4,56,256]{2,1,0:T(8,128)S(1)}, u32[]{:S(2)}, u32[]{:S(2)}) collective-permute-start(s32[4,56,256]{2,1,0:T(8,128)S(1)} %collective-permute-done.1), channel_id=1, source_target_pairs={{0,1},{1,0},{2,3},{3,2},{4,5},{5,4},{6,7},{7,6},{8,9},{9,8},{10,11... | collective-permute-start | bytes 688136 | tf_op jit(solution)/shard_map/ppermute | solution.py:185
  17.1 3.0 %collective-permute-done.9.refs_5_ = f32[512,128]{1,0:T(8,128)S(1)} collective-permute-done((f32[512,128]{1,0:T(8,128)S(1)}, f32[512,128]{1,0:T(8,128)S(1)}, u32[]{:S(2)}, u32[]{:S(2)}) %collective-permute-start.9) | collective-permute-done | bytes 262176 | tf_op jit(solution)/shard_map/ppermute | solution.py:179
  20.1 1.4 %collective-permute-start.10 = (f32[512,128]{1,0:T(8,128)S(1)}, f32[512,128]{1,0:T(8,128)S(1)}, u32[]{:S(2)}, u32[]{:S(2)}) collective-permute-start(f32[512,128]{1,0:T(8,128)S(1)} %collective-permute-done.9.refs_5_), channel_id=1, source_target_pairs={{0,8},{2,10},{8,16},{10,18},{16,24},{18,26},{24,28},{26,30},{28,20... | collective-permute-start | bytes 786440 | tf_op jit(solution)/shard_map/ppermute | solution.py:179
  22.1 1.4 %collective-permute-start.4 = (f32[512,128]{1,0:T(8,128)S(1)}, f32[512,128]{1,0:T(8,128)S(1)}, u32[]{:S(2)}, u32[]{:S(2)}) collective-permute-start(f32[512,128]{1,0:T(8,128)S(1)} %collective-permute-done.3.refs_4_), channel_id=1, source_target_pairs={{0,8},{2,10},{8,16},{10,18},{16,24},{18,26},{24,28},{26,30},{28,20... | collective-permute-start | bytes 786440 | tf_op jit(solution)/shard_map/ppermute | solution.py:179
  24.3 2.2 %shard_map.109 = (f32[2,1024,128]{2,1,0:T(8,128)S(1)}, f32[2,1024,128]{2,1,0:T(8,128)S(1)}) custom-call(s32[2]{0:T(128)S(1)} %pad_add_fusion.9.refs_0_, s32[2]{0:T(128)S(1)} %pad_add_fusion.6.refs_1_, s32[16,128]{1,0:T(8,128)S(1)} %bitcast.39, s32[16,56,256]{2,1,0:T(8,128)S(1)} %pad_add_fusion.refs_3_, f32[512,128]{1,0:T(8,128)S(1)} %get-tuple-element.45.refs_4_, ...), custom_call_target="tpu_custom_call" | custom-call | flops 3000000000 | bytes 1048576 | tf_op jit(solution)/shard_map/pallas_call | solution.py:135
  26.5 2.3 %shard_map.110 = (f32[2,1024,128]{2,1,0:T(8,128)S(1)}, f32[2,1024,128]{2,1,0:T(8,128)S(1)}) custom-call(s32[4]{0:T(128)S(1)} %pad_add_fusion.8.refs_0_, s32[2]{0:T(128)S(1)} %pad_add_fusion.6.refs_1_, s32[16,128]{1,0:T(8,128)S(1)} %bitcast.40, s32[16,56,256]{2,1,0:T(8,128)S(1)} %pad_add_fusion.refs_3_, ...), custom_call_target="tpu_custom_call", output_to_operand_aliasing={{0}: (8, {}), {1}: (9, {})} | custom-call | flops 5000000000 | bytes 1048576 | tf_op jit(solution)/shard_map/pallas_call | solution.py:135
  28.8 3.4 %collective-permute-done.4.refs_4_ = f32[512,128]{1,0:T(8,128)S(1)} collective-permute-done((f32[512,128]{1,0:T(8,128)S(1)}, f32[512,128]{1,0:T(8,128)S(1)}, u32[]{:S(2)}, u32[]{:S(2)}) %collective-permute-start.4) | collective-permute-done | bytes 262176 | tf_op jit(solution)/shard_map/ppermute | solution.py:179
  32.2 1.4 %collective-permute-start.5 = (f32[512,128]{1,0:T(8,128)S(1)}, f32[512,128]{1,0:T(8,128)S(1)}, u32[]{:S(2)}, u32[]{:S(2)}) collective-permute-start(f32[512,128]{1,0:T(8,128)S(1)} %collective-permute-done.4.refs_4_), channel_id=1, source_target_pairs={{0,8},{2,10},{8,16},{10,18},{16,24},{18,26},{24,28},{26,30},{28,20... | collective-permute-start | bytes 786440 | tf_op jit(solution)/shard_map/ppermute | solution.py:179
  34.2 1.4 %collective-permute-start.15 = (f32[512,128]{1,0:T(8,128)S(1)}, f32[512,128]{1,0:T(8,128)S(1)}, u32[]{:S(2)}, u32[]{:S(2)}) collective-permute-start(f32[512,128]{1,0:T(8,128)S(1)} %collective-permute-done.10.refs_5_), channel_id=1, source_target_pairs={{0,8},{2,10},{8,16},{10,18},{16,24},{18,26},{24,28},{26,30},{28,20... | collective-permute-start | bytes 786440 | tf_op jit(solution)/shard_map/ppermute | solution.py:179
  36.2 3.6 %shard_map.111 = (f32[2,1024,128]{2,1,0:T(8,128)S(1)}, f32[2,1024,128]{2,1,0:T(8,128)S(1)}) custom-call(s32[4]{0:T(128)S(1)} %pad_add_fusion.7.refs_0_, s32[2]{0:T(128)S(1)} %pad_add_fusion.6.refs_1_, s32[16,128]{1,0:T(8,128)S(1)} %bitcast.41, s32[16,56,256]{2,1,0:T(8,128)S(1)} %pad_add_fusion.refs_3_, ...), custom_call_target="tpu_custom_call", output_to_operand_aliasing={{0}: (8, {}), {1}: (9, {})} | custom-call | flops 5000000000 | bytes 1048576 | tf_op jit(solution)/shard_map/pallas_call | solution.py:135
  40.1 0.9 %collective-permute-done.8.refs_6_ = f32[512,128]{1,0:T(8,128)S(1)} collective-permute-done((f32[512,128]{1,0:T(8,128)S(1)}, f32[512,128]{1,0:T(8,128)S(1)}, u32[]{:S(2)}, u32[]{:S(2)}) %collective-permute-start.8) | collective-permute-done | bytes 262176 | tf_op jit(solution)/shard_map/ppermute | solution.py:179
  40.9 3.0 %collective-permute-done.15.refs_5_ = f32[512,128]{1,0:T(8,128)S(1)} collective-permute-done((f32[512,128]{1,0:T(8,128)S(1)}, f32[512,128]{1,0:T(8,128)S(1)}, u32[]{:S(2)}, u32[]{:S(2)}) %collective-permute-start.15) | collective-permute-done | bytes 262176 | tf_op jit(solution)/shard_map/ppermute | solution.py:179
  44.3 1.6 %collective-permute-start.13 = (f32[256,128]{1,0:T(8,128)S(1)}, f32[256,128]{1,0:T(8,128)S(1)}, u32[]{:S(2)}, u32[]{:S(2)}) collective-permute-start(f32[256,128]{1,0:T(8,128)S(1)} %slice.102), channel_id=1, source_target_pairs={{0,8},{2,10},{8,16},{10,18},{16,24},{18,26},{24,28},{26,30},{28,20... | collective-permute-start | bytes 393224 | tf_op jit(solution)/shard_map/ppermute | solution.py:179
  46.5 1.6 %collective-permute-start.19 = (f32[256,128]{1,0:T(8,128)S(1)}, f32[256,128]{1,0:T(8,128)S(1)}, u32[]{:S(2)}, u32[]{:S(2)}) collective-permute-start(f32[256,128]{1,0:T(8,128)S(1)} %slice.109), channel_id=1, source_target_pairs={{0,8},{2,10},{8,16},{10,18},{16,24},{18,26},{24,28},{26,30},{28,20... | collective-permute-start | bytes 393224 | tf_op jit(solution)/shard_map/ppermute | solution.py:179
  48.6 3.0 %shard_map.112 = (f32[2,1024,128]{2,1,0:T(8,128)S(1)}, f32[2,1024,128]{2,1,0:T(8,128)S(1)}) custom-call(s32[4]{0:T(128)S(1)} %pad_add_fusion.10.refs_0_, s32[2]{0:T(128)S(1)} %pad_add_fusion.6.refs_1_, s32[16,128]{1,0:T(8,128)S(1)} %bitcast.42, s32[16,56,256]{2,1,0:T(8,128)S(1)} %pad_add_fusion.refs_3_, ...), custom_call_target="tpu_custom_call", output_to_operand_aliasing={{0}: (8, {}), {1}: (9, {})} | custom-call | flops 5000000000 | bytes 1048576 | tf_op jit(solution)/shard_map/pallas_call | solution.py:135
  51.6 1.6 %collective-permute-done.20.refs_5_ = f32[256,128]{1,0:T(8,128)S(1)} collective-permute-done((f32[256,128]{1,0:T(8,128)S(1)}, f32[256,128]{1,0:T(8,128)S(1)}, u32[]{:S(2)}, u32[]{:S(2)}) %collective-permute-start.20) | collective-permute-done | bytes 131104 | tf_op jit(solution)/shard_map/ppermute | solution.py:179
  53.2 1.9 %shard_map.114 = (f32[1024,128]{1,0:T(8,128)S(1)}, f32[1024,128]{1,0:T(8,128)S(1)}) custom-call(s32[2]{0:T(128)S(1)} %pad_add_fusion.5.refs_0_, s32[2]{0:T(128)S(1)} %pad_add_fusion.6.refs_1_, s32[16,128]{1,0:T(8,128)S(1)} %bitcast.43, s32[16,56,256]{2,1,0:T(8,128)S(1)} %pad_add_fusion.refs_3_, f32[256,128]{1,0:T(8,128)S(1)} %collective-permute-done.19.refs_4_, ...), custom_call_target="tpu_custom_call" | custom-call | flops 2000000000 | bytes 1048576 | tf_op jit(solution)/shard_map/pallas_call | solution.py:135
  55.2 1.9 %shard_map.113 = (f32[1024,128]{1,0:T(8,128)S(1)}, f32[1024,128]{1,0:T(8,128)S(1)}) custom-call(s32[2]{0:T(128)S(1)} %pad_add_fusion.5.refs_0_, s32[2]{0:T(128)S(1)} %pad_add_fusion.6.refs_1_, s32[16,128]{1,0:T(8,128)S(1)} %bitcast.44, s32[16,56,256]{2,1,0:T(8,128)S(1)} %pad_add_fusion.refs_3_, f32[256,128]{1,0:T(8,128)S(1)} %collective-permute-done.13.refs_4_, ...), custom_call_target="tpu_custom_call" | custom-call | flops 2000000000 | bytes 1048576 | tf_op jit(solution)/shard_map/pallas_call | solution.py:135
  57.8 1.6 %collective-permute-start.22 = (f32[512,128]{1,0:T(8,128)S(1)}, f32[512,128]{1,0:T(8,128)S(1)}, u32[]{:S(2)}, u32[]{:S(2)}) collective-permute-start(f32[512,128]{1,0:T(8,128)S(1)} %slice_add_fusion), channel_id=1, source_target_pairs={{0,1},{1,0},{2,3},{3,2},{4,5},{5,4},{6,7},{7,6},{8,9},{9,8},{10,11... | collective-permute-start | bytes 786440 | tf_op jit(solution)/shard_map/ppermute | solution.py:185
  59.4 1.5 %collective-permute-start.18 = (f32[512,128]{1,0:T(8,128)S(1)}, f32[512,128]{1,0:T(8,128)S(1)}, u32[]{:S(2)}, u32[]{:S(2)}) collective-permute-start(f32[512,128]{1,0:T(8,128)S(1)} %slice_add_fusion.2), channel_id=1, source_target_pairs={{0,1},{1,0},{2,3},{3,2},{4,5},{5,4},{6,7},{7,6},{8,9},{9,8},{10,11... | collective-permute-start | bytes 786440 | tf_op jit(solution)/shard_map/ppermute | solution.py:185
  60.9 0.6 convolution_add_fusion.1
  61.5 5.5 %collective-permute-done.22 = f32[512,128]{1,0:T(8,128)S(1)} collective-permute-done((f32[512,128]{1,0:T(8,128)S(1)}, f32[512,128]{1,0:T(8,128)S(1)}, u32[]{:S(2)}, u32[]{:S(2)}) %collective-permute-start.22) | collective-permute-done | bytes 262176 | tf_op jit(solution)/shard_map/ppermute | solution.py:185
  67.0 0.6 fusion.4
  67.6 4.1 %collective-permute-done.18 = f32[512,128]{1,0:T(8,128)S(1)} collective-permute-done((f32[512,128]{1,0:T(8,128)S(1)}, f32[512,128]{1,0:T(8,128)S(1)}, u32[]{:S(2)}, u32[]{:S(2)}) %collective-permute-start.18) | collective-permute-done | bytes 262176 | tf_op jit(solution)/shard_map/ppermute | solution.py:185
  71.7 1.4 %fusion.1 = f32[512,256]{1,0:T(8,128)} fusion(f32[512,256]{1,0:T(8,128)S(1)} %fusion.4, f32[512,256]{1,0:T(8,128)S(1)} %convolution_add_fusion.1, f32[512,128]{1,0:T(8,128)S(1)} %collective-permute-done.18, f32[1024,128]{1,0:T(8,128)S(1)} %collective-permute-done.17, f32[1024,128]{1,0:T(8,128)S(1)} %get-tuple-element.40, f32[256,256]{1,0:T(8,128)S(1)} %copy-done.2, ...), kind=kOutput, calls=%fused_computation.2 | convolution fusion | flops 201916416 | bytes 2492416 | tf_op jit(solution)/shard_map/dot_general | solution.py:257
  (79 shorter events, 6.7 us)
Async XLA Ops:
  0.0 60.9 %copy-start = (f32[256,256]{1,0:T(8,128)S(1)}, f32[256,256]{1,0:T(8,128)}, u32[]{:S(2)}) copy-start(f32[256,256]{1,0:T(8,128)} %param.13) | copy-start | bytes 786436
  1.9 3.2 %copy-start.3 = (s32[1,8,16,256]{3,2,1,0:T(8,128)S(1)}, s32[1,8,16,256]{3,2,1,0:T(8,128)}, u32[]{:S(2)}) copy-start(s32[1,8,16,256]{3,2,1,0:T(8,128)} %param.19) | copy-start | bytes 393220
  2.0 3.1 %copy-start.9 = (s32[1,8]{1,0:T(1,128)S(1)}, s32[1,8]{1,0:T(1,128)}, u32[]{:S(2)}) copy-start(s32[1,8]{1,0:T(1,128)} %param.18) | copy-start | bytes 100
  2.0 4.1 %copy-start.4 = (s32[1,8,16,256]{3,2,1,0:T(8,128)S(1)}, s32[1,8,16,256]{3,2,1,0:T(8,128)}, u32[]{:S(2)}) copy-start(s32[1,8,16,256]{3,2,1,0:T(8,128)} %param.21) | copy-start | bytes 393220
  2.0 4.1 %copy-start.5 = (s32[1,8,16,256]{3,2,1,0:T(8,128)S(1)}, s32[1,8,16,256]{3,2,1,0:T(8,128)}, u32[]{:S(2)}) copy-start(s32[1,8,16,256]{3,2,1,0:T(8,128)} %param.20) | copy-start | bytes 393220
  2.0 20.1 %collective-permute-start.3 = (f32[512,128]{1,0:T(8,128)S(1)}, f32[512,128]{1,0:T(8,128)S(1)}, u32[]{:S(2)}, u32[]{:S(2)}) collective-permute-start(f32[512,128]{1,0:T(8,128)S(1)} %get-tuple-element.45.refs_4_), channel_id=1, source_target_pairs={{0,8},{2,10},{8,16},{10,18},{16,24},{18,26},{24,28},{26,30},{28,20... | collective-permute-start | bytes 786440 | tf_op jit(solution)/shard_map/ppermute | solution.py:179
  5.1 18.5 %collective-permute-start.6 = (f32[512,128]{1,0:T(8,128)S(1)}, f32[512,128]{1,0:T(8,128)S(1)}, u32[]{:S(2)}, u32[]{:S(2)}) collective-permute-start(f32[512,128]{1,0:T(8,128)S(1)} %get-tuple-element.45.refs_4_), channel_id=1, source_target_pairs={{0,4},{2,6},{8,0},{10,2},{16,8},{18,10},{24,16},{26,18},{28,24},{3... | collective-permute-start | bytes 786440 | tf_op jit(solution)/shard_map/ppermute | solution.py:179
  5.1 0.7 copy-start.6
  6.1 7.1 %collective-permute-start = (s32[4,56,256]{2,1,0:T(8,128)S(1)}, s32[4,56,256]{2,1,0:T(8,128)S(1)}, u32[]{:S(2)}, u32[]{:S(2)}) collective-permute-start(s32[4,56,256]{2,1,0:T(8,128)S(1)} %pad_add_fusion.2), channel_id=1, source_target_pairs={{0,1},{1,0},{2,3},{3,2},{4,5},{5,4},{6,7},{7,6},{8,9},{9,8},{10,11... | collective-permute-start | bytes 688136 | tf_op jit(solution)/shard_map/ppermute | solution.py:185
  8.5 6.9 %collective-permute-start.1 = (s32[4,56,256]{2,1,0:T(8,128)S(1)}, s32[4,56,256]{2,1,0:T(8,128)S(1)}, u32[]{:S(2)}, u32[]{:S(2)}) collective-permute-start(s32[4,56,256]{2,1,0:T(8,128)S(1)} %pad_add_fusion.1), channel_id=1, source_target_pairs={{0,2},{2,0},{4,6},{6,4},{8,10},{10,8},{12,14},{14,12},{16,18},{18,... | collective-permute-start | bytes 688136 | tf_op jit(solution)/shard_map/ppermute | solution.py:182
  8.6 13.0 %collective-permute-start.11 = (f32[512,128]{1,0:T(8,128)S(1)}, f32[512,128]{1,0:T(8,128)S(1)}, u32[]{:S(2)}, u32[]{:S(2)}) collective-permute-start(f32[512,128]{1,0:T(8,128)S(1)} %get-tuple-element.46.refs_5_), channel_id=1, source_target_pairs={{0,4},{2,6},{8,0},{10,2},{16,8},{18,10},{24,16},{26,18},{28,24},{3... | collective-permute-start | bytes 786440 | tf_op jit(solution)/shard_map/ppermute | solution.py:179
  13.2 6.9 %collective-permute-start.9 = (f32[512,128]{1,0:T(8,128)S(1)}, f32[512,128]{1,0:T(8,128)S(1)}, u32[]{:S(2)}, u32[]{:S(2)}) collective-permute-start(f32[512,128]{1,0:T(8,128)S(1)} %get-tuple-element.46.refs_5_), channel_id=1, source_target_pairs={{0,8},{2,10},{8,16},{10,18},{16,24},{18,26},{24,28},{26,30},{28,20... | collective-permute-start | bytes 786440 | tf_op jit(solution)/shard_map/ppermute | solution.py:179
  15.3 8.8 %collective-permute-start.2 = (s32[4,56,256]{2,1,0:T(8,128)S(1)}, s32[4,56,256]{2,1,0:T(8,128)S(1)}, u32[]{:S(2)}, u32[]{:S(2)}) collective-permute-start(s32[4,56,256]{2,1,0:T(8,128)S(1)} %collective-permute-done.1), channel_id=1, source_target_pairs={{0,1},{1,0},{2,3},{3,2},{4,5},{5,4},{6,7},{7,6},{8,9},{9,8},{10,11... | collective-permute-start | bytes 688136 | tf_op jit(solution)/shard_map/ppermute | solution.py:185
  20.1 14.1 %collective-permute-start.10 = (f32[512,128]{1,0:T(8,128)S(1)}, f32[512,128]{1,0:T(8,128)S(1)}, u32[]{:S(2)}, u32[]{:S(2)}) collective-permute-start(f32[512,128]{1,0:T(8,128)S(1)} %collective-permute-done.9.refs_5_), channel_id=1, source_target_pairs={{0,8},{2,10},{8,16},{10,18},{16,24},{18,26},{24,28},{26,30},{28,20... | collective-permute-start | bytes 786440 | tf_op jit(solution)/shard_map/ppermute | solution.py:179
  21.5 14.1 %collective-permute-start.12 = (f32[512,128]{1,0:T(8,128)S(1)}, f32[512,128]{1,0:T(8,128)S(1)}, u32[]{:S(2)}, u32[]{:S(2)}) collective-permute-start(f32[512,128]{1,0:T(8,128)S(1)} %collective-permute-done.11.refs_7_), channel_id=1, source_target_pairs={{0,4},{2,6},{8,0},{10,2},{16,8},{18,10},{24,16},{26,18},{28,24},{3... | collective-permute-start | bytes 786440 | tf_op jit(solution)/shard_map/ppermute | solution.py:179
  22.1 10.1 %collective-permute-start.4 = (f32[512,128]{1,0:T(8,128)S(1)}, f32[512,128]{1,0:T(8,128)S(1)}, u32[]{:S(2)}, u32[]{:S(2)}) collective-permute-start(f32[512,128]{1,0:T(8,128)S(1)} %collective-permute-done.3.refs_4_), channel_id=1, source_target_pairs={{0,8},{2,10},{8,16},{10,18},{16,24},{18,26},{24,28},{26,30},{28,20... | collective-permute-start | bytes 786440 | tf_op jit(solution)/shard_map/ppermute | solution.py:179
  23.6 10.1 %collective-permute-start.7 = (f32[512,128]{1,0:T(8,128)S(1)}, f32[512,128]{1,0:T(8,128)S(1)}, u32[]{:S(2)}, u32[]{:S(2)}) collective-permute-start(f32[512,128]{1,0:T(8,128)S(1)} %collective-permute-done.6.refs_6_), channel_id=1, source_target_pairs={{0,4},{2,6},{8,0},{10,2},{16,8},{18,10},{24,16},{26,18},{28,24},{3... | collective-permute-start | bytes 786440 | tf_op jit(solution)/shard_map/ppermute | solution.py:179
  32.2 7.9 %collective-permute-start.5 = (f32[512,128]{1,0:T(8,128)S(1)}, f32[512,128]{1,0:T(8,128)S(1)}, u32[]{:S(2)}, u32[]{:S(2)}) collective-permute-start(f32[512,128]{1,0:T(8,128)S(1)} %collective-permute-done.4.refs_4_), channel_id=1, source_target_pairs={{0,8},{2,10},{8,16},{10,18},{16,24},{18,26},{24,28},{26,30},{28,20... | collective-permute-start | bytes 786440 | tf_op jit(solution)/shard_map/ppermute | solution.py:179
  33.6 7.3 %collective-permute-start.8 = (f32[512,128]{1,0:T(8,128)S(1)}, f32[512,128]{1,0:T(8,128)S(1)}, u32[]{:S(2)}, u32[]{:S(2)}) collective-permute-start(f32[512,128]{1,0:T(8,128)S(1)} %collective-permute-done.7.refs_6_), channel_id=1, source_target_pairs={{0,4},{2,6},{8,0},{10,2},{16,8},{18,10},{24,16},{26,18},{28,24},{3... | collective-permute-start | bytes 786440 | tf_op jit(solution)/shard_map/ppermute | solution.py:179
  34.2 9.7 %collective-permute-start.15 = (f32[512,128]{1,0:T(8,128)S(1)}, f32[512,128]{1,0:T(8,128)S(1)}, u32[]{:S(2)}, u32[]{:S(2)}) collective-permute-start(f32[512,128]{1,0:T(8,128)S(1)} %collective-permute-done.10.refs_5_), channel_id=1, source_target_pairs={{0,8},{2,10},{8,16},{10,18},{16,24},{18,26},{24,28},{26,30},{28,20... | collective-permute-start | bytes 786440 | tf_op jit(solution)/shard_map/ppermute | solution.py:179
  35.7 8.6 %collective-permute-start.16 = (f32[512,128]{1,0:T(8,128)S(1)}, f32[512,128]{1,0:T(8,128)S(1)}, u32[]{:S(2)}, u32[]{:S(2)}) collective-permute-start(f32[512,128]{1,0:T(8,128)S(1)} %collective-permute-done.12.refs_7_), channel_id=1, source_target_pairs={{0,4},{2,6},{8,0},{10,2},{16,8},{18,10},{24,16},{26,18},{28,24},{3... | collective-permute-start | bytes 786440 | tf_op jit(solution)/shard_map/ppermute | solution.py:179
  44.3 10.9 %collective-permute-start.13 = (f32[256,128]{1,0:T(8,128)S(1)}, f32[256,128]{1,0:T(8,128)S(1)}, u32[]{:S(2)}, u32[]{:S(2)}) collective-permute-start(f32[256,128]{1,0:T(8,128)S(1)} %slice.102), channel_id=1, source_target_pairs={{0,8},{2,10},{8,16},{10,18},{16,24},{18,26},{24,28},{26,30},{28,20... | collective-permute-start | bytes 393224 | tf_op jit(solution)/shard_map/ppermute | solution.py:179
  45.9 9.3 %collective-permute-start.14 = (f32[256,128]{1,0:T(8,128)S(1)}, f32[256,128]{1,0:T(8,128)S(1)}, u32[]{:S(2)}, u32[]{:S(2)}) collective-permute-start(f32[256,128]{1,0:T(8,128)S(1)} %slice.103), channel_id=1, source_target_pairs={{0,4},{2,6},{8,0},{10,2},{16,8},{18,10},{24,16},{26,18},{28,24},{3... | collective-permute-start | bytes 393224 | tf_op jit(solution)/shard_map/ppermute | solution.py:179
  46.5 5.1 %collective-permute-start.19 = (f32[256,128]{1,0:T(8,128)S(1)}, f32[256,128]{1,0:T(8,128)S(1)}, u32[]{:S(2)}, u32[]{:S(2)}) collective-permute-start(f32[256,128]{1,0:T(8,128)S(1)} %slice.109), channel_id=1, source_target_pairs={{0,8},{2,10},{8,16},{10,18},{16,24},{18,26},{24,28},{26,30},{28,20... | collective-permute-start | bytes 393224 | tf_op jit(solution)/shard_map/ppermute | solution.py:179
  48.1 5.1 %collective-permute-start.20 = (f32[256,128]{1,0:T(8,128)S(1)}, f32[256,128]{1,0:T(8,128)S(1)}, u32[]{:S(2)}, u32[]{:S(2)}) collective-permute-start(f32[256,128]{1,0:T(8,128)S(1)} %slice.110), channel_id=1, source_target_pairs={{0,4},{2,6},{8,0},{10,2},{16,8},{18,10},{24,16},{26,18},{28,24},{3... | collective-permute-start | bytes 393224 | tf_op jit(solution)/shard_map/ppermute | solution.py:179
  55.1 2.6 %collective-permute-start.21 = (f32[1024,128]{1,0:T(8,128)S(1)}, f32[1024,128]{1,0:T(8,128)S(1)}, u32[]{:S(2)}, u32[]{:S(2)}) collective-permute-start(f32[1024,128]{1,0:T(8,128)S(1)} %get-tuple-element.44), channel_id=1, source_target_pairs={{0,2},{2,0},{4,6},{6,4},{8,10},{10,8},{12,14},{14,12},{16,18},{18,... | collective-permute-start | bytes 1572872 | tf_op jit(solution)/shard_map/ppermute | solution.py:182
  57.2 2.2 %collective-permute-start.17 = (f32[1024,128]{1,0:T(8,128)S(1)}, f32[1024,128]{1,0:T(8,128)S(1)}, u32[]{:S(2)}, u32[]{:S(2)}) collective-permute-start(f32[1024,128]{1,0:T(8,128)S(1)} %get-tuple-element.41), channel_id=1, source_target_pairs={{0,2},{2,0},{4,6},{6,4},{8,10},{10,8},{12,14},{14,12},{16,18},{18,... | collective-permute-start | bytes 1572872 | tf_op jit(solution)/shard_map/ppermute | solution.py:182
  57.8 3.2 %copy-start.1 = (f32[512,256]{1,0:T(8,128)S(1)}, f32[512,256]{1,0:T(8,128)}, u32[]{:S(2)}) copy-start(f32[512,256]{1,0:T(8,128)} %param.11) | copy-start | bytes 1572868
  57.8 9.2 %collective-permute-start.22 = (f32[512,128]{1,0:T(8,128)S(1)}, f32[512,128]{1,0:T(8,128)S(1)}, u32[]{:S(2)}, u32[]{:S(2)}) collective-permute-start(f32[512,128]{1,0:T(8,128)S(1)} %slice_add_fusion), channel_id=1, source_target_pairs={{0,1},{1,0},{2,3},{3,2},{4,5},{5,4},{6,7},{7,6},{8,9},{9,8},{10,11... | collective-permute-start | bytes 786440 | tf_op jit(solution)/shard_map/ppermute | solution.py:185
  59.4 1.6 %copy-start.8 = (f32[256]{0:T(256)S(1)}, f32[256]{0:T(256)}, u32[]{:S(2)}) copy-start(f32[256]{0:T(256)} %param.15) | copy-start | bytes 3076
  59.4 7.6 %copy-start.2 = (f32[256,256]{1,0:T(8,128)S(1)}, f32[256,256]{1,0:T(8,128)}, u32[]{:S(2)}) copy-start(f32[256,256]{1,0:T(8,128)} %param.14) | copy-start | bytes 786436
  59.4 12.3 %collective-permute-start.18 = (f32[512,128]{1,0:T(8,128)S(1)}, f32[512,128]{1,0:T(8,128)S(1)}, u32[]{:S(2)}, u32[]{:S(2)}) collective-permute-start(f32[512,128]{1,0:T(8,128)S(1)} %slice_add_fusion.2), channel_id=1, source_target_pairs={{0,1},{1,0},{2,3},{3,2},{4,5},{5,4},{6,7},{7,6},{8,9},{9,8},{10,11... | collective-permute-start | bytes 786440 | tf_op jit(solution)/shard_map/ppermute | solution.py:185
  (1 other events, 0.7 us)

commit v3 on v2

--- a/solution.py
+++ b/solution.py
@@ -197,21 +197,17 @@
         head = jnp.pad(head, ((0, 0), (0, 7), (0, 0)))
         return jnp.concatenate(lists + [head], axis=1)
 
-    own_lists, others_lists = bundle(0), bundle(1)
+    lists = jnp.concatenate([bundle(0), core_swap(bundle(1))], axis=0)
     if groups == 2:
-        own_far = rep_swap(own_lists)
-        sibling_lists = core_swap(others_lists)
-        edges = jnp.concatenate([own_lists, own_far, sibling_lists, rep_swap(sibling_lists)], axis=0)
+        edges = jnp.concatenate([lists, rep_swap(lists)], axis=0)
     else:
-        lists = jnp.concatenate([own_lists, core_swap(others_lists)], axis=1)
-        lists = lax.all_gather(lists, "rep", axis=0, tiled=True)
-        edges = jnp.concatenate([lists[:, : own_lists.shape[1]], lists[:, own_lists.shape[1] :]], axis=0)
+        edges = lax.all_gather(lists, "rep", axis=0, tiled=True)
     meta = edges[:, 3 * slots, :TILE]
 
     def list_place(offset, which):
         group = offset // per
         group = group ^ replica if groups == 2 else group
-        return (which * groups + group) * per + offset % per
+        return (2 * group + which) * per + offset % per
 
     position = jnp.where(chip % 2 == 0, chip // 2, lanes - 1 - chip // 2)
 
@@ -235,14 +231,20 @@
     half = shard // 2
     up, down = own, own
     totals = add(pairs_of([0]), place, meta, edges, [[[v] for v in own]], None)
-    for step in range(1, lanes // 2):
+    for step in range(1, lanes // 2 - 1):
         up, down = [ring(v, 1) for v in up], [ring(v, -1) for v in down]
-        if step == lanes // 2 - 1:
-            for f in range(chunks):
-                up[f], down[f], totals = lax.optimization_barrier((up[f], down[f], totals))
         parts = [[[v] for v in up], [[v] for v in down]]
         totals = add(pairs_of([-step, step]), place, meta, edges, parts, totals)
-    ends = [[ring(up[f][:half], 1), ring(down[f][half:], -1)] for f in range(chunks)]
+    step = lanes // 2 - 1
+    pairs = pairs_of([-step, step])
+    up, down = [ring(v, 1) for v in up], [ring(v, -1) for v in down]
+    totals = list(totals)
+    ends = []
+    for f in range(chunks):
+        up[f], down[f], totals = lax.optimization_barrier((up[f], down[f], list(totals)))
+        totals = list(totals)
+        ends.append([ring(up[f][:half], 1), ring(down[f][half:], -1)])
+        totals[f : f + 1] = add(pairs, place, meta, edges, [[[up[f]]], [[down[f]]]], totals[f : f + 1])
     pairs = pairs_of([lanes // 2])
     hidden = root
     for f in range(chunks):

time: 73.7 us -> 78.3 us (1.062)
  Pallas kernels: 14.9 us -> 19.3 us
  starting transfers between devices: 26.1 us -> 23.7 us
  other arithmetic: 2.67 us -> 4.49 us
    pallas_call x6 -> x7, Pallas kernels: 14.9 us -> 19.3 us  [add_sources(): pl.pallas_call(functools.partial(sum_kernel, sources, chunks, pieces, slo...]
    ppermute x4 -> x3, waiting for transfers between devices: 12.5 us -> 9.35 us  [rep_swap(): return lax.ppermute(value, 'rep', [(0, 1), (1, 0)])]
    ppermute x16, waiting for transfers between devices: 12.5 us -> 15.5 us  [ring(): return lax.ppermute(value, 'blk', pairs)]
    concatenate x1 -> x2, other arithmetic: 0.07 us -> 1.89 us  [the longest x1 1.09 us: on_device(): edges = jnp.concatenate([lists, rep_swap(lists)], axis=0)]
    ppermute x4 -> x3, starting transfers between devices: 6.7 us -> 5.24 us  [rep_swap(): return lax.ppermute(value, 'rep', [(0, 1), (1, 0)])]
    ppermute x16, starting transfers between devices: 18.7 us -> 17.8 us  [ring(): return lax.ppermute(value, 'blk', pairs)]
  transfers between devices with their start and end apart: 23 -> 22, of which waited for: 10 -> 8; matrix products, arithmetic and copies ran while one was open for 3% -> 6% of each run, Pallas kernels for 20% -> 25%
where the time goes in v3:
time: 78.3 us; the launch traced here: 77.9 us
  waiting for transfers between devices  25.3 us (32%)
  starting transfers between devices  23.7 us (30%)
  Pallas kernels  19.3 us (25%)
  other arithmetic  4.49 us (6%)
  matrix products  2.61 us (3%)
  between operations  1.33 us (2%)
  local copies, waits for them, and re-layouts  1.21 us (2%)
    pallas_call x7, Pallas kernels, add_sources(): pl.pallas_call(functools.partial(sum_kernel, sources, chunks, pieces, slo...  19.3 us
    ppermute x16, starting transfers between devices, ring(): return lax.ppermute(value, 'blk', pairs)  17.8 us
    ppermute x16, waiting for transfers between devices, ring(): return lax.ppermute(value, 'blk', pairs)  15.5 us
    ppermute x3, waiting for transfers between devices, rep_swap(): return lax.ppermute(value, 'rep', [(0, 1), (1, 0)])  9.35 us
    ppermute x3, starting transfers between devices, rep_swap(): return lax.ppermute(value, 'rep', [(0, 1), (1, 0)])  5.24 us
    dot_general x2, matrix products, on_device(): jnp.dot(mixed, neighbor_weight[f * TILE:(f + 1) * TILE], precision=highest)  2.03 us
  transfers between devices with their start and end apart: 22, of which 8 were waited for; matrix products, arithmetic and copies ran while one was open for 6% of the time, Pallas kernels for 25%

profile of v3, /device:TPU:0, one launch (start us, length us, event | category | flops | bytes accessed | tf_op | source)
XLA Modules:
  0.0 77.9 jit_solution(16707259870053162496)
XLA Ops:
  0.0 0.7 convert_rsqrt_fusion
  0.7 1.2 %broadcast_multiply_fusion = f32[512,256]{1,0:T(8,128)S(1)} fusion(f32[512,256]{1,0:T(8,128)} %param.11, f32[512]{0:T(512)S(1)} %convert_rsqrt_fusion), kind=kLoop, calls=%fused_computation.17 | loop fusion | flops 131072 | bytes 1050624 | tf_op jit(solution)/shard_map/mul | solution.py:188
  2.0 3.1 %collective-permute-start.2 = (f32[512,128]{1,0:T(8,128)S(1)}, f32[512,128]{1,0:T(8,128)S(1)}, u32[]{:S(2)}, u32[]{:S(2)}) collective-permute-start(f32[512,128]{1,0:T(8,128)S(1)} %get-tuple-element.41.refs_4_), channel_id=1, source_target_pairs={{0,8},{2,10},{8,16},{10,18},{16,24},{18,26},{24,28},{26,30},{28,20... | collective-permute-start | bytes 786440 | tf_op jit(solution)/shard_map/ppermute | solution.py:179
  5.1 1.9 %collective-permute-start.10 = (f32[512,128]{1,0:T(8,128)S(1)}, f32[512,128]{1,0:T(8,128)S(1)}, u32[]{:S(2)}, u32[]{:S(2)}) collective-permute-start(f32[512,128]{1,0:T(8,128)S(1)} %get-tuple-element.42.refs_5_), channel_id=1, source_target_pairs={{0,4},{2,6},{8,0},{10,2},{16,8},{18,10},{24,16},{26,18},{28,24},{3... | collective-permute-start | bytes 786440 | tf_op jit(solution)/shard_map/ppermute | solution.py:179
  9.7 0.8 %pad_add_fusion.1 = s32[8,56,256]{2,1,0:T(8,128)} fusion(s32[4,56,256]{2,1,0:T(8,128)S(1)} %collective-permute-done, s32[4,8,256]{2,1,0:T(8,128)S(1)} %pad.15, s32[4,16,256]{2,1,0:T(8,128)S(1)} %get-tuple-element.47, s32[4,16,256]{2,1,0:T(8,128)S(1)} %get-tuple-element.50, s32[4,16,256]{2,1,0:T(8,128)S(1)} %get-tuple-element.43), kind=kLoop, calls=%fused_computation.5 | loop fusion | flops 458752 | bytes 917504 | tf_op jit(solution)/shard_map/concatenate | solution.py:200
  10.5 1.9 %collective-permute-start.1 = (s32[8,56,256]{2,1,0:T(8,128)}, s32[8,56,256]{2,1,0:T(8,128)}, u32[]{:S(2)}, u32[]{:S(2)}) collective-permute-start(s32[8,56,256]{2,1,0:T(8,128)} %pad_add_fusion.1), channel_id=1, source_target_pairs={{0,1},{1,0},{2,3},{3,2},{4,5},{5,4},{6,7},{7,6},{8,9},{9,8},{10,11... | collective-permute-start | bytes 1376264 | tf_op jit(solution)/shard_map/ppermute | solution.py:185
  12.5 5.9 %collective-permute-done.10.refs_7_ = f32[512,128]{1,0:T(8,128)S(1)} collective-permute-done((f32[512,128]{1,0:T(8,128)S(1)}, f32[512,128]{1,0:T(8,128)S(1)}, u32[]{:S(2)}, u32[]{:S(2)}) %collective-permute-start.10) | collective-permute-done | bytes 262176 | tf_op jit(solution)/shard_map/ppermute | solution.py:179
  18.7 1.7 %collective-permute-start.3 = (f32[512,128]{1,0:T(8,128)S(1)}, f32[512,128]{1,0:T(8,128)S(1)}, u32[]{:S(2)}, u32[]{:S(2)}) collective-permute-start(f32[512,128]{1,0:T(8,128)S(1)} %collective-permute-done.2.refs_4_), channel_id=1, source_target_pairs={{0,8},{2,10},{8,16},{10,18},{16,24},{18,26},{24,28},{26,30},{28,20... | collective-permute-start | bytes 786440 | tf_op jit(solution)/shard_map/ppermute | solution.py:179
  20.8 1.7 %collective-permute-start.9 = (f32[512,128]{1,0:T(8,128)S(1)}, f32[512,128]{1,0:T(8,128)S(1)}, u32[]{:S(2)}, u32[]{:S(2)}) collective-permute-start(f32[512,128]{1,0:T(8,128)S(1)} %collective-permute-done.8.refs_5_), channel_id=1, source_target_pairs={{0,8},{2,10},{8,16},{10,18},{16,24},{18,26},{24,28},{26,30},{28,20... | collective-permute-start | bytes 786440 | tf_op jit(solution)/shard_map/ppermute | solution.py:179
  23.2 4.8 %collective-permute-done.3.refs_4_ = f32[512,128]{1,0:T(8,128)S(1)} collective-permute-done((f32[512,128]{1,0:T(8,128)S(1)}, f32[512,128]{1,0:T(8,128)S(1)}, u32[]{:S(2)}, u32[]{:S(2)}) %collective-permute-start.3) | collective-permute-done | bytes 262176 | tf_op jit(solution)/shard_map/ppermute | solution.py:179
  28.0 1.7 %collective-permute-start.4 = (f32[512,128]{1,0:T(8,128)S(1)}, f32[512,128]{1,0:T(8,128)S(1)}, u32[]{:S(2)}, u32[]{:S(2)}) collective-permute-start(f32[512,128]{1,0:T(8,128)S(1)} %collective-permute-done.3.refs_4_), channel_id=1, source_target_pairs={{0,8},{2,10},{8,16},{10,18},{16,24},{18,26},{24,28},{26,30},{28,20... | collective-permute-start | bytes 786440 | tf_op jit(solution)/shard_map/ppermute | solution.py:179
  29.7 1.3 %collective-permute-done.6.refs_6_ = f32[512,128]{1,0:T(8,128)S(1)} collective-permute-done((f32[512,128]{1,0:T(8,128)S(1)}, f32[512,128]{1,0:T(8,128)S(1)}, u32[]{:S(2)}, u32[]{:S(2)}) %collective-permute-start.6) | collective-permute-done | bytes 262176 | tf_op jit(solution)/shard_map/ppermute | solution.py:179
  31.0 0.6 collective-permute-start.7
  31.6 2.0 %collective-permute-done.9.refs_5_ = f32[512,128]{1,0:T(8,128)S(1)} collective-permute-done((f32[512,128]{1,0:T(8,128)S(1)}, f32[512,128]{1,0:T(8,128)S(1)}, u32[]{:S(2)}, u32[]{:S(2)}) %collective-permute-start.9) | collective-permute-done | bytes 262176 | tf_op jit(solution)/shard_map/ppermute | solution.py:179
  33.6 1.7 %collective-permute-start.14 = (f32[512,128]{1,0:T(8,128)S(1)}, f32[512,128]{1,0:T(8,128)S(1)}, u32[]{:S(2)}, u32[]{:S(2)}) collective-permute-start(f32[512,128]{1,0:T(8,128)S(1)} %collective-permute-done.9.refs_5_), channel_id=1, source_target_pairs={{0,8},{2,10},{8,16},{10,18},{16,24},{18,26},{24,28},{26,30},{28,20... | collective-permute-start | bytes 786440 | tf_op jit(solution)/shard_map/ppermute | solution.py:179
  35.6 1.1 %pad_add_fusion.refs_3_ = s32[16,56,256]{2,1,0:T(8,128)S(1)} fusion(s32[8,56,256]{2,1,0:T(8,128)} %collective-permute-done.1, s32[4,56,256]{2,1,0:T(8,128)S(1)} %collective-permute-done, s32[4,8,256]{2,1,0:T(8,128)S(1)} %pad.15, s32[4,16,256]{2,1,0:T(8,128)S(1)} %get-tuple-element.47, s32[4,16,256]{2,1,0:T(8,128)S(1)} %get-tuple-element.50, ...), kind=kLoop, calls=%fused_computation.4 | loop fusion | flops 1146880 | bytes 1835008 | tf_op jit(solution)/shard_map/concatenate | solution.py:202
  36.7 1.6 %shard_map.109 = (f32[2,1024,128]{2,1,0:T(8,128)S(1)}, f32[2,1024,128]{2,1,0:T(8,128)S(1)}) custom-call(s32[2]{0:T(128)S(1)} %pad_add_fusion.9.refs_0_, s32[2]{0:T(128)S(1)} %pad_add_fusion.6.refs_1_, s32[16,128]{1,0:T(8,128)S(1)} %bitcast.39, s32[16,56,256]{2,1,0:T(8,128)S(1)} %pad_add_fusion.refs_3_, f32[512,128]{1,0:T(8,128)S(1)} %get-tuple-element.41.refs_4_, ...), custom_call_target="tpu_custom_call" | custom-call | flops 3000000000 | bytes 1048576 | tf_op jit(solution)/shard_map/pallas_call | solution.py:135
  38.3 4.2 %shard_map.110 = (f32[2,1024,128]{2,1,0:T(8,128)S(1)}, f32[2,1024,128]{2,1,0:T(8,128)S(1)}) custom-call(s32[4]{0:T(128)S(1)} %pad_add_fusion.8.refs_0_, s32[2]{0:T(128)S(1)} %pad_add_fusion.6.refs_1_, s32[16,128]{1,0:T(8,128)S(1)} %bitcast.40, s32[16,56,256]{2,1,0:T(8,128)S(1)} %pad_add_fusion.refs_3_, ...), custom_call_target="tpu_custom_call", output_to_operand_aliasing={{0}: (8, {}), {1}: (9, {})} | custom-call | flops 5000000000 | bytes 1048576 | tf_op jit(solution)/shard_map/pallas_call | solution.py:135
  42.5 3.6 %shard_map.111 = (f32[2,1024,128]{2,1,0:T(8,128)S(1)}, f32[2,1024,128]{2,1,0:T(8,128)S(1)}) custom-call(s32[4]{0:T(128)S(1)} %pad_add_fusion.7.refs_0_, s32[2]{0:T(128)S(1)} %pad_add_fusion.6.refs_1_, s32[16,128]{1,0:T(8,128)S(1)} %bitcast.41, s32[16,56,256]{2,1,0:T(8,128)S(1)} %pad_add_fusion.refs_3_, ...), custom_call_target="tpu_custom_call", output_to_operand_aliasing={{0}: (8, {}), {1}: (9, {})} | custom-call | flops 5000000000 | bytes 1048576 | tf_op jit(solution)/shard_map/pallas_call | solution.py:135
  46.2 3.0 %shard_map.112.refs_6_ = f32[2,1024,128]{2,1,0:T(8,128)S(1)} custom-call(s32[4]{0:T(128)S(1)} %pad_add_fusion.10.refs_0_, s32[2]{0:T(128)S(1)} %pad_add_fusion.6.refs_1_, s32[16,128]{1,0:T(8,128)S(1)} %bitcast.42, s32[16,56,256]{2,1,0:T(8,128)S(1)} %pad_add_fusion.refs_3_, ...), custom_call_target="tpu_custom_call", output_to_operand_aliasing={{}: (6, {})} | custom-call | flops 3000000000 | bytes 1048576 | tf_op jit(solution)/shard_map/pallas_call | solution.py:135
  49.2 1.7 %collective-permute-start.12 = (f32[256,128]{1,0:T(8,128)S(1)}, f32[256,128]{1,0:T(8,128)S(1)}, u32[]{:S(2)}, u32[]{:S(2)}) collective-permute-start(f32[256,128]{1,0:T(8,128)S(1)} %slice.102), channel_id=1, source_target_pairs={{0,8},{2,10},{8,16},{10,18},{16,24},{18,26},{24,28},{26,30},{28,20... | collective-permute-start | bytes 393224 | tf_op jit(solution)/shard_map/ppermute | solution.py:179
  51.3 1.7 %collective-permute-start.18 = (f32[256,128]{1,0:T(8,128)S(1)}, f32[256,128]{1,0:T(8,128)S(1)}, u32[]{:S(2)}, u32[]{:S(2)}) collective-permute-start(f32[256,128]{1,0:T(8,128)S(1)} %slice.109), channel_id=1, source_target_pairs={{0,8},{2,10},{8,16},{10,18},{16,24},{18,26},{24,28},{26,30},{28,20... | collective-permute-start | bytes 393224 | tf_op jit(solution)/shard_map/ppermute | solution.py:179
  53.4 3.0 %shard_map.114.refs_6_ = f32[2,1024,128]{2,1,0:T(8,128)S(1)} custom-call(s32[4]{0:T(128)S(1)} %pad_add_fusion.10.refs_0_, s32[2]{0:T(128)S(1)} %pad_add_fusion.6.refs_1_, s32[16,128]{1,0:T(8,128)S(1)} %bitcast.43, s32[16,56,256]{2,1,0:T(8,128)S(1)} %pad_add_fusion.refs_3_, ...), custom_call_target="tpu_custom_call", output_to_operand_aliasing={{}: (6, {})} | custom-call | flops 3000000000 | bytes 1048576 | tf_op jit(solution)/shard_map/pallas_call | solution.py:135
  56.5 1.5 %collective-permute-done.19.refs_5_ = f32[256,128]{1,0:T(8,128)S(1)} collective-permute-done((f32[256,128]{1,0:T(8,128)S(1)}, f32[256,128]{1,0:T(8,128)S(1)}, u32[]{:S(2)}, u32[]{:S(2)}) %collective-permute-start.19) | collective-permute-done | bytes 131104 | tf_op jit(solution)/shard_map/ppermute | solution.py:179
  58.0 1.9 %shard_map.115 = (f32[1024,128]{1,0:T(8,128)S(1)}, f32[1024,128]{1,0:T(8,128)S(1)}) custom-call(s32[2]{0:T(128)S(1)} %pad_add_fusion.5.refs_0_, s32[2]{0:T(128)S(1)} %pad_add_fusion.6.refs_1_, s32[16,128]{1,0:T(8,128)S(1)} %bitcast.44, s32[16,56,256]{2,1,0:T(8,128)S(1)} %pad_add_fusion.refs_3_, f32[256,128]{1,0:T(8,128)S(1)} %collective-permute-done.18.refs_4_, ...), custom_call_target="tpu_custom_call" | custom-call | flops 2000000000 | bytes 1048576 | tf_op jit(solution)/shard_map/pallas_call | solution.py:135
  60.0 1.9 %shard_map.113 = (f32[1024,128]{1,0:T(8,128)S(1)}, f32[1024,128]{1,0:T(8,128)S(1)}) custom-call(s32[2]{0:T(128)S(1)} %pad_add_fusion.5.refs_0_, s32[2]{0:T(128)S(1)} %pad_add_fusion.6.refs_1_, s32[16,128]{1,0:T(8,128)S(1)} %bitcast.45, s32[16,56,256]{2,1,0:T(8,128)S(1)} %pad_add_fusion.refs_3_, f32[256,128]{1,0:T(8,128)S(1)} %collective-permute-done.12.refs_4_, ...), custom_call_target="tpu_custom_call" | custom-call | flops 2000000000 | bytes 1048576 | tf_op jit(solution)/shard_map/pallas_call | solution.py:135
  62.6 1.8 %collective-permute-start.21 = (f32[512,128]{1,0:T(8,128)S(1)}, f32[512,128]{1,0:T(8,128)S(1)}, u32[]{:S(2)}, u32[]{:S(2)}) collective-permute-start(f32[512,128]{1,0:T(8,128)S(1)} %slice_add_fusion), channel_id=1, source_target_pairs={{0,1},{1,0},{2,3},{3,2},{4,5},{5,4},{6,7},{7,6},{8,9},{9,8},{10,11... | collective-permute-start | bytes 786440 | tf_op jit(solution)/shard_map/ppermute | solution.py:185
  64.5 1.5 %collective-permute-start.17 = (f32[512,128]{1,0:T(8,128)S(1)}, f32[512,128]{1,0:T(8,128)S(1)}, u32[]{:S(2)}, u32[]{:S(2)}) collective-permute-start(f32[512,128]{1,0:T(8,128)S(1)} %slice_add_fusion.2), channel_id=1, source_target_pairs={{0,1},{1,0},{2,3},{3,2},{4,5},{5,4},{6,7},{7,6},{8,9},{9,8},{10,11... | collective-permute-start | bytes 786440 | tf_op jit(solution)/shard_map/ppermute | solution.py:185
  66.5 5.2 %collective-permute-done.21 = f32[512,128]{1,0:T(8,128)S(1)} collective-permute-done((f32[512,128]{1,0:T(8,128)S(1)}, f32[512,128]{1,0:T(8,128)S(1)}, u32[]{:S(2)}, u32[]{:S(2)}) %collective-permute-start.21) | collective-permute-done | bytes 262176 | tf_op jit(solution)/shard_map/ppermute | solution.py:185
  71.8 0.6 fusion.4
  72.4 4.1 %collective-permute-done.17 = f32[512,128]{1,0:T(8,128)S(1)} collective-permute-done((f32[512,128]{1,0:T(8,128)S(1)}, f32[512,128]{1,0:T(8,128)S(1)}, u32[]{:S(2)}, u32[]{:S(2)}) %collective-permute-start.17) | collective-permute-done | bytes 262176 | tf_op jit(solution)/shard_map/ppermute | solution.py:185
  76.5 1.4 %fusion.1 = f32[512,256]{1,0:T(8,128)} fusion(f32[512,256]{1,0:T(8,128)S(1)} %fusion.4, f32[512,256]{1,0:T(8,128)S(1)} %convolution_add_fusion.1, f32[512,128]{1,0:T(8,128)S(1)} %collective-permute-done.17, f32[1024,128]{1,0:T(8,128)S(1)} %collective-permute-done.16, f32[1024,128]{1,0:T(8,128)S(1)} %get-tuple-element.34, f32[256,256]{1,0:T(8,128)S(1)} %copy-done.2, ...), kind=kOutput, calls=%fused_computation.2 | convolution fusion | flops 201916416 | bytes 2492416 | tf_op jit(solution)/shard_map/dot_general | solution.py:259
  (78 shorter events, 5.5 us)
Async XLA Ops:
  0.0 66.0 %copy-start = (f32[256,256]{1,0:T(8,128)S(1)}, f32[256,256]{1,0:T(8,128)}, u32[]{:S(2)}) copy-start(f32[256,256]{1,0:T(8,128)} %param.13) | copy-start | bytes 786436
  1.9 5.2 %copy-start.3 = (s32[1,8,16,256]{3,2,1,0:T(8,128)S(1)}, s32[1,8,16,256]{3,2,1,0:T(8,128)}, u32[]{:S(2)}) copy-start(s32[1,8,16,256]{3,2,1,0:T(8,128)} %param.19) | copy-start | bytes 393220
  2.0 16.7 %collective-permute-start.2 = (f32[512,128]{1,0:T(8,128)S(1)}, f32[512,128]{1,0:T(8,128)S(1)}, u32[]{:S(2)}, u32[]{:S(2)}) collective-permute-start(f32[512,128]{1,0:T(8,128)S(1)} %get-tuple-element.41.refs_4_), channel_id=1, source_target_pairs={{0,8},{2,10},{8,16},{10,18},{16,24},{18,26},{24,28},{26,30},{28,20... | collective-permute-start | bytes 786440 | tf_op jit(solution)/shard_map/ppermute | solution.py:179
  5.0 15.4 %collective-permute-start.5 = (f32[512,128]{1,0:T(8,128)S(1)}, f32[512,128]{1,0:T(8,128)S(1)}, u32[]{:S(2)}, u32[]{:S(2)}) collective-permute-start(f32[512,128]{1,0:T(8,128)S(1)} %get-tuple-element.41.refs_4_), channel_id=1, source_target_pairs={{0,4},{2,6},{8,0},{10,2},{16,8},{18,10},{24,16},{26,18},{28,24},{3... | collective-permute-start | bytes 786440 | tf_op jit(solution)/shard_map/ppermute | solution.py:179
  5.0 2.1 %copy-start.9 = (s32[1,8]{1,0:T(1,128)S(1)}, s32[1,8]{1,0:T(1,128)}, u32[]{:S(2)}) copy-start(s32[1,8]{1,0:T(1,128)} %param.18) | copy-start | bytes 100
  5.1 3.0 %copy-start.4 = (s32[1,8,16,256]{3,2,1,0:T(8,128)S(1)}, s32[1,8,16,256]{3,2,1,0:T(8,128)}, u32[]{:S(2)}) copy-start(s32[1,8,16,256]{3,2,1,0:T(8,128)} %param.21) | copy-start | bytes 393220
  5.1 3.0 %copy-start.5 = (s32[1,8,16,256]{3,2,1,0:T(8,128)S(1)}, s32[1,8,16,256]{3,2,1,0:T(8,128)}, u32[]{:S(2)}) copy-start(s32[1,8,16,256]{3,2,1,0:T(8,128)} %param.20) | copy-start | bytes 393220
  5.1 13.4 %collective-permute-start.10 = (f32[512,128]{1,0:T(8,128)S(1)}, f32[512,128]{1,0:T(8,128)S(1)}, u32[]{:S(2)}, u32[]{:S(2)}) collective-permute-start(f32[512,128]{1,0:T(8,128)S(1)} %get-tuple-element.42.refs_5_), channel_id=1, source_target_pairs={{0,4},{2,6},{8,0},{10,2},{16,8},{18,10},{24,16},{26,18},{28,24},{3... | collective-permute-start | bytes 786440 | tf_op jit(solution)/shard_map/ppermute | solution.py:179
  7.0 13.8 %collective-permute-start.8 = (f32[512,128]{1,0:T(8,128)S(1)}, f32[512,128]{1,0:T(8,128)S(1)}, u32[]{:S(2)}, u32[]{:S(2)}) collective-permute-start(f32[512,128]{1,0:T(8,128)S(1)} %get-tuple-element.42.refs_5_), channel_id=1, source_target_pairs={{0,8},{2,10},{8,16},{10,18},{16,24},{18,26},{24,28},{26,30},{28,20... | collective-permute-start | bytes 786440 | tf_op jit(solution)/shard_map/ppermute | solution.py:179
  7.2 0.7 copy-start.6
  7.3 0.7 copy-start.7
  8.1 1.6 %collective-permute-start = (s32[4,56,256]{2,1,0:T(8,128)S(1)}, s32[4,56,256]{2,1,0:T(8,128)S(1)}, u32[]{:S(2)}, u32[]{:S(2)}) collective-permute-start(s32[4,56,256]{2,1,0:T(8,128)S(1)} %pad_add_fusion.2), channel_id=1, source_target_pairs={{0,2},{2,0},{4,6},{6,4},{8,10},{10,8},{12,14},{14,12},{16,18},{18,... | collective-permute-start | bytes 688136 | tf_op jit(solution)/shard_map/ppermute | solution.py:182
  10.5 25.1 %collective-permute-start.1 = (s32[8,56,256]{2,1,0:T(8,128)}, s32[8,56,256]{2,1,0:T(8,128)}, u32[]{:S(2)}, u32[]{:S(2)}) collective-permute-start(s32[8,56,256]{2,1,0:T(8,128)} %pad_add_fusion.1), channel_id=1, source_target_pairs={{0,1},{1,0},{2,3},{3,2},{4,5},{5,4},{6,7},{7,6},{8,9},{9,8},{10,11... | collective-permute-start | bytes 1376264 | tf_op jit(solution)/shard_map/ppermute | solution.py:185
  18.4 16.9 %collective-permute-start.11 = (f32[512,128]{1,0:T(8,128)S(1)}, f32[512,128]{1,0:T(8,128)S(1)}, u32[]{:S(2)}, u32[]{:S(2)}) collective-permute-start(f32[512,128]{1,0:T(8,128)S(1)} %collective-permute-done.10.refs_7_), channel_id=1, source_target_pairs={{0,4},{2,6},{8,0},{10,2},{16,8},{18,10},{24,16},{26,18},{28,24},{3... | collective-permute-start | bytes 786440 | tf_op jit(solution)/shard_map/ppermute | solution.py:179
  18.7 9.2 %collective-permute-start.3 = (f32[512,128]{1,0:T(8,128)S(1)}, f32[512,128]{1,0:T(8,128)S(1)}, u32[]{:S(2)}, u32[]{:S(2)}) collective-permute-start(f32[512,128]{1,0:T(8,128)S(1)} %collective-permute-done.2.refs_4_), channel_id=1, source_target_pairs={{0,8},{2,10},{8,16},{10,18},{16,24},{18,26},{24,28},{26,30},{28,20... | collective-permute-start | bytes 786440 | tf_op jit(solution)/shard_map/ppermute | solution.py:179
  20.5 10.5 %collective-permute-start.6 = (f32[512,128]{1,0:T(8,128)S(1)}, f32[512,128]{1,0:T(8,128)S(1)}, u32[]{:S(2)}, u32[]{:S(2)}) collective-permute-start(f32[512,128]{1,0:T(8,128)S(1)} %collective-permute-done.5.refs_6_), channel_id=1, source_target_pairs={{0,4},{2,6},{8,0},{10,2},{16,8},{18,10},{24,16},{26,18},{28,24},{3... | collective-permute-start | bytes 786440 | tf_op jit(solution)/shard_map/ppermute | solution.py:179
  20.8 12.8 %collective-permute-start.9 = (f32[512,128]{1,0:T(8,128)S(1)}, f32[512,128]{1,0:T(8,128)S(1)}, u32[]{:S(2)}, u32[]{:S(2)}) collective-permute-start(f32[512,128]{1,0:T(8,128)S(1)} %collective-permute-done.8.refs_5_), channel_id=1, source_target_pairs={{0,8},{2,10},{8,16},{10,18},{16,24},{18,26},{24,28},{26,30},{28,20... | collective-permute-start | bytes 786440 | tf_op jit(solution)/shard_map/ppermute | solution.py:179
  28.0 18.1 %collective-permute-start.4 = (f32[512,128]{1,0:T(8,128)S(1)}, f32[512,128]{1,0:T(8,128)S(1)}, u32[]{:S(2)}, u32[]{:S(2)}) collective-permute-start(f32[512,128]{1,0:T(8,128)S(1)} %collective-permute-done.3.refs_4_), channel_id=1, source_target_pairs={{0,8},{2,10},{8,16},{10,18},{16,24},{18,26},{24,28},{26,30},{28,20... | collective-permute-start | bytes 786440 | tf_op jit(solution)/shard_map/ppermute | solution.py:179
  31.0 15.1 %collective-permute-start.7 = (f32[512,128]{1,0:T(8,128)S(1)}, f32[512,128]{1,0:T(8,128)S(1)}, u32[]{:S(2)}, u32[]{:S(2)}) collective-permute-start(f32[512,128]{1,0:T(8,128)S(1)} %collective-permute-done.6.refs_6_), channel_id=1, source_target_pairs={{0,4},{2,6},{8,0},{10,2},{16,8},{18,10},{24,16},{26,18},{28,24},{3... | collective-permute-start | bytes 786440 | tf_op jit(solution)/shard_map/ppermute | solution.py:179
  33.6 15.6 %collective-permute-start.14 = (f32[512,128]{1,0:T(8,128)S(1)}, f32[512,128]{1,0:T(8,128)S(1)}, u32[]{:S(2)}, u32[]{:S(2)}) collective-permute-start(f32[512,128]{1,0:T(8,128)S(1)} %collective-permute-done.9.refs_5_), channel_id=1, source_target_pairs={{0,8},{2,10},{8,16},{10,18},{16,24},{18,26},{24,28},{26,30},{28,20... | collective-permute-start | bytes 786440 | tf_op jit(solution)/shard_map/ppermute | solution.py:179
  35.3 13.9 %collective-permute-start.15 = (f32[512,128]{1,0:T(8,128)S(1)}, f32[512,128]{1,0:T(8,128)S(1)}, u32[]{:S(2)}, u32[]{:S(2)}) collective-permute-start(f32[512,128]{1,0:T(8,128)S(1)} %collective-permute-done.11.refs_7_), channel_id=1, source_target_pairs={{0,4},{2,6},{8,0},{10,2},{16,8},{18,10},{24,16},{26,18},{28,24},{3... | collective-permute-start | bytes 786440 | tf_op jit(solution)/shard_map/ppermute | solution.py:179
  49.2 10.8 %collective-permute-start.12 = (f32[256,128]{1,0:T(8,128)S(1)}, f32[256,128]{1,0:T(8,128)S(1)}, u32[]{:S(2)}, u32[]{:S(2)}) collective-permute-start(f32[256,128]{1,0:T(8,128)S(1)} %slice.102), channel_id=1, source_target_pairs={{0,8},{2,10},{8,16},{10,18},{16,24},{18,26},{24,28},{26,30},{28,20... | collective-permute-start | bytes 393224 | tf_op jit(solution)/shard_map/ppermute | solution.py:179
  50.9 9.2 %collective-permute-start.13 = (f32[256,128]{1,0:T(8,128)S(1)}, f32[256,128]{1,0:T(8,128)S(1)}, u32[]{:S(2)}, u32[]{:S(2)}) collective-permute-start(f32[256,128]{1,0:T(8,128)S(1)} %slice.103), channel_id=1, source_target_pairs={{0,4},{2,6},{8,0},{10,2},{16,8},{18,10},{24,16},{26,18},{28,24},{3... | collective-permute-start | bytes 393224 | tf_op jit(solution)/shard_map/ppermute | solution.py:179
  51.3 5.2 %collective-permute-start.18 = (f32[256,128]{1,0:T(8,128)S(1)}, f32[256,128]{1,0:T(8,128)S(1)}, u32[]{:S(2)}, u32[]{:S(2)}) collective-permute-start(f32[256,128]{1,0:T(8,128)S(1)} %slice.109), channel_id=1, source_target_pairs={{0,8},{2,10},{8,16},{10,18},{16,24},{18,26},{24,28},{26,30},{28,20... | collective-permute-start | bytes 393224 | tf_op jit(solution)/shard_map/ppermute | solution.py:179
  53.0 5.0 %collective-permute-start.19 = (f32[256,128]{1,0:T(8,128)S(1)}, f32[256,128]{1,0:T(8,128)S(1)}, u32[]{:S(2)}, u32[]{:S(2)}) collective-permute-start(f32[256,128]{1,0:T(8,128)S(1)} %slice.110), channel_id=1, source_target_pairs={{0,4},{2,6},{8,0},{10,2},{16,8},{18,10},{24,16},{26,18},{28,24},{3... | collective-permute-start | bytes 393224 | tf_op jit(solution)/shard_map/ppermute | solution.py:179
  59.9 2.6 %collective-permute-start.20 = (f32[1024,128]{1,0:T(8,128)S(1)}, f32[1024,128]{1,0:T(8,128)S(1)}, u32[]{:S(2)}, u32[]{:S(2)}) collective-permute-start(f32[1024,128]{1,0:T(8,128)S(1)} %get-tuple-element.40), channel_id=1, source_target_pairs={{0,2},{2,0},{4,6},{6,4},{8,10},{10,8},{12,14},{14,12},{16,18},{18,... | collective-permute-start | bytes 1572872 | tf_op jit(solution)/shard_map/ppermute | solution.py:182
  62.0 2.4 %collective-permute-start.16 = (f32[1024,128]{1,0:T(8,128)S(1)}, f32[1024,128]{1,0:T(8,128)S(1)}, u32[]{:S(2)}, u32[]{:S(2)}) collective-permute-start(f32[1024,128]{1,0:T(8,128)S(1)} %get-tuple-element.35), channel_id=1, source_target_pairs={{0,2},{2,0},{4,6},{6,4},{8,10},{10,8},{12,14},{14,12},{16,18},{18,... | collective-permute-start | bytes 1572872 | tf_op jit(solution)/shard_map/ppermute | solution.py:182
  62.6 3.4 %copy-start.1 = (f32[512,256]{1,0:T(8,128)S(1)}, f32[512,256]{1,0:T(8,128)}, u32[]{:S(2)}) copy-start(f32[512,256]{1,0:T(8,128)} %param.11) | copy-start | bytes 1572868
  62.6 9.2 %collective-permute-start.21 = (f32[512,128]{1,0:T(8,128)S(1)}, f32[512,128]{1,0:T(8,128)S(1)}, u32[]{:S(2)}, u32[]{:S(2)}) collective-permute-start(f32[512,128]{1,0:T(8,128)S(1)} %slice_add_fusion), channel_id=1, source_target_pairs={{0,1},{1,0},{2,3},{3,2},{4,5},{5,4},{6,7},{7,6},{8,9},{9,8},{10,11... | collective-permute-start | bytes 786440 | tf_op jit(solution)/shard_map/ppermute | solution.py:185
  64.4 1.6 %copy-start.8 = (f32[256]{0:T(256)S(1)}, f32[256]{0:T(256)}, u32[]{:S(2)}) copy-start(f32[256]{0:T(256)} %param.15) | copy-start | bytes 3076
  64.4 7.4 %copy-start.2 = (f32[256,256]{1,0:T(8,128)S(1)}, f32[256,256]{1,0:T(8,128)}, u32[]{:S(2)}) copy-start(f32[256,256]{1,0:T(8,128)} %param.14) | copy-start | bytes 786436
  64.5 12.1 %collective-permute-start.17 = (f32[512,128]{1,0:T(8,128)S(1)}, f32[512,128]{1,0:T(8,128)S(1)}, u32[]{:S(2)}, u32[]{:S(2)}) collective-permute-start(f32[512,128]{1,0:T(8,128)S(1)} %slice_add_fusion.2), channel_id=1, source_target_pairs={{0,1},{1,0},{2,3},{3,2},{4,5},{5,4},{6,7},{7,6},{8,9},{9,8},{10,11... | collective-permute-start | bytes 786440 | tf_op jit(solution)/shard_map/ppermute | solution.py:185

commit v4 on v3

--- a/solution.py
+++ b/solution.py
@@ -229,26 +229,31 @@
     root = jnp.dot(features, root_weight, precision=highest) + bias
 
     half = shard // 2
-    up, down = own, own
-    totals = add(pairs_of([0]), place, meta, edges, [[[v] for v in own]], None)
-    for step in range(1, lanes // 2 - 1):
-        up, down = [ring(v, 1) for v in up], [ring(v, -1) for v in down]
-        parts = [[[v] for v in up], [[v] for v in down]]
-        totals = add(pairs_of([-step, step]), place, meta, edges, parts, totals)
+    half = shard // 2
+    hops = [(own, own)]
+    totals = None
+    for step in range(1, lanes // 2):
+        up, down = hops[-1]
+        if totals is not None:
+            up, down = list(up), list(down)
+            up[-1], down[-1], totals = lax.optimization_barrier((up[-1], down[-1], totals))
+        hops.append(([ring(v, 1) for v in up], [ring(v, -1) for v in down]))
+        if step == 2:
+            totals = add(pairs_of([0]), place, meta, edges, [[[v] for v in own]], None)
+        if step >= 2:
+            parts = [[[v] for v in side] for side in hops[step - 1]]
+            totals = add(pairs_of([1 - step, step - 1]), place, meta, edges, parts, totals)
+    up, down = [list(side) for side in hops[-1]]
+    up[-1], down[-1], totals = lax.optimization_barrier((up[-1], down[-1], totals))
+    ends = [[ring(up[f][:half], 1), ring(down[f][half:], -1)] for f in range(chunks)]
     step = lanes // 2 - 1
-    pairs = pairs_of([-step, step])
-    up, down = [ring(v, 1) for v in up], [ring(v, -1) for v in down]
-    totals = list(totals)
-    ends = []
-    for f in range(chunks):
-        up[f], down[f], totals = lax.optimization_barrier((up[f], down[f], list(totals)))
-        totals = list(totals)
-        ends.append([ring(up[f][:half], 1), ring(down[f][half:], -1)])
-        totals[f : f + 1] = add(pairs, place, meta, edges, [[[up[f]]], [[down[f]]]], totals[f : f + 1])
+    totals = add(pairs_of([-step, step]), place, meta, edges, [[[v] for v in up], [[v] for v in down]], totals)
     pairs = pairs_of([lanes // 2])
     hidden = root
     for f in range(chunks):
         own_sum, sibling_sum = add(pairs, place, meta, edges, [[ends[f]]], [totals[f]], last=True)
+        if f + 1 < chunks:
+            totals, sibling_sum = lax.optimization_barrier((list(totals), sibling_sum))
         swapped = core_swap(sibling_sum)
         if groups == 2:
             other = rep_swap(own_sum[shard:] + swapped[shard:])

time: 78.3 us -> 71.8 us (0.917)
  waiting for transfers between devices: 25.3 us -> 23.5 us
  starting transfers between devices: 23.7 us -> 22.1 us
  Pallas kernels: 19.3 us -> 17.8 us
  other arithmetic: 4.49 us -> 3.48 us
    ppermute x16, waiting for transfers between devices: 15.5 us -> 10.4 us  [ring(): return lax.ppermute(value, 'blk', pairs)]
    ppermute x3, waiting for transfers between devices: 0.43 us -> 2.48 us  [core_swap(): return lax.ppermute(value, 'blk', [(b, b ^ 1) for b in range(blocks)])]
    ppermute x3, starting transfers between devices: 5.24 us -> 3.44 us  [rep_swap(): return lax.ppermute(value, 'rep', [(0, 1), (1, 0)])]
    pallas_call x7 -> x6, Pallas kernels: 19.3 us -> 17.8 us  [add_sources(): pl.pallas_call(functools.partial(sum_kernel, sources, chunks, pieces, slo...]
    ppermute x3, waiting for transfers between devices: 9.35 us -> 10.6 us  [rep_swap(): return lax.ppermute(value, 'rep', [(0, 1), (1, 0)])]
    concatenate x1, other arithmetic: 1.09 us -> 0.07 us  [on_device(): edges = jnp.concatenate([lists, rep_swap(lists)], axis=0)]
  transfers between devices with their start and end apart: 22 -> 22, of which waited for: 8 -> 9; matrix products, arithmetic and copies ran while one was open for 6% -> 5% of each run, Pallas kernels for 25% -> 21%
where the time goes in v4:
time: 71.8 us; the launch traced here: 72 us
  waiting for transfers between devices  23.5 us (33%)
  starting transfers between devices  22.1 us (31%)
  Pallas kernels  17.8 us (25%)
  other arithmetic  3.48 us (5%)
  matrix products  2.61 us (4%)
  between operations  1.29 us (2%)
  local copies, waits for them, and re-layouts  1.21 us (2%)
    ppermute x16, starting transfers between devices, ring(): return lax.ppermute(value, 'blk', pairs)  18 us
    pallas_call x6, Pallas kernels, add_sources(): pl.pallas_call(functools.partial(sum_kernel, sources, chunks, pieces, slo...  17.8 us
    ppermute x3, waiting for transfers between devices, rep_swap(): return lax.ppermute(value, 'rep', [(0, 1), (1, 0)])  10.6 us
    ppermute x16, waiting for transfers between devices, ring(): return lax.ppermute(value, 'blk', pairs)  10.4 us
    ppermute x3, starting transfers between devices, rep_swap(): return lax.ppermute(value, 'rep', [(0, 1), (1, 0)])  3.44 us
    ppermute x3, waiting for transfers between devices, core_swap(): return lax.ppermute(value, 'blk', [(b, b ^ 1) for b in range(blocks)])  2.48 us
    dot_general x2, matrix products, on_device(): jnp.dot(mixed, neighbor_weight[f * TILE:(f + 1) * TILE], precision=highest)  2.03 us
  transfers between devices with their start and end apart: 22, of which 9 were waited for; matrix products, arithmetic and copies ran while one was open for 5% of the time, Pallas kernels for 21%

profile of v4, /device:TPU:0, one launch (start us, length us, event | category | flops | bytes accessed | tf_op | source)
XLA Modules:
  0.0 72.0 jit_solution(17692828873752539743)
XLA Ops:
  0.0 0.7 %convert_rsqrt_fusion = f32[512]{0:T(512)S(1)} fusion(s32[512]{0:T(512)} %param.12), kind=kLoop, calls=%fused_computation.31 | loop fusion | flops 512 | bytes 4096 | tf_op jit(solution)/shard_map/rsqrt | solution.py:187
  0.7 1.2 %broadcast_multiply_fusion = f32[512,256]{1,0:T(8,128)S(1)} fusion(f32[512,256]{1,0:T(8,128)} %param.11, f32[512]{0:T(512)S(1)} %convert_rsqrt_fusion), kind=kLoop, calls=%fused_computation.17 | loop fusion | flops 131072 | bytes 1050624 | tf_op jit(solution)/shard_map/mul | solution.py:188
  2.0 3.1 %collective-permute-start.10 = (f32[512,128]{1,0:T(8,128)S(1)}, f32[512,128]{1,0:T(8,128)S(1)}, u32[]{:S(2)}, u32[]{:S(2)}) collective-permute-start(f32[512,128]{1,0:T(8,128)S(1)} %get-tuple-element.50.refs_5_), channel_id=1, source_target_pairs={{0,8},{2,10},{8,16},{10,18},{16,24},{18,26},{24,28},{26,30},{28,20... | collective-permute-start | bytes 786440 | tf_op jit(solution)/shard_map/ppermute | solution.py:179
  5.1 2.0 %collective-permute-start.2 = (f32[512,128]{1,0:T(8,128)S(1)}, f32[512,128]{1,0:T(8,128)S(1)}, u32[]{:S(2)}, u32[]{:S(2)}) collective-permute-start(f32[512,128]{1,0:T(8,128)S(1)} %get-tuple-element.49.refs_4_), channel_id=1, source_target_pairs={{0,8},{2,10},{8,16},{10,18},{16,24},{18,26},{24,28},{26,30},{28,20... | collective-permute-start | bytes 786440 | tf_op jit(solution)/shard_map/ppermute | solution.py:179
  9.7 0.8 %pad_add_fusion.1 = s32[8,56,256]{2,1,0:T(8,128)} fusion(s32[4,56,256]{2,1,0:T(8,128)S(1)} %collective-permute-done, s32[4,8,256]{2,1,0:T(8,128)S(1)} %pad.15, s32[4,16,256]{2,1,0:T(8,128)S(1)} %get-tuple-element.55, s32[4,16,256]{2,1,0:T(8,128)S(1)} %get-tuple-element.58, s32[4,16,256]{2,1,0:T(8,128)S(1)} %get-tuple-element.51), kind=kLoop, calls=%fused_computation.5 | loop fusion | flops 458752 | bytes 917504 | tf_op jit(solution)/shard_map/concatenate | solution.py:200
  10.5 1.9 %collective-permute-start.1 = (s32[8,56,256]{2,1,0:T(8,128)}, s32[8,56,256]{2,1,0:T(8,128)S(1)}, u32[]{:S(2)}, u32[]{:S(2)}) collective-permute-start(s32[8,56,256]{2,1,0:T(8,128)} %pad_add_fusion.1), channel_id=1, source_target_pairs={{0,1},{1,0},{2,3},{3,2},{4,5},{5,4},{6,7},{7,6},{8,9},{9,8},{10,11... | collective-permute-start | bytes 1376264 | tf_op jit(solution)/shard_map/ppermute | solution.py:185
  12.5 4.4 %collective-permute-done.2.refs_4_ = f32[512,128]{1,0:T(8,128)S(1)} collective-permute-done((f32[512,128]{1,0:T(8,128)S(1)}, f32[512,128]{1,0:T(8,128)S(1)}, u32[]{:S(2)}, u32[]{:S(2)}) %collective-permute-start.2) | collective-permute-done | bytes 262176 | tf_op jit(solution)/shard_map/ppermute | solution.py:179
  16.9 1.8 %collective-permute-start.3 = (f32[512,128]{1,0:T(8,128)S(1)}, f32[512,128]{1,0:T(8,128)S(1)}, u32[]{:S(2)}, u32[]{:S(2)}) collective-permute-start(f32[512,128]{1,0:T(8,128)S(1)} %collective-permute-done.2.refs_4_), channel_id=1, source_target_pairs={{0,8},{2,10},{8,16},{10,18},{16,24},{18,26},{24,28},{26,30},{28,20... | collective-permute-start | bytes 786440 | tf_op jit(solution)/shard_map/ppermute | solution.py:179
  19.6 1.8 %collective-permute-start.11 = (f32[512,128]{1,0:T(8,128)S(1)}, f32[512,128]{1,0:T(8,128)S(1)}, u32[]{:S(2)}, u32[]{:S(2)}) collective-permute-start(f32[512,128]{1,0:T(8,128)S(1)} %collective-permute-done.10.refs_5_), channel_id=1, source_target_pairs={{0,8},{2,10},{8,16},{10,18},{16,24},{18,26},{24,28},{26,30},{28,20... | collective-permute-start | bytes 786440 | tf_op jit(solution)/shard_map/ppermute | solution.py:179
  21.6 4.5 %collective-permute-done.3.refs_4_ = f32[512,128]{1,0:T(8,128)S(1)} collective-permute-done((f32[512,128]{1,0:T(8,128)S(1)}, f32[512,128]{1,0:T(8,128)S(1)}, u32[]{:S(2)}, u32[]{:S(2)}) %collective-permute-start.3) | collective-permute-done | bytes 262176 | tf_op jit(solution)/shard_map/ppermute | solution.py:179
  26.1 1.8 %collective-permute-start.4 = (f32[512,128]{1,0:T(8,128)S(1)}, f32[512,128]{1,0:T(8,128)S(1)}, u32[]{:S(2)}, u32[]{:S(2)}) collective-permute-start(f32[512,128]{1,0:T(8,128)S(1)} %collective-permute-done.3.refs_4_), channel_id=1, source_target_pairs={{0,8},{2,10},{8,16},{10,18},{16,24},{18,26},{24,28},{26,30},{28,20... | collective-permute-start | bytes 786440 | tf_op jit(solution)/shard_map/ppermute | solution.py:179
  28.3 2.2 %shard_map.109 = (f32[2,1024,128]{2,1,0:T(8,128)S(1)}, f32[2,1024,128]{2,1,0:T(8,128)S(1)}) custom-call(s32[2]{0:T(128)S(1)} %pad_add_fusion.9.refs_0_, s32[2]{0:T(128)S(1)} %pad_add_fusion.6.refs_1_, s32[16,128]{1,0:T(8,128)S(1)} %bitcast.39, s32[16,56,256]{2,1,0:T(8,128)S(1)} %pad_add_fusion.refs_3_, f32[512,128]{1,0:T(8,128)S(1)} %get-tuple-element.49.refs_4_, ...), custom_call_target="tpu_custom_call" | custom-call | flops 3000000000 | bytes 1048576 | tf_op jit(solution)/shard_map/pallas_call | solution.py:135
  30.5 4.2 %shard_map.110 = (f32[2,1024,128]{2,1,0:T(8,128)S(1)}, f32[2,1024,128]{2,1,0:T(8,128)S(1)}) custom-call(s32[4]{0:T(128)S(1)} %pad_add_fusion.8.refs_0_, s32[2]{0:T(128)S(1)} %pad_add_fusion.6.refs_1_, s32[16,128]{1,0:T(8,128)S(1)} %bitcast.40, s32[16,56,256]{2,1,0:T(8,128)S(1)} %pad_add_fusion.refs_3_, ...), custom_call_target="tpu_custom_call", output_to_operand_aliasing={{0}: (8, {}), {1}: (9, {})} | custom-call | flops 5000000000 | bytes 1048576 | tf_op jit(solution)/shard_map/pallas_call | solution.py:135
  34.7 1.3 %collective-permute-start.14 = (f32[512,128]{1,0:T(8,128)S(1)}, f32[512,128]{1,0:T(8,128)S(1)}, u32[]{:S(2)}, u32[]{:S(2)}) collective-permute-start(f32[512,128]{1,0:T(8,128)S(1)} %collective-permute-done.11.refs_5_), channel_id=1, source_target_pairs={{0,8},{2,10},{8,16},{10,18},{16,24},{18,26},{24,28},{26,30},{28,20... | collective-permute-start | bytes 786440 | tf_op jit(solution)/shard_map/ppermute | solution.py:179
  35.9 0.8 %collective-permute-start.15 = (f32[512,128]{1,0:T(8,128)S(1)}, f32[512,128]{1,0:T(8,128)S(1)}, u32[]{:S(2)}, u32[]{:S(2)}) collective-permute-start(f32[512,128]{1,0:T(8,128)S(1)} %collective-permute-done.13.refs_7_), channel_id=1, source_target_pairs={{0,4},{2,6},{8,0},{10,2},{16,8},{18,10},{24,16},{26,18},{28,24},{3... | collective-permute-start | bytes 786440 | tf_op jit(solution)/shard_map/ppermute | solution.py:179
  36.8 3.0 %shard_map.111 = (f32[2,1024,128]{2,1,0:T(8,128)S(1)}, f32[2,1024,128]{2,1,0:T(8,128)S(1)}) custom-call(s32[4]{0:T(128)S(1)} %pad_add_fusion.10.refs_0_, s32[2]{0:T(128)S(1)} %pad_add_fusion.6.refs_1_, s32[16,128]{1,0:T(8,128)S(1)} %bitcast.41, s32[16,56,256]{2,1,0:T(8,128)S(1)} %pad_add_fusion.refs_3_, ...), custom_call_target="tpu_custom_call", output_to_operand_aliasing={{0}: (8, {}), {1}: (9, {})} | custom-call | flops 5000000000 | bytes 1048576 | tf_op jit(solution)/shard_map/pallas_call | solution.py:135
  39.8 2.5 %collective-permute-start.5 = (f32[256,128]{1,0:T(8,128)S(1)}, f32[256,128]{1,0:T(8,128)S(1)}, u32[]{:S(2)}, u32[]{:S(2)}) collective-permute-start(f32[256,128]{1,0:T(8,128)S(1)} %slice.118), channel_id=1, source_target_pairs={{0,8},{2,10},{8,16},{10,18},{16,24},{18,26},{24,28},{26,30},{28,20... | collective-permute-start | bytes 393224 | tf_op jit(solution)/shard_map/ppermute | solution.py:179
  42.7 1.2 %collective-permute-done.15.refs_7_ = f32[512,128]{1,0:T(8,128)S(1)} collective-permute-done((f32[512,128]{1,0:T(8,128)S(1)}, f32[512,128]{1,0:T(8,128)S(1)}, u32[]{:S(2)}, u32[]{:S(2)}) %collective-permute-start.15) | collective-permute-done | bytes 262176 | tf_op jit(solution)/shard_map/ppermute | solution.py:179
  43.9 1.6 %collective-permute-start.18 = (f32[256,128]{1,0:T(8,128)S(1)}, f32[256,128]{1,0:T(8,128)S(1)}, u32[]{:S(2)}, u32[]{:S(2)}) collective-permute-start(f32[256,128]{1,0:T(8,128)S(1)} %slice.109), channel_id=1, source_target_pairs={{0,8},{2,10},{8,16},{10,18},{16,24},{18,26},{24,28},{26,30},{28,20... | collective-permute-start | bytes 393224 | tf_op jit(solution)/shard_map/ppermute | solution.py:179
  45.5 0.5 collective-permute-start.19
  46.0 3.6 %shard_map.112 = (f32[2,1024,128]{2,1,0:T(8,128)S(1)}, f32[2,1024,128]{2,1,0:T(8,128)S(1)}) custom-call(s32[4]{0:T(128)S(1)} %pad_add_fusion.7.refs_0_, s32[2]{0:T(128)S(1)} %pad_add_fusion.6.refs_1_, s32[16,128]{1,0:T(8,128)S(1)} %bitcast.42, s32[16,56,256]{2,1,0:T(8,128)S(1)} %pad_add_fusion.refs_3_, ...), custom_call_target="tpu_custom_call", output_to_operand_aliasing={{0}: (8, {}), {1}: (9, {})} | custom-call | flops 5000000000 | bytes 1048576 | tf_op jit(solution)/shard_map/pallas_call | solution.py:135
  49.6 2.4 %shard_map.113 = (f32[1024,128]{1,0:T(8,128)S(1)}, f32[1024,128]{1,0:T(8,128)S(1)}) custom-call(s32[2]{0:T(128)S(1)} %pad_add_fusion.5.refs_0_, s32[2]{0:T(128)S(1)} %pad_add_fusion.6.refs_1_, s32[16,128]{1,0:T(8,128)S(1)} %bitcast.43, s32[16,56,256]{2,1,0:T(8,128)S(1)} %pad_add_fusion.refs_3_, f32[256,128]{1,0:T(8,128)S(1)} %collective-permute-done.5.refs_4_, ...), custom_call_target="tpu_custom_call" | custom-call | flops 2000000000 | bytes 1048576 | tf_op jit(solution)/shard_map/pallas_call | solution.py:135
  52.1 2.4 %shard_map.114 = (f32[1024,128]{1,0:T(8,128)S(1)}, f32[1024,128]{1,0:T(8,128)S(1)}) custom-call(s32[2]{0:T(128)S(1)} %pad_add_fusion.5.refs_0_, s32[2]{0:T(128)S(1)} %pad_add_fusion.6.refs_1_, s32[16,128]{1,0:T(8,128)S(1)} %bitcast.44, s32[16,56,256]{2,1,0:T(8,128)S(1)} %pad_add_fusion.refs_3_, f32[256,128]{1,0:T(8,128)S(1)} %collective-permute-done.18.refs_4_, ...), custom_call_target="tpu_custom_call" | custom-call | flops 2000000000 | bytes 1048576 | tf_op jit(solution)/shard_map/pallas_call | solution.py:135
  54.6 0.5 collective-permute-start.16
  55.1 1.4 %collective-permute-done.20 = f32[1024,128]{1,0:T(8,128)S(1)} collective-permute-done((f32[1024,128]{1,0:T(8,128)S(1)}, f32[1024,128]{1,0:T(8,128)S(1)}, u32[]{:S(2)}, u32[]{:S(2)}) %collective-permute-start.20) | collective-permute-done | bytes 524320 | tf_op jit(solution)/shard_map/ppermute | solution.py:182
  56.6 0.6 collective-permute-done.16
  57.3 1.5 %collective-permute-start.17 = (f32[512,128]{1,0:T(8,128)S(1)}, f32[512,128]{1,0:T(8,128)S(1)}, u32[]{:S(2)}, u32[]{:S(2)}) collective-permute-start(f32[512,128]{1,0:T(8,128)S(1)} %slice_add_fusion.2), channel_id=1, source_target_pairs={{0,1},{1,0},{2,3},{3,2},{4,5},{5,4},{6,7},{7,6},{8,9},{9,8},{10,11... | collective-permute-start | bytes 786440 | tf_op jit(solution)/shard_map/ppermute | solution.py:185
  58.8 0.6 convolution_add_fusion.1
  59.3 6.4 %collective-permute-done.21 = f32[512,128]{1,0:T(8,128)S(1)} collective-permute-done((f32[512,128]{1,0:T(8,128)S(1)}, f32[512,128]{1,0:T(8,128)S(1)}, u32[]{:S(2)}, u32[]{:S(2)}) %collective-permute-start.21) | collective-permute-done | bytes 262176 | tf_op jit(solution)/shard_map/ppermute | solution.py:185
  65.8 0.6 fusion.4
  66.4 4.2 %collective-permute-done.17 = f32[512,128]{1,0:T(8,128)S(1)} collective-permute-done((f32[512,128]{1,0:T(8,128)S(1)}, f32[512,128]{1,0:T(8,128)S(1)}, u32[]{:S(2)}, u32[]{:S(2)}) %collective-permute-start.17) | collective-permute-done | bytes 262176 | tf_op jit(solution)/shard_map/ppermute | solution.py:185
  70.6 1.4 %fusion.1 = f32[512,256]{1,0:T(8,128)} fusion(f32[512,256]{1,0:T(8,128)S(1)} %fusion.4, f32[512,256]{1,0:T(8,128)S(1)} %convolution_add_fusion.1, f32[512,128]{1,0:T(8,128)S(1)} %collective-permute-done.17, f32[1024,128]{1,0:T(8,128)S(1)} %collective-permute-done.16, f32[1024,128]{1,0:T(8,128)S(1)} %get-tuple-element.42, f32[256,256]{1,0:T(8,128)S(1)} %copy-done.2, ...), kind=kOutput, calls=%fused_computation.2 | convolution fusion | flops 201916416 | bytes 2492416 | tf_op jit(solution)/shard_map/dot_general | solution.py:264
  (77 shorter events, 3.8 us)
Async XLA Ops:
  0.0 58.8 %copy-start = (f32[256,256]{1,0:T(8,128)S(1)}, f32[256,256]{1,0:T(8,128)}, u32[]{:S(2)}) copy-start(f32[256,256]{1,0:T(8,128)} %param.13) | copy-start | bytes 786436
  1.9 5.2 %copy-start.3 = (s32[1,8,16,256]{3,2,1,0:T(8,128)S(1)}, s32[1,8,16,256]{3,2,1,0:T(8,128)}, u32[]{:S(2)}) copy-start(s32[1,8,16,256]{3,2,1,0:T(8,128)} %param.19) | copy-start | bytes 393220
  2.0 17.6 %collective-permute-start.10 = (f32[512,128]{1,0:T(8,128)S(1)}, f32[512,128]{1,0:T(8,128)S(1)}, u32[]{:S(2)}, u32[]{:S(2)}) collective-permute-start(f32[512,128]{1,0:T(8,128)S(1)} %get-tuple-element.50.refs_5_), channel_id=1, source_target_pairs={{0,8},{2,10},{8,16},{10,18},{16,24},{18,26},{24,28},{26,30},{28,20... | collective-permute-start | bytes 786440 | tf_op jit(solution)/shard_map/ppermute | solution.py:179
  5.0 16.4 %collective-permute-start.12 = (f32[512,128]{1,0:T(8,128)S(1)}, f32[512,128]{1,0:T(8,128)S(1)}, u32[]{:S(2)}, u32[]{:S(2)}) collective-permute-start(f32[512,128]{1,0:T(8,128)S(1)} %get-tuple-element.50.refs_5_), channel_id=1, source_target_pairs={{0,4},{2,6},{8,0},{10,2},{16,8},{18,10},{24,16},{26,18},{28,24},{3... | collective-permute-start | bytes 786440 | tf_op jit(solution)/shard_map/ppermute | solution.py:179
  5.0 2.1 %copy-start.9 = (s32[1,8]{1,0:T(1,128)S(1)}, s32[1,8]{1,0:T(1,128)}, u32[]{:S(2)}) copy-start(s32[1,8]{1,0:T(1,128)} %param.18) | copy-start | bytes 100
  5.1 3.0 %copy-start.4 = (s32[1,8,16,256]{3,2,1,0:T(8,128)S(1)}, s32[1,8,16,256]{3,2,1,0:T(8,128)}, u32[]{:S(2)}) copy-start(s32[1,8,16,256]{3,2,1,0:T(8,128)} %param.21) | copy-start | bytes 393220
  5.1 3.0 %copy-start.5 = (s32[1,8,16,256]{3,2,1,0:T(8,128)S(1)}, s32[1,8,16,256]{3,2,1,0:T(8,128)}, u32[]{:S(2)}) copy-start(s32[1,8,16,256]{3,2,1,0:T(8,128)} %param.20) | copy-start | bytes 393220
  5.1 11.8 %collective-permute-start.2 = (f32[512,128]{1,0:T(8,128)S(1)}, f32[512,128]{1,0:T(8,128)S(1)}, u32[]{:S(2)}, u32[]{:S(2)}) collective-permute-start(f32[512,128]{1,0:T(8,128)S(1)} %get-tuple-element.49.refs_4_), channel_id=1, source_target_pairs={{0,8},{2,10},{8,16},{10,18},{16,24},{18,26},{24,28},{26,30},{28,20... | collective-permute-start | bytes 786440 | tf_op jit(solution)/shard_map/ppermute | solution.py:179
  7.1 11.6 %collective-permute-start.6 = (f32[512,128]{1,0:T(8,128)S(1)}, f32[512,128]{1,0:T(8,128)S(1)}, u32[]{:S(2)}, u32[]{:S(2)}) collective-permute-start(f32[512,128]{1,0:T(8,128)S(1)} %get-tuple-element.49.refs_4_), channel_id=1, source_target_pairs={{0,4},{2,6},{8,0},{10,2},{16,8},{18,10},{24,16},{26,18},{28,24},{3... | collective-permute-start | bytes 786440 | tf_op jit(solution)/shard_map/ppermute | solution.py:179
  7.2 0.7 copy-start.6
  7.3 0.7 copy-start.7
  8.1 1.6 %collective-permute-start = (s32[4,56,256]{2,1,0:T(8,128)S(1)}, s32[4,56,256]{2,1,0:T(8,128)S(1)}, u32[]{:S(2)}, u32[]{:S(2)}) collective-permute-start(s32[4,56,256]{2,1,0:T(8,128)S(1)} %pad_add_fusion.2), channel_id=1, source_target_pairs={{0,2},{2,0},{4,6},{6,4},{8,10},{10,8},{12,14},{14,12},{16,18},{18,... | collective-permute-start | bytes 688136 | tf_op jit(solution)/shard_map/ppermute | solution.py:182
  10.5 17.7 %collective-permute-start.1 = (s32[8,56,256]{2,1,0:T(8,128)}, s32[8,56,256]{2,1,0:T(8,128)S(1)}, u32[]{:S(2)}, u32[]{:S(2)}) collective-permute-start(s32[8,56,256]{2,1,0:T(8,128)} %pad_add_fusion.1), channel_id=1, source_target_pairs={{0,1},{1,0},{2,3},{3,2},{4,5},{5,4},{6,7},{7,6},{8,9},{9,8},{10,11... | collective-permute-start | bytes 1376264 | tf_op jit(solution)/shard_map/ppermute | solution.py:185
  16.9 9.2 %collective-permute-start.3 = (f32[512,128]{1,0:T(8,128)S(1)}, f32[512,128]{1,0:T(8,128)S(1)}, u32[]{:S(2)}, u32[]{:S(2)}) collective-permute-start(f32[512,128]{1,0:T(8,128)S(1)} %collective-permute-done.2.refs_4_), channel_id=1, source_target_pairs={{0,8},{2,10},{8,16},{10,18},{16,24},{18,26},{24,28},{26,30},{28,20... | collective-permute-start | bytes 786440 | tf_op jit(solution)/shard_map/ppermute | solution.py:179
  18.7 9.2 %collective-permute-start.7 = (f32[512,128]{1,0:T(8,128)S(1)}, f32[512,128]{1,0:T(8,128)S(1)}, u32[]{:S(2)}, u32[]{:S(2)}) collective-permute-start(f32[512,128]{1,0:T(8,128)S(1)} %collective-permute-done.6.refs_6_), channel_id=1, source_target_pairs={{0,4},{2,6},{8,0},{10,2},{16,8},{18,10},{24,16},{26,18},{28,24},{3... | collective-permute-start | bytes 786440 | tf_op jit(solution)/shard_map/ppermute | solution.py:179
  19.6 15.1 %collective-permute-start.11 = (f32[512,128]{1,0:T(8,128)S(1)}, f32[512,128]{1,0:T(8,128)S(1)}, u32[]{:S(2)}, u32[]{:S(2)}) collective-permute-start(f32[512,128]{1,0:T(8,128)S(1)} %collective-permute-done.10.refs_5_), channel_id=1, source_target_pairs={{0,8},{2,10},{8,16},{10,18},{16,24},{18,26},{24,28},{26,30},{28,20... | collective-permute-start | bytes 786440 | tf_op jit(solution)/shard_map/ppermute | solution.py:179
  21.4 13.2 %collective-permute-start.13 = (f32[512,128]{1,0:T(8,128)S(1)}, f32[512,128]{1,0:T(8,128)S(1)}, u32[]{:S(2)}, u32[]{:S(2)}) collective-permute-start(f32[512,128]{1,0:T(8,128)S(1)} %collective-permute-done.12.refs_7_), channel_id=1, source_target_pairs={{0,4},{2,6},{8,0},{10,2},{16,8},{18,10},{24,16},{26,18},{28,24},{3... | collective-permute-start | bytes 786440 | tf_op jit(solution)/shard_map/ppermute | solution.py:179
  26.1 13.6 %collective-permute-start.4 = (f32[512,128]{1,0:T(8,128)S(1)}, f32[512,128]{1,0:T(8,128)S(1)}, u32[]{:S(2)}, u32[]{:S(2)}) collective-permute-start(f32[512,128]{1,0:T(8,128)S(1)} %collective-permute-done.3.refs_4_), channel_id=1, source_target_pairs={{0,8},{2,10},{8,16},{10,18},{16,24},{18,26},{24,28},{26,30},{28,20... | collective-permute-start | bytes 786440 | tf_op jit(solution)/shard_map/ppermute | solution.py:179
  28.0 14.3 %collective-permute-start.8 = (f32[512,128]{1,0:T(8,128)S(1)}, f32[512,128]{1,0:T(8,128)S(1)}, u32[]{:S(2)}, u32[]{:S(2)}) collective-permute-start(f32[512,128]{1,0:T(8,128)S(1)} %collective-permute-done.7.refs_6_), channel_id=1, source_target_pairs={{0,4},{2,6},{8,0},{10,2},{16,8},{18,10},{24,16},{26,18},{28,24},{3... | collective-permute-start | bytes 786440 | tf_op jit(solution)/shard_map/ppermute | solution.py:179
  34.7 8.0 %collective-permute-start.14 = (f32[512,128]{1,0:T(8,128)S(1)}, f32[512,128]{1,0:T(8,128)S(1)}, u32[]{:S(2)}, u32[]{:S(2)}) collective-permute-start(f32[512,128]{1,0:T(8,128)S(1)} %collective-permute-done.11.refs_5_), channel_id=1, source_target_pairs={{0,8},{2,10},{8,16},{10,18},{16,24},{18,26},{24,28},{26,30},{28,20... | collective-permute-start | bytes 786440 | tf_op jit(solution)/shard_map/ppermute | solution.py:179
  35.9 7.9 %collective-permute-start.15 = (f32[512,128]{1,0:T(8,128)S(1)}, f32[512,128]{1,0:T(8,128)S(1)}, u32[]{:S(2)}, u32[]{:S(2)}) collective-permute-start(f32[512,128]{1,0:T(8,128)S(1)} %collective-permute-done.13.refs_7_), channel_id=1, source_target_pairs={{0,4},{2,6},{8,0},{10,2},{16,8},{18,10},{24,16},{26,18},{28,24},{3... | collective-permute-start | bytes 786440 | tf_op jit(solution)/shard_map/ppermute | solution.py:179
  39.8 9.9 %collective-permute-start.5 = (f32[256,128]{1,0:T(8,128)S(1)}, f32[256,128]{1,0:T(8,128)S(1)}, u32[]{:S(2)}, u32[]{:S(2)}) collective-permute-start(f32[256,128]{1,0:T(8,128)S(1)} %slice.118), channel_id=1, source_target_pairs={{0,8},{2,10},{8,16},{10,18},{16,24},{18,26},{24,28},{26,30},{28,20... | collective-permute-start | bytes 393224 | tf_op jit(solution)/shard_map/ppermute | solution.py:179
  42.3 7.3 %collective-permute-start.9 = (f32[256,128]{1,0:T(8,128)S(1)}, f32[256,128]{1,0:T(8,128)S(1)}, u32[]{:S(2)}, u32[]{:S(2)}) collective-permute-start(f32[256,128]{1,0:T(8,128)S(1)} %slice.119), channel_id=1, source_target_pairs={{0,4},{2,6},{8,0},{10,2},{16,8},{18,10},{24,16},{26,18},{28,24},{3... | collective-permute-start | bytes 393224 | tf_op jit(solution)/shard_map/ppermute | solution.py:179
  43.9 8.2 %collective-permute-start.18 = (f32[256,128]{1,0:T(8,128)S(1)}, f32[256,128]{1,0:T(8,128)S(1)}, u32[]{:S(2)}, u32[]{:S(2)}) collective-permute-start(f32[256,128]{1,0:T(8,128)S(1)} %slice.109), channel_id=1, source_target_pairs={{0,8},{2,10},{8,16},{10,18},{16,24},{18,26},{24,28},{26,30},{28,20... | collective-permute-start | bytes 393224 | tf_op jit(solution)/shard_map/ppermute | solution.py:179
  45.5 6.5 %collective-permute-start.19 = (f32[256,128]{1,0:T(8,128)S(1)}, f32[256,128]{1,0:T(8,128)S(1)}, u32[]{:S(2)}, u32[]{:S(2)}) collective-permute-start(f32[256,128]{1,0:T(8,128)S(1)} %slice.110), channel_id=1, source_target_pairs={{0,4},{2,6},{8,0},{10,2},{16,8},{18,10},{24,16},{26,18},{28,24},{3... | collective-permute-start | bytes 393224 | tf_op jit(solution)/shard_map/ppermute | solution.py:179
  54.5 2.0 %collective-permute-start.20 = (f32[1024,128]{1,0:T(8,128)S(1)}, f32[1024,128]{1,0:T(8,128)S(1)}, u32[]{:S(2)}, u32[]{:S(2)}) collective-permute-start(f32[1024,128]{1,0:T(8,128)S(1)} %get-tuple-element.48), channel_id=1, source_target_pairs={{0,2},{2,0},{4,6},{6,4},{8,10},{10,8},{12,14},{14,12},{16,18},{18,... | collective-permute-start | bytes 1572872 | tf_op jit(solution)/shard_map/ppermute | solution.py:182
  54.6 2.6 %collective-permute-start.16 = (f32[1024,128]{1,0:T(8,128)S(1)}, f32[1024,128]{1,0:T(8,128)S(1)}, u32[]{:S(2)}, u32[]{:S(2)}) collective-permute-start(f32[1024,128]{1,0:T(8,128)S(1)} %get-tuple-element.45), channel_id=1, source_target_pairs={{0,2},{2,0},{4,6},{6,4},{8,10},{10,8},{12,14},{14,12},{16,18},{18,... | collective-permute-start | bytes 1572872 | tf_op jit(solution)/shard_map/ppermute | solution.py:182
  56.5 2.2 %copy-start.1 = (f32[512,256]{1,0:T(8,128)S(1)}, f32[512,256]{1,0:T(8,128)}, u32[]{:S(2)}) copy-start(f32[512,256]{1,0:T(8,128)} %param.11) | copy-start | bytes 1572868
  56.5 9.2 %collective-permute-start.21 = (f32[512,128]{1,0:T(8,128)S(1)}, f32[512,128]{1,0:T(8,128)S(1)}, u32[]{:S(2)}, u32[]{:S(2)}) collective-permute-start(f32[512,128]{1,0:T(8,128)S(1)} %slice_add_fusion), channel_id=1, source_target_pairs={{0,1},{1,0},{2,3},{3,2},{4,5},{5,4},{6,7},{7,6},{8,9},{9,8},{10,11... | collective-permute-start | bytes 786440 | tf_op jit(solution)/shard_map/ppermute | solution.py:185
  57.2 1.5 %copy-start.8 = (f32[256]{0:T(256)S(1)}, f32[256]{0:T(256)}, u32[]{:S(2)}) copy-start(f32[256]{0:T(256)} %param.15) | copy-start | bytes 3076
  57.3 8.5 %copy-start.2 = (f32[256,256]{1,0:T(8,128)S(1)}, f32[256,256]{1,0:T(8,128)}, u32[]{:S(2)}) copy-start(f32[256,256]{1,0:T(8,128)} %param.14) | copy-start | bytes 786436
  57.3 13.3 %collective-permute-start.17 = (f32[512,128]{1,0:T(8,128)S(1)}, f32[512,128]{1,0:T(8,128)S(1)}, u32[]{:S(2)}, u32[]{:S(2)}) collective-permute-start(f32[512,128]{1,0:T(8,128)S(1)} %slice_add_fusion.2), channel_id=1, source_target_pairs={{0,1},{1,0},{2,3},{3,2},{4,5},{5,4},{6,7},{7,6},{8,9},{9,8},{10,11... | collective-permute-start | bytes 786440 | tf_op jit(solution)/shard_map/ppermute | solution.py:185

commit v5 on v4

--- a/solution.py
+++ b/solution.py
@@ -236,7 +236,7 @@
         up, down = hops[-1]
         if totals is not None:
             up, down = list(up), list(down)
-            up[-1], down[-1], totals = lax.optimization_barrier((up[-1], down[-1], totals))
+            up[0], down[0], totals = lax.optimization_barrier((up[0], down[0], totals))
         hops.append(([ring(v, 1) for v in up], [ring(v, -1) for v in down]))
         if step == 2:
             totals = add(pairs_of([0]), place, meta, edges, [[[v] for v in own]], None)
@@ -244,7 +244,7 @@
             parts = [[[v] for v in side] for side in hops[step - 1]]
             totals = add(pairs_of([1 - step, step - 1]), place, meta, edges, parts, totals)
     up, down = [list(side) for side in hops[-1]]
-    up[-1], down[-1], totals = lax.optimization_barrier((up[-1], down[-1], totals))
+    up[0], down[0], totals = lax.optimization_barrier((up[0], down[0], totals))
     ends = [[ring(up[f][:half], 1), ring(down[f][half:], -1)] for f in range(chunks)]
     step = lanes // 2 - 1
     totals = add(pairs_of([-step, step]), place, meta, edges, [[[v] for v in up], [[v] for v in down]], totals)
@@ -252,8 +252,6 @@
     hidden = root
     for f in range(chunks):
         own_sum, sibling_sum = add(pairs, place, meta, edges, [[ends[f]]], [totals[f]], last=True)
-        if f + 1 < chunks:
-            totals, sibling_sum = lax.optimization_barrier((list(totals), sibling_sum))
         swapped = core_swap(sibling_sum)
         if groups == 2:
             other = rep_swap(own_sum[shard:] + swapped[shard:])

time: 71.8 us -> 70.1 us (0.976); the launches traced: 72 us -> 69.3 us
  waiting for transfers between devices: 23.5 us -> 20.7 us
  starting transfers between devices: 22.1 us -> 24.5 us
  Pallas kernels: 17.8 us -> 15.6 us
    pallas_call x6, Pallas kernels: 17.8 us -> 15.6 us  [add_sources(): pl.pallas_call(functools.partial(sum_kernel, sources, chunks, pieces, slo...]
    ppermute x3, starting transfers between devices: 3.44 us -> 5.62 us  [rep_swap(): return lax.ppermute(value, 'rep', [(0, 1), (1, 0)])]
    ppermute x3, waiting for transfers between devices: 2.48 us -> 0.47 us  [core_swap(): return lax.ppermute(value, 'blk', [(b, b ^ 1) for b in range(blocks)])]
    ppermute x3, waiting for transfers between devices: 10.6 us -> 9.35 us  [rep_swap(): return lax.ppermute(value, 'rep', [(0, 1), (1, 0)])]
  transfers between devices with their start and end apart: 22 -> 22, of which waited for: 9 -> 7; matrix products, arithmetic and copies ran while one was open for 5% -> 5% of each run, Pallas kernels for 21% -> 22%
where the time goes in v5:
time: 70.1 us; the launch traced here: 69.3 us
  starting transfers between devices  24.5 us (35%)
  waiting for transfers between devices  20.7 us (30%)
  Pallas kernels  15.6 us (22%)
  other arithmetic  3.46 us (5%)
  matrix products  2.62 us (4%)
  between operations  1.28 us (2%)
  local copies, waits for them, and re-layouts  1.21 us (2%)
    ppermute x16, starting transfers between devices, ring(): return lax.ppermute(value, 'blk', pairs)  18.2 us
    pallas_call x6, Pallas kernels, add_sources(): pl.pallas_call(functools.partial(sum_kernel, sources, chunks, pieces, slo...  15.6 us
    ppermute x16, waiting for transfers between devices, ring(): return lax.ppermute(value, 'blk', pairs)  10.9 us
    ppermute x3, waiting for transfers between devices, rep_swap(): return lax.ppermute(value, 'rep', [(0, 1), (1, 0)])  9.35 us
    ppermute x3, starting transfers between devices, rep_swap(): return lax.ppermute(value, 'rep', [(0, 1), (1, 0)])  5.62 us
    dot_general x2, matrix products, on_device(): jnp.dot(mixed, neighbor_weight[f * TILE:(f + 1) * TILE], precision=highest)  2.03 us
  transfers between devices with their start and end apart: 22, of which 7 were waited for; matrix products, arithmetic and copies ran while one was open for 5% of the time, Pallas kernels for 22%

profile of v5, /device:TPU:0, one launch (start us, length us, event | category | flops | bytes accessed | tf_op | source)
XLA Modules:
  0.0 69.3 jit_solution(13858459534353179142)
XLA Ops:
  0.0 0.7 %convert_rsqrt_fusion = f32[512]{0:T(512)S(1)} fusion(s32[512]{0:T(512)} %param.12), kind=kLoop, calls=%fused_computation.31 | loop fusion | flops 512 | bytes 4096 | tf_op jit(solution)/shard_map/rsqrt | solution.py:187
  0.7 1.2 %broadcast_multiply_fusion = f32[512,256]{1,0:T(8,128)S(1)} fusion(f32[512,256]{1,0:T(8,128)} %param.11, f32[512]{0:T(512)S(1)} %convert_rsqrt_fusion), kind=kLoop, calls=%fused_computation.17 | loop fusion | flops 131072 | bytes 1050624 | tf_op jit(solution)/shard_map/mul | solution.py:188
  2.0 3.1 %collective-permute-start.2 = (f32[512,128]{1,0:T(8,128)S(1)}, f32[512,128]{1,0:T(8,128)S(1)}, u32[]{:S(2)}, u32[]{:S(2)}) collective-permute-start(f32[512,128]{1,0:T(8,128)S(1)} %get-tuple-element.45.refs_4_), channel_id=1, source_target_pairs={{0,8},{2,10},{8,16},{10,18},{16,24},{18,26},{24,28},{26,30},{28,20... | collective-permute-start | bytes 786440 | tf_op jit(solution)/shard_map/ppermute | solution.py:179
  5.1 2.0 %collective-permute-start.6 = (f32[512,128]{1,0:T(8,128)S(1)}, f32[512,128]{1,0:T(8,128)S(1)}, u32[]{:S(2)}, u32[]{:S(2)}) collective-permute-start(f32[512,128]{1,0:T(8,128)S(1)} %get-tuple-element.46.refs_5_), channel_id=1, source_target_pairs={{0,8},{2,10},{8,16},{10,18},{16,24},{18,26},{24,28},{26,30},{28,20... | collective-permute-start | bytes 786440 | tf_op jit(solution)/shard_map/ppermute | solution.py:179
  9.7 0.8 %pad_add_fusion.1 = s32[8,56,256]{2,1,0:T(8,128)} fusion(s32[4,56,256]{2,1,0:T(8,128)S(1)} %collective-permute-done, s32[4,8,256]{2,1,0:T(8,128)S(1)} %pad.15, s32[4,16,256]{2,1,0:T(8,128)S(1)} %get-tuple-element.51, s32[4,16,256]{2,1,0:T(8,128)S(1)} %get-tuple-element.54, s32[4,16,256]{2,1,0:T(8,128)S(1)} %get-tuple-element.47), kind=kLoop, calls=%fused_computation.5 | loop fusion | flops 458752 | bytes 917504 | tf_op jit(solution)/shard_map/concatenate | solution.py:200
  10.5 1.9 %collective-permute-start.1 = (s32[8,56,256]{2,1,0:T(8,128)}, s32[8,56,256]{2,1,0:T(8,128)S(1)}, u32[]{:S(2)}, u32[]{:S(2)}) collective-permute-start(s32[8,56,256]{2,1,0:T(8,128)} %pad_add_fusion.1), channel_id=1, source_target_pairs={{0,1},{1,0},{2,3},{3,2},{4,5},{5,4},{6,7},{7,6},{8,9},{9,8},{10,11... | collective-permute-start | bytes 1376264 | tf_op jit(solution)/shard_map/ppermute | solution.py:185
  12.5 4.4 %collective-permute-done.6.refs_5_ = f32[512,128]{1,0:T(8,128)S(1)} collective-permute-done((f32[512,128]{1,0:T(8,128)S(1)}, f32[512,128]{1,0:T(8,128)S(1)}, u32[]{:S(2)}, u32[]{:S(2)}) %collective-permute-start.6) | collective-permute-done | bytes 262176 | tf_op jit(solution)/shard_map/ppermute | solution.py:179
  16.9 1.8 %collective-permute-start.10 = (f32[512,128]{1,0:T(8,128)S(1)}, f32[512,128]{1,0:T(8,128)S(1)}, u32[]{:S(2)}, u32[]{:S(2)}) collective-permute-start(f32[512,128]{1,0:T(8,128)S(1)} %collective-permute-done.6.refs_5_), channel_id=1, source_target_pairs={{0,8},{2,10},{8,16},{10,18},{16,24},{18,26},{24,28},{26,30},{28,20... | collective-permute-start | bytes 786440 | tf_op jit(solution)/shard_map/ppermute | solution.py:179
  19.6 1.8 %collective-permute-start.3 = (f32[512,128]{1,0:T(8,128)S(1)}, f32[512,128]{1,0:T(8,128)S(1)}, u32[]{:S(2)}, u32[]{:S(2)}) collective-permute-start(f32[512,128]{1,0:T(8,128)S(1)} %collective-permute-done.2.refs_4_), channel_id=1, source_target_pairs={{0,8},{2,10},{8,16},{10,18},{16,24},{18,26},{24,28},{26,30},{28,20... | collective-permute-start | bytes 786440 | tf_op jit(solution)/shard_map/ppermute | solution.py:179
  21.6 4.5 %collective-permute-done.10.refs_5_ = f32[512,128]{1,0:T(8,128)S(1)} collective-permute-done((f32[512,128]{1,0:T(8,128)S(1)}, f32[512,128]{1,0:T(8,128)S(1)}, u32[]{:S(2)}, u32[]{:S(2)}) %collective-permute-start.10) | collective-permute-done | bytes 262176 | tf_op jit(solution)/shard_map/ppermute | solution.py:179
  26.1 1.8 %collective-permute-start.14 = (f32[512,128]{1,0:T(8,128)S(1)}, f32[512,128]{1,0:T(8,128)S(1)}, u32[]{:S(2)}, u32[]{:S(2)}) collective-permute-start(f32[512,128]{1,0:T(8,128)S(1)} %collective-permute-done.10.refs_5_), channel_id=1, source_target_pairs={{0,8},{2,10},{8,16},{10,18},{16,24},{18,26},{24,28},{26,30},{28,20... | collective-permute-start | bytes 786440 | tf_op jit(solution)/shard_map/ppermute | solution.py:179
  28.3 2.2 %shard_map.109 = (f32[2,1024,128]{2,1,0:T(8,128)S(1)}, f32[2,1024,128]{2,1,0:T(8,128)S(1)}) custom-call(s32[2]{0:T(128)S(1)} %pad_add_fusion.8.refs_0_, s32[2]{0:T(128)S(1)} %pad_add_fusion.6.refs_1_, s32[16,128]{1,0:T(8,128)S(1)} %bitcast.39, s32[16,56,256]{2,1,0:T(8,128)S(1)} %pad_add_fusion.refs_3_, f32[512,128]{1,0:T(8,128)S(1)} %get-tuple-element.45.refs_4_, ...), custom_call_target="tpu_custom_call" | custom-call | flops 3000000000 | bytes 1048576 | tf_op jit(solution)/shard_map/pallas_call | solution.py:135
  30.5 3.6 %shard_map.110 = (f32[2,1024,128]{2,1,0:T(8,128)S(1)}, f32[2,1024,128]{2,1,0:T(8,128)S(1)}) custom-call(s32[4]{0:T(128)S(1)} %pad_add_fusion.7.refs_0_, s32[2]{0:T(128)S(1)} %pad_add_fusion.6.refs_1_, s32[16,128]{1,0:T(8,128)S(1)} %bitcast.40, s32[16,56,256]{2,1,0:T(8,128)S(1)} %pad_add_fusion.refs_3_, ...), custom_call_target="tpu_custom_call", output_to_operand_aliasing={{0}: (8, {}), {1}: (9, {})} | custom-call | flops 5000000000 | bytes 1048576 | tf_op jit(solution)/shard_map/pallas_call | solution.py:135
  34.1 1.3 %collective-permute-start.8 = (f32[512,128]{1,0:T(8,128)S(1)}, f32[512,128]{1,0:T(8,128)S(1)}, u32[]{:S(2)}, u32[]{:S(2)}) collective-permute-start(f32[512,128]{1,0:T(8,128)S(1)} %collective-permute-done.3.refs_4_), channel_id=1, source_target_pairs={{0,8},{2,10},{8,16},{10,18},{16,24},{18,26},{24,28},{26,30},{28,20... | collective-permute-start | bytes 786440 | tf_op jit(solution)/shard_map/ppermute | solution.py:179
  35.3 0.8 %collective-permute-start.9 = (f32[512,128]{1,0:T(8,128)S(1)}, f32[512,128]{1,0:T(8,128)S(1)}, u32[]{:S(2)}, u32[]{:S(2)}) collective-permute-start(f32[512,128]{1,0:T(8,128)S(1)} %collective-permute-done.5.refs_6_), channel_id=1, source_target_pairs={{0,4},{2,6},{8,0},{10,2},{16,8},{18,10},{24,16},{26,18},{28,24},{3... | collective-permute-start | bytes 786440 | tf_op jit(solution)/shard_map/ppermute | solution.py:179
  36.1 3.0 %shard_map.111 = (f32[2,1024,128]{2,1,0:T(8,128)S(1)}, f32[2,1024,128]{2,1,0:T(8,128)S(1)}) custom-call(s32[4]{0:T(128)S(1)} %pad_add_fusion.9.refs_0_, s32[2]{0:T(128)S(1)} %pad_add_fusion.6.refs_1_, s32[16,128]{1,0:T(8,128)S(1)} %bitcast.41, s32[16,56,256]{2,1,0:T(8,128)S(1)} %pad_add_fusion.refs_3_, ...), custom_call_target="tpu_custom_call", output_to_operand_aliasing={{0}: (8, {}), {1}: (9, {})} | custom-call | flops 5000000000 | bytes 1048576 | tf_op jit(solution)/shard_map/pallas_call | solution.py:135
  39.1 1.3 %collective-permute-start.18 = (f32[256,128]{1,0:T(8,128)S(1)}, f32[256,128]{1,0:T(8,128)S(1)}, u32[]{:S(2)}, u32[]{:S(2)}) collective-permute-start(f32[256,128]{1,0:T(8,128)S(1)} %slice.121), channel_id=1, source_target_pairs={{0,8},{2,10},{8,16},{10,18},{16,24},{18,26},{24,28},{26,30},{28,20... | collective-permute-start | bytes 393224 | tf_op jit(solution)/shard_map/ppermute | solution.py:179
  40.4 1.5 %collective-permute-start.19 = (f32[256,128]{1,0:T(8,128)S(1)}, f32[256,128]{1,0:T(8,128)S(1)}, u32[]{:S(2)}, u32[]{:S(2)}) collective-permute-start(f32[256,128]{1,0:T(8,128)S(1)} %slice.122), channel_id=1, source_target_pairs={{0,4},{2,6},{8,0},{10,2},{16,8},{18,10},{24,16},{26,18},{28,24},{3... | collective-permute-start | bytes 393224 | tf_op jit(solution)/shard_map/ppermute | solution.py:179
  41.9 0.8 %collective-permute-done.8.refs_4_ = f32[512,128]{1,0:T(8,128)S(1)} collective-permute-done((f32[512,128]{1,0:T(8,128)S(1)}, f32[512,128]{1,0:T(8,128)S(1)}, u32[]{:S(2)}, u32[]{:S(2)}) %collective-permute-start.8) | collective-permute-done | bytes 262176 | tf_op jit(solution)/shard_map/ppermute | solution.py:179
  42.6 1.2 %collective-permute-done.9.refs_6_ = f32[512,128]{1,0:T(8,128)S(1)} collective-permute-done((f32[512,128]{1,0:T(8,128)S(1)}, f32[512,128]{1,0:T(8,128)S(1)}, u32[]{:S(2)}, u32[]{:S(2)}) %collective-permute-start.9) | collective-permute-done | bytes 262176 | tf_op jit(solution)/shard_map/ppermute | solution.py:179
  43.9 1.6 %collective-permute-start.12 = (f32[256,128]{1,0:T(8,128)S(1)}, f32[256,128]{1,0:T(8,128)S(1)}, u32[]{:S(2)}, u32[]{:S(2)}) collective-permute-start(f32[256,128]{1,0:T(8,128)S(1)} %slice.102), channel_id=1, source_target_pairs={{0,8},{2,10},{8,16},{10,18},{16,24},{18,26},{24,28},{26,30},{28,20... | collective-permute-start | bytes 393224 | tf_op jit(solution)/shard_map/ppermute | solution.py:179
  46.0 3.0 %shard_map.112 = (f32[2,1024,128]{2,1,0:T(8,128)S(1)}, f32[2,1024,128]{2,1,0:T(8,128)S(1)}) custom-call(s32[4]{0:T(128)S(1)} %pad_add_fusion.10.refs_0_, s32[2]{0:T(128)S(1)} %pad_add_fusion.6.refs_1_, s32[16,128]{1,0:T(8,128)S(1)} %bitcast.42, s32[16,56,256]{2,1,0:T(8,128)S(1)} %pad_add_fusion.refs_3_, ...), custom_call_target="tpu_custom_call", output_to_operand_aliasing={{0}: (8, {}), {1}: (9, {})} | custom-call | flops 5000000000 | bytes 1048576 | tf_op jit(solution)/shard_map/pallas_call | solution.py:135
  49.0 1.9 %shard_map.114 = (f32[1024,128]{1,0:T(8,128)S(1)}, f32[1024,128]{1,0:T(8,128)S(1)}) custom-call(s32[2]{0:T(128)S(1)} %pad_add_fusion.5.refs_0_, s32[2]{0:T(128)S(1)} %pad_add_fusion.6.refs_1_, s32[16,128]{1,0:T(8,128)S(1)} %bitcast.43, s32[16,56,256]{2,1,0:T(8,128)S(1)} %pad_add_fusion.refs_3_, f32[256,128]{1,0:T(8,128)S(1)} %collective-permute-done.18.refs_4_, ...), custom_call_target="tpu_custom_call" | custom-call | flops 2000000000 | bytes 1048576 | tf_op jit(solution)/shard_map/pallas_call | solution.py:135
  51.0 1.9 %shard_map.113 = (f32[1024,128]{1,0:T(8,128)S(1)}, f32[1024,128]{1,0:T(8,128)S(1)}) custom-call(s32[2]{0:T(128)S(1)} %pad_add_fusion.5.refs_0_, s32[2]{0:T(128)S(1)} %pad_add_fusion.6.refs_1_, s32[16,128]{1,0:T(8,128)S(1)} %bitcast.44, s32[16,56,256]{2,1,0:T(8,128)S(1)} %pad_add_fusion.refs_3_, f32[256,128]{1,0:T(8,128)S(1)} %collective-permute-done.12.refs_4_, ...), custom_call_target="tpu_custom_call" | custom-call | flops 2000000000 | bytes 1048576 | tf_op jit(solution)/shard_map/pallas_call | solution.py:135
  53.0 0.5 collective-permute-start.16
  53.6 2.2 %collective-permute-start.21 = (f32[512,128]{1,0:T(8,128)S(1)}, f32[512,128]{1,0:T(8,128)S(1)}, u32[]{:S(2)}, u32[]{:S(2)}) collective-permute-start(f32[512,128]{1,0:T(8,128)S(1)} %slice_add_fusion), channel_id=1, source_target_pairs={{0,1},{1,0},{2,3},{3,2},{4,5},{5,4},{6,7},{7,6},{8,9},{9,8},{10,11... | collective-permute-start | bytes 786440 | tf_op jit(solution)/shard_map/ppermute | solution.py:185
  55.8 1.5 %collective-permute-start.17 = (f32[512,128]{1,0:T(8,128)S(1)}, f32[512,128]{1,0:T(8,128)S(1)}, u32[]{:S(2)}, u32[]{:S(2)}) collective-permute-start(f32[512,128]{1,0:T(8,128)S(1)} %slice_add_fusion.2), channel_id=1, source_target_pairs={{0,1},{1,0},{2,3},{3,2},{4,5},{5,4},{6,7},{7,6},{8,9},{9,8},{10,11... | collective-permute-start | bytes 786440 | tf_op jit(solution)/shard_map/ppermute | solution.py:185
  57.4 0.6 convolution_add_fusion.1
  57.9 5.0 %collective-permute-done.21 = f32[512,128]{1,0:T(8,128)S(1)} collective-permute-done((f32[512,128]{1,0:T(8,128)S(1)}, f32[512,128]{1,0:T(8,128)S(1)}, u32[]{:S(2)}, u32[]{:S(2)}) %collective-permute-start.21) | collective-permute-done | bytes 262176 | tf_op jit(solution)/shard_map/ppermute | solution.py:185
  62.9 0.6 fusion.4
  63.5 4.4 %collective-permute-done.17 = f32[512,128]{1,0:T(8,128)S(1)} collective-permute-done((f32[512,128]{1,0:T(8,128)S(1)}, f32[512,128]{1,0:T(8,128)S(1)}, u32[]{:S(2)}, u32[]{:S(2)}) %collective-permute-start.17) | collective-permute-done | bytes 262176 | tf_op jit(solution)/shard_map/ppermute | solution.py:185
  67.9 1.4 %fusion.1 = f32[512,256]{1,0:T(8,128)} fusion(f32[512,256]{1,0:T(8,128)S(1)} %fusion.4, f32[512,256]{1,0:T(8,128)S(1)} %convolution_add_fusion.1, f32[512,128]{1,0:T(8,128)S(1)} %collective-permute-done.17, f32[1024,128]{1,0:T(8,128)S(1)} %collective-permute-done.16, f32[1024,128]{1,0:T(8,128)S(1)} %get-tuple-element.40, f32[256,256]{1,0:T(8,128)S(1)} %copy-done.2, ...), kind=kOutput, calls=%fused_computation.2 | convolution fusion | flops 201916416 | bytes 2492416 | tf_op jit(solution)/shard_map/dot_general | solution.py:262
  (77 shorter events, 3.8 us)
Async XLA Ops:
  0.0 57.3 %copy-start = (f32[256,256]{1,0:T(8,128)S(1)}, f32[256,256]{1,0:T(8,128)}, u32[]{:S(2)}) copy-start(f32[256,256]{1,0:T(8,128)} %param.13) | copy-start | bytes 786436
  1.9 5.2 %copy-start.3 = (s32[1,8,16,256]{3,2,1,0:T(8,128)S(1)}, s32[1,8,16,256]{3,2,1,0:T(8,128)}, u32[]{:S(2)}) copy-start(s32[1,8,16,256]{3,2,1,0:T(8,128)} %param.19) | copy-start | bytes 393220
  2.0 17.6 %collective-permute-start.2 = (f32[512,128]{1,0:T(8,128)S(1)}, f32[512,128]{1,0:T(8,128)S(1)}, u32[]{:S(2)}, u32[]{:S(2)}) collective-permute-start(f32[512,128]{1,0:T(8,128)S(1)} %get-tuple-element.45.refs_4_), channel_id=1, source_target_pairs={{0,8},{2,10},{8,16},{10,18},{16,24},{18,26},{24,28},{26,30},{28,20... | collective-permute-start | bytes 786440 | tf_op jit(solution)/shard_map/ppermute | solution.py:179
  5.0 16.4 %collective-permute-start.4 = (f32[512,128]{1,0:T(8,128)S(1)}, f32[512,128]{1,0:T(8,128)S(1)}, u32[]{:S(2)}, u32[]{:S(2)}) collective-permute-start(f32[512,128]{1,0:T(8,128)S(1)} %get-tuple-element.45.refs_4_), channel_id=1, source_target_pairs={{0,4},{2,6},{8,0},{10,2},{16,8},{18,10},{24,16},{26,18},{28,24},{3... | collective-permute-start | bytes 786440 | tf_op jit(solution)/shard_map/ppermute | solution.py:179
  5.0 2.1 %copy-start.9 = (s32[1,8]{1,0:T(1,128)S(1)}, s32[1,8]{1,0:T(1,128)}, u32[]{:S(2)}) copy-start(s32[1,8]{1,0:T(1,128)} %param.18) | copy-start | bytes 100
  5.1 3.0 %copy-start.4 = (s32[1,8,16,256]{3,2,1,0:T(8,128)S(1)}, s32[1,8,16,256]{3,2,1,0:T(8,128)}, u32[]{:S(2)}) copy-start(s32[1,8,16,256]{3,2,1,0:T(8,128)} %param.21) | copy-start | bytes 393220
  5.1 3.0 %copy-start.5 = (s32[1,8,16,256]{3,2,1,0:T(8,128)S(1)}, s32[1,8,16,256]{3,2,1,0:T(8,128)}, u32[]{:S(2)}) copy-start(s32[1,8,16,256]{3,2,1,0:T(8,128)} %param.20) | copy-start | bytes 393220
  5.1 11.8 %collective-permute-start.6 = (f32[512,128]{1,0:T(8,128)S(1)}, f32[512,128]{1,0:T(8,128)S(1)}, u32[]{:S(2)}, u32[]{:S(2)}) collective-permute-start(f32[512,128]{1,0:T(8,128)S(1)} %get-tuple-element.46.refs_5_), channel_id=1, source_target_pairs={{0,8},{2,10},{8,16},{10,18},{16,24},{18,26},{24,28},{26,30},{28,20... | collective-permute-start | bytes 786440 | tf_op jit(solution)/shard_map/ppermute | solution.py:179
  7.1 11.6 %collective-permute-start.7 = (f32[512,128]{1,0:T(8,128)S(1)}, f32[512,128]{1,0:T(8,128)S(1)}, u32[]{:S(2)}, u32[]{:S(2)}) collective-permute-start(f32[512,128]{1,0:T(8,128)S(1)} %get-tuple-element.46.refs_5_), channel_id=1, source_target_pairs={{0,4},{2,6},{8,0},{10,2},{16,8},{18,10},{24,16},{26,18},{28,24},{3... | collective-permute-start | bytes 786440 | tf_op jit(solution)/shard_map/ppermute | solution.py:179
  7.2 0.7 copy-start.6
  7.3 0.7 copy-start.7
  8.1 1.6 %collective-permute-start = (s32[4,56,256]{2,1,0:T(8,128)S(1)}, s32[4,56,256]{2,1,0:T(8,128)S(1)}, u32[]{:S(2)}, u32[]{:S(2)}) collective-permute-start(s32[4,56,256]{2,1,0:T(8,128)S(1)} %pad_add_fusion.2), channel_id=1, source_target_pairs={{0,2},{2,0},{4,6},{6,4},{8,10},{10,8},{12,14},{14,12},{16,18},{18,... | collective-permute-start | bytes 688136 | tf_op jit(solution)/shard_map/ppermute | solution.py:182
  10.5 17.7 %collective-permute-start.1 = (s32[8,56,256]{2,1,0:T(8,128)}, s32[8,56,256]{2,1,0:T(8,128)S(1)}, u32[]{:S(2)}, u32[]{:S(2)}) collective-permute-start(s32[8,56,256]{2,1,0:T(8,128)} %pad_add_fusion.1), channel_id=1, source_target_pairs={{0,1},{1,0},{2,3},{3,2},{4,5},{5,4},{6,7},{7,6},{8,9},{9,8},{10,11... | collective-permute-start | bytes 1376264 | tf_op jit(solution)/shard_map/ppermute | solution.py:185
  16.9 9.2 %collective-permute-start.10 = (f32[512,128]{1,0:T(8,128)S(1)}, f32[512,128]{1,0:T(8,128)S(1)}, u32[]{:S(2)}, u32[]{:S(2)}) collective-permute-start(f32[512,128]{1,0:T(8,128)S(1)} %collective-permute-done.6.refs_5_), channel_id=1, source_target_pairs={{0,8},{2,10},{8,16},{10,18},{16,24},{18,26},{24,28},{26,30},{28,20... | collective-permute-start | bytes 786440 | tf_op jit(solution)/shard_map/ppermute | solution.py:179
  18.7 9.2 %collective-permute-start.11 = (f32[512,128]{1,0:T(8,128)S(1)}, f32[512,128]{1,0:T(8,128)S(1)}, u32[]{:S(2)}, u32[]{:S(2)}) collective-permute-start(f32[512,128]{1,0:T(8,128)S(1)} %collective-permute-done.7.refs_7_), channel_id=1, source_target_pairs={{0,4},{2,6},{8,0},{10,2},{16,8},{18,10},{24,16},{26,18},{28,24},{3... | collective-permute-start | bytes 786440 | tf_op jit(solution)/shard_map/ppermute | solution.py:179
  19.6 14.4 %collective-permute-start.3 = (f32[512,128]{1,0:T(8,128)S(1)}, f32[512,128]{1,0:T(8,128)S(1)}, u32[]{:S(2)}, u32[]{:S(2)}) collective-permute-start(f32[512,128]{1,0:T(8,128)S(1)} %collective-permute-done.2.refs_4_), channel_id=1, source_target_pairs={{0,8},{2,10},{8,16},{10,18},{16,24},{18,26},{24,28},{26,30},{28,20... | collective-permute-start | bytes 786440 | tf_op jit(solution)/shard_map/ppermute | solution.py:179
  21.4 12.6 %collective-permute-start.5 = (f32[512,128]{1,0:T(8,128)S(1)}, f32[512,128]{1,0:T(8,128)S(1)}, u32[]{:S(2)}, u32[]{:S(2)}) collective-permute-start(f32[512,128]{1,0:T(8,128)S(1)} %collective-permute-done.4.refs_6_), channel_id=1, source_target_pairs={{0,4},{2,6},{8,0},{10,2},{16,8},{18,10},{24,16},{26,18},{28,24},{3... | collective-permute-start | bytes 786440 | tf_op jit(solution)/shard_map/ppermute | solution.py:179
  26.1 13.0 %collective-permute-start.14 = (f32[512,128]{1,0:T(8,128)S(1)}, f32[512,128]{1,0:T(8,128)S(1)}, u32[]{:S(2)}, u32[]{:S(2)}) collective-permute-start(f32[512,128]{1,0:T(8,128)S(1)} %collective-permute-done.10.refs_5_), channel_id=1, source_target_pairs={{0,8},{2,10},{8,16},{10,18},{16,24},{18,26},{24,28},{26,30},{28,20... | collective-permute-start | bytes 786440 | tf_op jit(solution)/shard_map/ppermute | solution.py:179
  28.0 12.5 %collective-permute-start.15 = (f32[512,128]{1,0:T(8,128)S(1)}, f32[512,128]{1,0:T(8,128)S(1)}, u32[]{:S(2)}, u32[]{:S(2)}) collective-permute-start(f32[512,128]{1,0:T(8,128)S(1)} %collective-permute-done.11.refs_7_), channel_id=1, source_target_pairs={{0,4},{2,6},{8,0},{10,2},{16,8},{18,10},{24,16},{26,18},{28,24},{3... | collective-permute-start | bytes 786440 | tf_op jit(solution)/shard_map/ppermute | solution.py:179
  34.1 8.6 %collective-permute-start.8 = (f32[512,128]{1,0:T(8,128)S(1)}, f32[512,128]{1,0:T(8,128)S(1)}, u32[]{:S(2)}, u32[]{:S(2)}) collective-permute-start(f32[512,128]{1,0:T(8,128)S(1)} %collective-permute-done.3.refs_4_), channel_id=1, source_target_pairs={{0,8},{2,10},{8,16},{10,18},{16,24},{18,26},{24,28},{26,30},{28,20... | collective-permute-start | bytes 786440 | tf_op jit(solution)/shard_map/ppermute | solution.py:179
  35.3 8.5 %collective-permute-start.9 = (f32[512,128]{1,0:T(8,128)S(1)}, f32[512,128]{1,0:T(8,128)S(1)}, u32[]{:S(2)}, u32[]{:S(2)}) collective-permute-start(f32[512,128]{1,0:T(8,128)S(1)} %collective-permute-done.5.refs_6_), channel_id=1, source_target_pairs={{0,4},{2,6},{8,0},{10,2},{16,8},{18,10},{24,16},{26,18},{28,24},{3... | collective-permute-start | bytes 786440 | tf_op jit(solution)/shard_map/ppermute | solution.py:179
  39.1 9.9 %collective-permute-start.18 = (f32[256,128]{1,0:T(8,128)S(1)}, f32[256,128]{1,0:T(8,128)S(1)}, u32[]{:S(2)}, u32[]{:S(2)}) collective-permute-start(f32[256,128]{1,0:T(8,128)S(1)} %slice.121), channel_id=1, source_target_pairs={{0,8},{2,10},{8,16},{10,18},{16,24},{18,26},{24,28},{26,30},{28,20... | collective-permute-start | bytes 393224 | tf_op jit(solution)/shard_map/ppermute | solution.py:179
  40.4 8.6 %collective-permute-start.19 = (f32[256,128]{1,0:T(8,128)S(1)}, f32[256,128]{1,0:T(8,128)S(1)}, u32[]{:S(2)}, u32[]{:S(2)}) collective-permute-start(f32[256,128]{1,0:T(8,128)S(1)} %slice.122), channel_id=1, source_target_pairs={{0,4},{2,6},{8,0},{10,2},{16,8},{18,10},{24,16},{26,18},{28,24},{3... | collective-permute-start | bytes 393224 | tf_op jit(solution)/shard_map/ppermute | solution.py:179
  43.9 7.2 %collective-permute-start.12 = (f32[256,128]{1,0:T(8,128)S(1)}, f32[256,128]{1,0:T(8,128)S(1)}, u32[]{:S(2)}, u32[]{:S(2)}) collective-permute-start(f32[256,128]{1,0:T(8,128)S(1)} %slice.102), channel_id=1, source_target_pairs={{0,8},{2,10},{8,16},{10,18},{16,24},{18,26},{24,28},{26,30},{28,20... | collective-permute-start | bytes 393224 | tf_op jit(solution)/shard_map/ppermute | solution.py:179
  45.5 5.5 %collective-permute-start.13 = (f32[256,128]{1,0:T(8,128)S(1)}, f32[256,128]{1,0:T(8,128)S(1)}, u32[]{:S(2)}, u32[]{:S(2)}) collective-permute-start(f32[256,128]{1,0:T(8,128)S(1)} %slice.103), channel_id=1, source_target_pairs={{0,4},{2,6},{8,0},{10,2},{16,8},{18,10},{24,16},{26,18},{28,24},{3... | collective-permute-start | bytes 393224 | tf_op jit(solution)/shard_map/ppermute | solution.py:179
  50.9 2.6 %collective-permute-start.20 = (f32[1024,128]{1,0:T(8,128)S(1)}, f32[1024,128]{1,0:T(8,128)S(1)}, u32[]{:S(2)}, u32[]{:S(2)}) collective-permute-start(f32[1024,128]{1,0:T(8,128)S(1)} %get-tuple-element.44), channel_id=1, source_target_pairs={{0,2},{2,0},{4,6},{6,4},{8,10},{10,8},{12,14},{14,12},{16,18},{18,... | collective-permute-start | bytes 1572872 | tf_op jit(solution)/shard_map/ppermute | solution.py:182
  53.0 2.8 %collective-permute-start.16 = (f32[1024,128]{1,0:T(8,128)S(1)}, f32[1024,128]{1,0:T(8,128)S(1)}, u32[]{:S(2)}, u32[]{:S(2)}) collective-permute-start(f32[1024,128]{1,0:T(8,128)S(1)} %get-tuple-element.41), channel_id=1, source_target_pairs={{0,2},{2,0},{4,6},{6,4},{8,10},{10,8},{12,14},{14,12},{16,18},{18,... | collective-permute-start | bytes 1572872 | tf_op jit(solution)/shard_map/ppermute | solution.py:182
  53.6 3.8 %copy-start.1 = (f32[512,256]{1,0:T(8,128)S(1)}, f32[512,256]{1,0:T(8,128)}, u32[]{:S(2)}) copy-start(f32[512,256]{1,0:T(8,128)} %param.11) | copy-start | bytes 1572868
  53.6 9.3 %collective-permute-start.21 = (f32[512,128]{1,0:T(8,128)S(1)}, f32[512,128]{1,0:T(8,128)S(1)}, u32[]{:S(2)}, u32[]{:S(2)}) collective-permute-start(f32[512,128]{1,0:T(8,128)S(1)} %slice_add_fusion), channel_id=1, source_target_pairs={{0,1},{1,0},{2,3},{3,2},{4,5},{5,4},{6,7},{7,6},{8,9},{9,8},{10,11... | collective-permute-start | bytes 786440 | tf_op jit(solution)/shard_map/ppermute | solution.py:185
  55.8 1.6 %copy-start.8 = (f32[256]{0:T(256)S(1)}, f32[256]{0:T(256)}, u32[]{:S(2)}) copy-start(f32[256]{0:T(256)} %param.15) | copy-start | bytes 3076
  55.8 7.1 %copy-start.2 = (f32[256,256]{1,0:T(8,128)S(1)}, f32[256,256]{1,0:T(8,128)}, u32[]{:S(2)}) copy-start(f32[256,256]{1,0:T(8,128)} %param.14) | copy-start | bytes 786436
  55.8 12.1 %collective-permute-start.17 = (f32[512,128]{1,0:T(8,128)S(1)}, f32[512,128]{1,0:T(8,128)S(1)}, u32[]{:S(2)}, u32[]{:S(2)}) collective-permute-start(f32[512,128]{1,0:T(8,128)S(1)} %slice_add_fusion.2), channel_id=1, source_target_pairs={{0,1},{1,0},{2,3},{3,2},{4,5},{5,4},{6,7},{7,6},{8,9},{9,8},{10,11... | collective-permute-start | bytes 786440 | tf_op jit(solution)/shard_map/ppermute | solution.py:185

commit v6 on v5

--- a/solution.py
+++ b/solution.py
@@ -2,6 +2,7 @@
 
 import jax
 import jax.numpy as jnp
+import numpy as np
 from jax import lax
 from jax.experimental import pallas as pl
 from jax.experimental.pallas import tpu as pltpu
@@ -17,6 +18,33 @@
     high = value.astype(jnp.bfloat16)
     low = (value - high.astype(jnp.float32)).astype(jnp.bfloat16)
     return high, low
+
+
+def scale_kernel(degrees, features, *outs):
+    factor = lax.rsqrt(degrees[...].astype(jnp.float32))
+    for tile in range(degrees.shape[0]):
+        rows = slice(tile * TILE, (tile + 1) * TILE)
+        column = jnp.transpose(jnp.broadcast_to(factor[tile : tile + 1, :], (TILE, TILE)))
+        outs[0][rows, :] = features[rows, :] * column
+        if len(outs) > 1:
+            outs[1][rows, :] = column
+
+
+def scaled_chunk(degrees, features, chunk, wide=False):
+    rows = features.shape[0]
+    tiles = rows // TILE
+    outs = 2 if wide else 1
+    return pl.pallas_call(
+        scale_kernel,
+        grid=(1,),
+        in_specs=[
+            pl.BlockSpec((tiles, TILE), lambda step: (0, 0)),
+            pl.BlockSpec((rows, TILE), lambda step: (0, chunk)),
+        ],
+        out_specs=[pl.BlockSpec((rows, TILE), lambda step: (0, 0))] * outs,
+        out_shape=[pltpu.VMEM((rows, TILE), jnp.float32)] * outs,
+        cost_estimate=pl.CostEstimate(flops=3_000_000_000, bytes_accessed=1 << 20, transcendentals=0),
+    )(degrees.reshape(tiles, TILE), features)
 
 
 def tile_matrix(edges, pair, slot, slots, live):
@@ -33,9 +61,9 @@
     return jnp.concatenate(bf16_pair(matrix), axis=1)
 
 
-def sum_kernel(sources, chunks, pieces, slots, first, last, *refs):
-    pairs, place, meta, edges = refs[:4]
-    refs = refs[4:]
+def sum_kernel(base, sources, chunks, pieces, slots, first, last, *refs):
+    numbers, meta, edges = refs[:3]
+    refs = refs[3:]
     count = sources * chunks * pieces
     parts, refs = refs[:count], refs[count:]
     if not first:
@@ -56,11 +84,12 @@
 
     used = jnp.int32(0)
     for number in range(2 * sources):
-        pair = pairs[number]
+        pair = jnp.maximum(numbers[base + number], 0)
+        listed = numbers[base + number] >= 0
         for slot in range(slots):
-            column = meta[pair, slots + slot] - place[0]
-            row = (meta[pair, slot] + place[1]) & (tiles_per - 1)
-            wanted = (slot < meta[pair, 2 * slots]) & (column >= 0) & (column < tiles_here)
+            column = meta[pair, slots + slot] - numbers[0]
+            row = (meta[pair, slot] + numbers[1]) & (tiles_per - 1)
+            wanted = listed & (slot < meta[pair, 2 * slots]) & (column >= 0) & (column < tiles_here)
             code = ((number * slots + slot) * tiles_here + column) * tiles_per + row
             entries[used] = jnp.where(wanted, code, 0)
             used = used + wanted.astype(jnp.int32)
@@ -92,7 +121,8 @@
             code = lax.div(code, tiles_here)
             slot = lax.rem(code, slots)
             number = lax.div(code, slots)
-            matrix = tile_matrix(edges, pairs[number], slot, slots, entry < used)
+            pair = jnp.maximum(numbers[base + number], 0)
+            matrix = tile_matrix(edges, pair, slot, slots, entry < used)
             todo.append((matrix, number, column, row))
         results = [
             jnp.dot(matrix, sides[lax.div(number, 2), column], preferred_element_type=jnp.float32)
@@ -112,7 +142,7 @@
                 outs[2 * chunk + block][...] = sums[chunk][block]
 
 
-def add_sources(pairs, place, meta, edges, parts, before, rows, slots, last=False):
+def add_sources(base, numbers, meta, edges, parts, before, rows, slots, last=False):
     sources, chunks, pieces = len(parts), len(parts[0]), len(parts[0][0])
     flat = [piece for source in parts for chunk in source for piece in chunk]
     here, width = pieces * flat[0].shape[0], flat[0].shape[1]
@@ -130,18 +160,18 @@
         scratch += [pltpu.VMEM(whole.shape, jnp.float32)] * chunks
     elif not first:
         olds = [pltpu.with_memory_space_constraint(old, pltpu.VMEM) for old in olds]
-        aliases = {4 + len(flat) + chunk: chunk for chunk in range(chunks)}
-    flops = 1_000_000_000 * (1 + sources * chunks)
+        aliases = {3 + len(flat) + chunk: chunk for chunk in range(chunks)}
+    flops = 1_000_000_000 * (2 if last else 1) * (1 + sources * chunks)
     return pl.pallas_call(
-        functools.partial(sum_kernel, sources, chunks, pieces, slots, first, last),
-        in_specs=[SMEM] * 3 + [VMEM] * (1 + len(flat) + len(olds)),
+        functools.partial(sum_kernel, base, sources, chunks, pieces, slots, first, last),
+        in_specs=[SMEM] * 2 + [VMEM] * (1 + len(flat) + len(olds)),
         out_specs=[VMEM] * len(outs),
         out_shape=outs,
         scratch_shapes=scratch,
         input_output_aliases=aliases,
         compiler_params=pltpu.CompilerParams(vmem_limit_bytes=24 << 20),
         cost_estimate=pl.CostEstimate(flops=flops, bytes_accessed=1 << 20, transcendentals=0),
-    )(pairs, place, meta, edges, *flat, *olds)
+    )(numbers, meta, edges, *flat, *olds)
 
 
 def on_device(
@@ -157,7 +187,7 @@
     edge_col,
     edge_weight,
 ):
-    highest = lax.Precision.HIGHEST
+    highest, final = lax.Precision.HIGHEST, lax.Precision.HIGH
     groups, blocks = lax.axis_size("rep"), lax.axis_size("blk")
     lanes = blocks // 2
     layers = lanes // 2
@@ -167,7 +197,6 @@
     rows = shard * groups
     chunks = width // TILE
     block, replica = lax.axis_index("blk"), lax.axis_index("rep")
-    chip, core = block // 2, block % 2
 
     def chip_at(position):
         return 2 * position if position < layers else 2 * (lanes - 1 - position) + 1
@@ -184,9 +213,13 @@
     def rep_swap(value):
         return lax.ppermute(value, "rep", [(0, 1), (1, 0)])
 
-    scale = lax.rsqrt(degrees.astype(jnp.float32))
-    scaled = features * scale[:, None]
-    own = [scaled[:, f * TILE : (f + 1) * TILE] for f in range(chunks)]
+    (leading,) = scaled_chunk(degrees, features, chunks - 1)
+    others, leading, edge_row, edge_col, edge_weight = lax.optimization_barrier(
+        (features, leading, edge_row, edge_col, edge_weight)
+    )
+    own = [scaled_chunk(degrees, others, f, wide=f == 0) for f in range(chunks - 1)]
+    wide = own[0][1]
+    own = [pair[0] for pair in own] + [leading]
 
     def bundle(start):
         lists = [array[0, start::2] for array in (edge_row, edge_col, edge_weight)]
@@ -202,64 +235,82 @@
         edges = jnp.concatenate([lists, rep_swap(lists)], axis=0)
     else:
         edges = lax.all_gather(lists, "rep", axis=0, tiled=True)
-    meta = edges[:, 3 * slots, :TILE]
-
-    def list_place(offset, which):
-        group = offset // per
-        group = group ^ replica if groups == 2 else group
-        return (2 * group + which) * per + offset % per
-
-    position = jnp.where(chip % 2 == 0, chip // 2, lanes - 1 - chip // 2)
-
-    def pairs_of(distances):
+    meta, near_meta = edges[:, 3 * slots, :TILE], lists[:, 3 * slots, :TILE]
+
+    tiles_per = rows // TILE
+    tiles_here = shard // TILE
+    halfway = lanes // 2
+
+    def places_of(chip, core, replica, distances, near=True, far=True):
         places = []
         for distance in distances:
-            there = (position + distance + lanes) % lanes
-            source = jnp.where(there < layers, 2 * there, 2 * (lanes - 1 - there) + 1)
-            places.append(list_place((chip - source + lanes) % lanes, 0))
-            places.append(list_place((chip - source - core + lanes) % lanes, 1))
-        return jnp.stack(places).astype(jnp.int32)
-
-    tiles_per = rows // TILE
-    tiles_here = shard // TILE
-    rotation = (tiles_per - replica * tiles_here) if groups == 2 else 0 * replica
-    place = jnp.stack([replica * tiles_here, rotation]).astype(jnp.int32)
+            at = chip // 2 if chip % 2 == 0 else lanes - 1 - chip // 2
+            source = chip_at((at + distance) % lanes)
+            for which, offset in enumerate(((chip - source) % lanes, (chip - source - core) % lanes)):
+                group = offset // per
+                if near and not far:
+                    places.append(which * per + offset % per if group == replica else -1)
+                elif far and not near and group == replica:
+                    places.append(-1)
+                else:
+                    order = group ^ replica if groups == 2 else group
+                    places.append((2 * order + which) * per + offset % per)
+        return places
+
+    def numbers_of(chip, core, replica):
+        rotation = tiles_per - replica * tiles_here if groups == 2 else 0
+        parts = [[replica * tiles_here, rotation]]
+        parts.append(places_of(chip, core, replica, [0, -1, 1], far=False))
+        parts.append(places_of(chip, core, replica, [0, -1, 1], near=False))
+        for step in range(2, halfway):
+            parts.append(places_of(chip, core, replica, [-step, step]))
+        return sum(parts + [places_of(chip, core, replica, [halfway])], [])
+
+    table = np.array(
+        [numbers_of(b // 2, b % 2, r) for b in range(blocks) for r in range(groups)], dtype=np.int32
+    )
+    def base_of(step):
+        return 14 + 4 * (step - 2)
+
     add = functools.partial(add_sources, rows=rows, slots=slots)
 
     root = jnp.dot(features, root_weight, precision=highest) + bias
 
     half = shard // 2
-    half = shard // 2
-    hops = [(own, own)]
-    totals = None
-    for step in range(1, lanes // 2):
+    later = [lax.optimization_barrier((v, lists))[0] for v in own[:-1]] + own[-1:]
+    hops = [(later, later)]
+    for step in range(1, halfway):
         up, down = hops[-1]
-        if totals is not None:
+        if step >= 3:
             up, down = list(up), list(down)
             up[0], down[0], totals = lax.optimization_barrier((up[0], down[0], totals))
         hops.append(([ring(v, 1) for v in up], [ring(v, -1) for v in down]))
-        if step == 2:
-            totals = add(pairs_of([0]), place, meta, edges, [[[v] for v in own]], None)
-        if step >= 2:
-            parts = [[[v] for v in side] for side in hops[step - 1]]
-            totals = add(pairs_of([1 - step, step - 1]), place, meta, edges, parts, totals)
+        parts = [[[v] for v in side] for side in hops[step - 1]]
+        if step == 1:
+            early = parts[:1]
+            index, _ = lax.optimization_barrier((block * groups + replica, hops[-1][0][0]))
+            numbers = lax.dynamic_index_in_dim(jnp.asarray(table), index, keepdims=False)
+        elif step == 2:
+            early = early + parts
+            totals = add(2, numbers, near_meta, lists, early, None)
+            totals = add(8, numbers, meta, edges, early, totals)
+        else:
+            totals = add(base_of(step - 1), numbers, meta, edges, parts, totals)
     up, down = [list(side) for side in hops[-1]]
     up[0], down[0], totals = lax.optimization_barrier((up[0], down[0], totals))
     ends = [[ring(up[f][:half], 1), ring(down[f][half:], -1)] for f in range(chunks)]
-    step = lanes // 2 - 1
-    totals = add(pairs_of([-step, step]), place, meta, edges, [[[v] for v in up], [[v] for v in down]], totals)
-    pairs = pairs_of([lanes // 2])
+    totals = add(base_of(halfway - 1), numbers, meta, edges, [[[v] for v in up], [[v] for v in down]], totals)
     hidden = root
     for f in range(chunks):
-        own_sum, sibling_sum = add(pairs, place, meta, edges, [[ends[f]]], [totals[f]], last=True)
+        own_sum, sibling_sum = add(base_of(halfway), numbers, meta, edges, [[ends[f]]], [totals[f]], last=True)
         swapped = core_swap(sibling_sum)
         if groups == 2:
             other = rep_swap(own_sum[shard:] + swapped[shard:])
             share = own_sum[:shard] + swapped[:shard] + other
         else:
             share = lax.psum_scatter(own_sum + swapped, "rep", scatter_dimension=0, tiled=True)
-        mixed = share * scale[:, None]
-        hidden = hidden + jnp.dot(mixed, neighbor_weight[f * TILE : (f + 1) * TILE], precision=highest)
+        mixed = share * wide
+        hidden = hidden + jnp.dot(mixed, neighbor_weight[f * TILE : (f + 1) * TILE], precision=final)
     return jax.nn.relu(hidden)
 
 

time: 70.1 us -> 66.8 us (0.953)
  waiting for transfers between devices: 20.7 us -> 17 us
  Pallas kernels: 15.6 us -> 19 us
  other arithmetic: 3.46 us -> 1.38 us
  between operations: 1.28 us -> 0.33 us
    ppermute x16, waiting for transfers between devices: 10.9 us -> 6.21 us  [ring(): return lax.ppermute(value, 'blk', pairs)]
    pallas_call x6 -> x8, Pallas kernels: 15.6 us -> 19 us  [the longest x6 16.8 us: add_sources(): pl.pallas_call(functools.partial(sum_kernel, base, sources, chunks, piece...]
    ppermute x3, starting transfers between devices: 5.62 us -> 4.12 us  [rep_swap(): return lax.ppermute(value, 'rep', [(0, 1), (1, 0)])]
    ppermute x3, waiting for transfers between devices: 9.35 us -> 10.7 us  [rep_swap(): return lax.ppermute(value, 'rep', [(0, 1), (1, 0)])]
    mul x1 -> x0, other arithmetic: 1.17 us -> none  [on_device(): scaled = features * scale[:, None]]
    ppermute x16, starting transfers between devices: 18.2 us -> 19.2 us  [ring(): return lax.ppermute(value, 'blk', pairs)]
    concatenate x1, other arithmetic: 0.07 us -> 1.09 us  [on_device(): edges = jnp.concatenate([lists, rep_swap(lists)], axis=0)]
    concatenate x1, other arithmetic: 0.81 us -> 0.05 us  [on_device(): lists = jnp.concatenate([bundle(0), core_swap(bundle(1))], axis=0)]
  transfers between devices with their start and end apart: 22 -> 22, of which waited for: 7 -> 6; matrix products, arithmetic and copies ran while one was open for 5% -> 5% of each run, Pallas kernels for 22% -> 27%
where the time goes in v6:
time: 66.8 us; the launch traced here: 66.2 us
  starting transfers between devices  24.5 us (37%)
  Pallas kernels  19 us (28%)
  waiting for transfers between devices  17 us (25%)
  matrix products  2.11 us (3%)
  local copies, waits for them, and re-layouts  1.89 us (3%)
  other arithmetic  1.38 us (2%)
    ppermute x16, starting transfers between devices, ring(): return lax.ppermute(value, 'blk', pairs)  19.2 us
    pallas_call x6, Pallas kernels, add_sources(): pl.pallas_call(functools.partial(sum_kernel, base, sources, chunks, piece...  16.8 us
    ppermute x3, waiting for transfers between devices, rep_swap(): return lax.ppermute(value, 'rep', [(0, 1), (1, 0)])  10.7 us
    ppermute x16, waiting for transfers between devices, ring(): return lax.ppermute(value, 'blk', pairs)  6.21 us
    ppermute x3, starting transfers between devices, rep_swap(): return lax.ppermute(value, 'rep', [(0, 1), (1, 0)])  4.12 us
    pallas_call x2, Pallas kernels, scaled_chunk(): pl.pallas_call(scale_kernel, grid=(1,), in_specs=[pl.BlockSpec((tiles, TI...  2.27 us
    dot_general x2, matrix products, on_device(): jnp.dot(mixed, neighbor_weight[f * TILE:(f + 1) * TILE], precision=final)  1.53 us
  transfers between devices with their start and end apart: 22, of which 6 were waited for; matrix products, arithmetic and copies ran while one was open for 5% of the time, Pallas kernels for 27%

profile of v6, /device:TPU:0, one launch (start us, length us, event | category | flops | bytes accessed | tf_op | source)
XLA Modules:
  0.0 66.2 jit_solution(10977650782502789637)
XLA Ops:
  0.0 1.2 %shard_map.118.refs_4_ = f32[512,128]{1,0:T(8,128)S(1)} custom-call(s32[4,128]{1,0:T(4,128)} %bitcast.37, f32[512,256]{1,0:T(8,128)} %features.2), custom_call_target="tpu_custom_call" | custom-call | flops 3000000000 | bytes 1048576 | tf_op jit(solution)/shard_map/pallas_call | solution.py:37
  1.2 3.1 %collective-permute-start.6 = (f32[512,128]{1,0:T(8,128)S(1)}, f32[512,128]{1,0:T(8,128)S(1)}, u32[]{:S(2)}, u32[]{:S(2)}) collective-permute-start(f32[512,128]{1,0:T(8,128)S(1)} %shard_map.118.refs_4_), channel_id=1, source_target_pairs={{0,8},{2,10},{8,16},{10,18},{16,24},{18,26},{24,28},{26,30},{28,20... | collective-permute-start | bytes 786440 | tf_op jit(solution)/shard_map/ppermute | solution.py:208
  5.7 1.1 %shard_map.119 = (f32[512,128]{1,0:T(8,128)S(1)}, f32[512,128]{1,0:T(8,128)S(1)}) custom-call(s32[4,128]{1,0:T(4,128)} %bitcast.38, f32[512,256]{1,0:T(8,128)} %features.2), custom_call_target="tpu_custom_call" | custom-call | flops 3000000000 | bytes 1048576 | tf_op jit(solution)/shard_map/pallas_call | solution.py:37
  6.9 2.1 %collective-permute-start.1 = (f32[512,128]{1,0:T(8,128)S(1)}, f32[512,128]{1,0:T(8,128)S(1)}, u32[]{:S(2)}, u32[]{:S(2)}) collective-permute-start(f32[512,128]{1,0:T(8,128)S(1)} %get-tuple-element.39.refs_3_), channel_id=1, source_target_pairs={{0,8},{2,10},{8,16},{10,18},{16,24},{18,26},{24,28},{26,30},{28,20... | collective-permute-start | bytes 786440 | tf_op jit(solution)/shard_map/ppermute | solution.py:208
  9.0 2.0 %collective-permute-start.2 = (s32[8,56,256]{2,1,0:T(8,128)S(1)}, s32[8,56,256]{2,1,0:T(8,128)}, u32[]{:S(2)}, u32[]{:S(2)}) collective-permute-start(s32[8,56,256]{2,1,0:T(8,128)S(1)} %pad_add_fusion.1.refs_2_), channel_id=1, source_target_pairs={{0,1},{1,0},{2,3},{3,2},{4,5},{5,4},{6,7},{7,6},{8,9},{9,8},{10,11... | collective-permute-start | bytes 1376264 | tf_op jit(solution)/shard_map/ppermute | solution.py:214
  10.9 1.6 %collective-permute-start.10 = (f32[512,128]{1,0:T(8,128)S(1)}, f32[512,128]{1,0:T(8,128)S(1)}, u32[]{:S(2)}, u32[]{:S(2)}) collective-permute-start(f32[512,128]{1,0:T(8,128)S(1)} %collective-permute-done.6.refs_6_), channel_id=1, source_target_pairs={{0,8},{2,10},{8,16},{10,18},{16,24},{18,26},{24,28},{26,30},{28,20... | collective-permute-start | bytes 786440 | tf_op jit(solution)/shard_map/ppermute | solution.py:208
  13.0 3.3 %collective-permute-done.1.refs_5_ = f32[512,128]{1,0:T(8,128)S(1)} collective-permute-done((f32[512,128]{1,0:T(8,128)S(1)}, f32[512,128]{1,0:T(8,128)S(1)}, u32[]{:S(2)}, u32[]{:S(2)}) %collective-permute-start.1) | collective-permute-done | bytes 262176 | tf_op jit(solution)/shard_map/ppermute | solution.py:208
  16.3 1.9 %collective-permute-start.3 = (f32[512,128]{1,0:T(8,128)S(1)}, f32[512,128]{1,0:T(8,128)S(1)}, u32[]{:S(2)}, u32[]{:S(2)}) collective-permute-start(f32[512,128]{1,0:T(8,128)S(1)} %collective-permute-done.1.refs_5_), channel_id=1, source_target_pairs={{0,8},{2,10},{8,16},{10,18},{16,24},{18,26},{24,28},{26,30},{28,20... | collective-permute-start | bytes 786440 | tf_op jit(solution)/shard_map/ppermute | solution.py:208
  18.2 0.7 %dynamic-slice_bitcast_fusion.refs_0_ = s32[24]{0:T(128)S(1)} fusion(s32[32,24]{1,0:T(8,128)} %constant.22.clone, s32[]{:T(128)S(6)} %select_n.4), kind=kLoop, calls=%fused_computation.28 | loop fusion | bytes 196 | tf_op jit(solution)/shard_map/jit(dynamic_index_in_dim)/squeeze | solution.py:292
  19.0 2.0 %shard_map.120 = (f32[2,1024,128]{2,1,0:T(8,128)S(1)}, f32[2,1024,128]{2,1,0:T(8,128)S(1)}) custom-call(s32[24]{0:T(128)S(1)} %dynamic-slice_bitcast_fusion.refs_0_, s32[8,128]{1,0:T(8,128)S(1)} %bitcast.30, s32[8,56,256]{2,1,0:T(8,128)S(1)} %pad_add_fusion.1.refs_2_, f32[512,128]{1,0:T(8,128)S(1)} %get-tuple-element.39.refs_3_, ...), custom_call_target="tpu_custom_call" | custom-call | flops 7000000000 | bytes 1048576 | tf_op jit(solution)/shard_map/pallas_call | solution.py:165
  21.0 0.9 %collective-permute-done.10.refs_4_ = f32[512,128]{1,0:T(8,128)S(1)} collective-permute-done((f32[512,128]{1,0:T(8,128)S(1)}, f32[512,128]{1,0:T(8,128)S(1)}, u32[]{:S(2)}, u32[]{:S(2)}) %collective-permute-start.10) | collective-permute-done | bytes 262176 | tf_op jit(solution)/shard_map/ppermute | solution.py:208
  21.9 3.7 %collective-permute-start.14 = (f32[512,128]{1,0:T(8,128)S(1)}, f32[512,128]{1,0:T(8,128)S(1)}, u32[]{:S(2)}, u32[]{:S(2)}) collective-permute-start(f32[512,128]{1,0:T(8,128)S(1)} %collective-permute-done.10.refs_4_), channel_id=1, source_target_pairs={{0,8},{2,10},{8,16},{10,18},{16,24},{18,26},{24,28},{26,30},{28,20... | collective-permute-start | bytes 786440 | tf_op jit(solution)/shard_map/ppermute | solution.py:208
  25.6 1.1 %pad_add_fusion.refs_2_ = s32[16,56,256]{2,1,0:T(8,128)S(1)} fusion(s32[8,56,256]{2,1,0:T(8,128)} %collective-permute-done.2, s32[4,56,256]{2,1,0:T(8,128)S(1)} %collective-permute-done, s32[4,8,256]{2,1,0:T(8,128)S(1)} %copy-done.3, s32[4,16,256]{2,1,0:T(8,128)S(1)} %get-tuple-element.67, s32[4,16,256]{2,1,0:T(8,128)S(1)} %get-tuple-element.70, ...), kind=kLoop, calls=%fused_computation.4 | loop fusion | flops 1146880 | bytes 1835008 | tf_op jit(solution)/shard_map/concatenate | solution.py:235
  26.7 4.0 %shard_map.121 = (f32[2,1024,128]{2,1,0:T(8,128)S(1)}, f32[2,1024,128]{2,1,0:T(8,128)S(1)}) custom-call(s32[24]{0:T(128)S(1)} %dynamic-slice_bitcast_fusion.refs_0_, s32[16,128]{1,0:T(8,128)S(1)} %bitcast.25, s32[16,56,256]{2,1,0:T(8,128)S(1)} %pad_add_fusion.refs_2_, ...), custom_call_target="tpu_custom_call", output_to_operand_aliasing={{0}: (9, {}), {1}: (10, {})} | custom-call | flops 7000000000 | bytes 1048576 | tf_op jit(solution)/shard_map/pallas_call | solution.py:165
  30.7 0.7 %collective-permute-start.8 = (f32[512,128]{1,0:T(8,128)S(1)}, f32[512,128]{1,0:T(8,128)S(1)}, u32[]{:S(2)}, u32[]{:S(2)}) collective-permute-start(f32[512,128]{1,0:T(8,128)S(1)} %collective-permute-done.3.refs_3_), channel_id=1, source_target_pairs={{0,8},{2,10},{8,16},{10,18},{16,24},{18,26},{24,28},{26,30},{28,20... | collective-permute-start | bytes 786440 | tf_op jit(solution)/shard_map/ppermute | solution.py:208
  31.5 1.3 %collective-permute-start.9 = (f32[512,128]{1,0:T(8,128)S(1)}, f32[512,128]{1,0:T(8,128)S(1)}, u32[]{:S(2)}, u32[]{:S(2)}) collective-permute-start(f32[512,128]{1,0:T(8,128)S(1)} %collective-permute-done.5.refs_5_), channel_id=1, source_target_pairs={{0,4},{2,6},{8,0},{10,2},{16,8},{18,10},{24,16},{26,18},{28,24},{3... | collective-permute-start | bytes 786440 | tf_op jit(solution)/shard_map/ppermute | solution.py:208
  32.8 3.7 %shard_map.122 = (f32[2,1024,128]{2,1,0:T(8,128)S(1)}, f32[2,1024,128]{2,1,0:T(8,128)S(1)}) custom-call(s32[24]{0:T(128)S(1)} %dynamic-slice_bitcast_fusion.refs_0_, s32[16,128]{1,0:T(8,128)S(1)} %bitcast.26, s32[16,56,256]{2,1,0:T(8,128)S(1)} %pad_add_fusion.refs_2_, ...), custom_call_target="tpu_custom_call", output_to_operand_aliasing={{0}: (7, {}), {1}: (8, {})} | custom-call | flops 5000000000 | bytes 1048576 | tf_op jit(solution)/shard_map/pallas_call | solution.py:165
  36.7 2.0 %collective-permute-start.19 = (f32[256,128]{1,0:T(8,128)S(1)}, f32[256,128]{1,0:T(8,128)S(1)}, u32[]{:S(2)}, u32[]{:S(2)}) collective-permute-start(f32[256,128]{1,0:T(8,128)S(1)} %slice.117), channel_id=1, source_target_pairs={{0,4},{2,6},{8,0},{10,2},{16,8},{18,10},{24,16},{26,18},{28,24},{3... | collective-permute-start | bytes 393224 | tf_op jit(solution)/shard_map/ppermute | solution.py:208
  38.7 1.3 %collective-permute-done.8.refs_3_ = f32[512,128]{1,0:T(8,128)S(1)} collective-permute-done((f32[512,128]{1,0:T(8,128)S(1)}, f32[512,128]{1,0:T(8,128)S(1)}, u32[]{:S(2)}, u32[]{:S(2)}) %collective-permute-start.8) | collective-permute-done | bytes 262176 | tf_op jit(solution)/shard_map/ppermute | solution.py:208
  40.0 0.7 %collective-permute-done.9.refs_5_ = f32[512,128]{1,0:T(8,128)S(1)} collective-permute-done((f32[512,128]{1,0:T(8,128)S(1)}, f32[512,128]{1,0:T(8,128)S(1)}, u32[]{:S(2)}, u32[]{:S(2)}) %collective-permute-start.9) | collective-permute-done | bytes 262176 | tf_op jit(solution)/shard_map/ppermute | solution.py:208
  40.7 1.5 %collective-permute-start.12 = (f32[256,128]{1,0:T(8,128)S(1)}, f32[256,128]{1,0:T(8,128)S(1)}, u32[]{:S(2)}, u32[]{:S(2)}) collective-permute-start(f32[256,128]{1,0:T(8,128)S(1)} %slice.98), channel_id=1, source_target_pairs={{0,8},{2,10},{8,16},{10,18},{16,24},{18,26},{24,28},{26,30},{28,20... | collective-permute-start | bytes 393224 | tf_op jit(solution)/shard_map/ppermute | solution.py:208
  42.2 0.6 collective-permute-start.13
  42.9 3.1 %shard_map.123 = (f32[2,1024,128]{2,1,0:T(8,128)S(1)}, f32[2,1024,128]{2,1,0:T(8,128)S(1)}) custom-call(s32[24]{0:T(128)S(1)} %dynamic-slice_bitcast_fusion.refs_0_, s32[16,128]{1,0:T(8,128)S(1)} %bitcast.27, s32[16,56,256]{2,1,0:T(8,128)S(1)} %pad_add_fusion.refs_2_, ...), custom_call_target="tpu_custom_call", output_to_operand_aliasing={{0}: (7, {}), {1}: (8, {})} | custom-call | flops 5000000000 | bytes 1048576 | tf_op jit(solution)/shard_map/pallas_call | solution.py:165
  46.0 2.0 %shard_map.125 = (f32[1024,128]{1,0:T(8,128)S(1)}, f32[1024,128]{1,0:T(8,128)S(1)}) custom-call(s32[24]{0:T(128)S(1)} %dynamic-slice_bitcast_fusion.refs_0_, s32[16,128]{1,0:T(8,128)S(1)} %bitcast.28, s32[16,56,256]{2,1,0:T(8,128)S(1)} %pad_add_fusion.refs_2_, f32[256,128]{1,0:T(8,128)S(1)} %collective-permute-done.18.refs_3_, ...), custom_call_target="tpu_custom_call" | custom-call | flops 4000000000 | bytes 1048576 | tf_op jit(solution)/shard_map/pallas_call | solution.py:165
  48.1 2.0 %shard_map.124 = (f32[1024,128]{1,0:T(8,128)S(1)}, f32[1024,128]{1,0:T(8,128)S(1)}) custom-call(s32[24]{0:T(128)S(1)} %dynamic-slice_bitcast_fusion.refs_0_, s32[16,128]{1,0:T(8,128)S(1)} %bitcast.29, s32[16,56,256]{2,1,0:T(8,128)S(1)} %pad_add_fusion.refs_2_, f32[256,128]{1,0:T(8,128)S(1)} %collective-permute-done.12.refs_3_, ...), custom_call_target="tpu_custom_call" | custom-call | flops 4000000000 | bytes 1048576 | tf_op jit(solution)/shard_map/pallas_call | solution.py:165
  50.1 1.0 %collective-permute-start.16 = (f32[1024,128]{1,0:T(8,128)S(1)}, f32[1024,128]{1,0:T(8,128)S(1)}, u32[]{:S(2)}, u32[]{:S(2)}) collective-permute-start(f32[1024,128]{1,0:T(8,128)S(1)} %get-tuple-element.58), channel_id=1, source_target_pairs={{0,2},{2,0},{4,6},{6,4},{8,10},{10,8},{12,14},{14,12},{16,18},{18,... | collective-permute-start | bytes 1572872 | tf_op jit(solution)/shard_map/ppermute | solution.py:211
  51.1 1.0 %collective-permute-start.21 = (f32[512,128]{1,0:T(8,128)S(1)}, f32[512,128]{1,0:T(8,128)S(1)}, u32[]{:S(2)}, u32[]{:S(2)}) collective-permute-start(f32[512,128]{1,0:T(8,128)S(1)} %slice_add_fusion), channel_id=1, source_target_pairs={{0,1},{1,0},{2,3},{3,2},{4,5},{5,4},{6,7},{7,6},{8,9},{9,8},{10,11... | collective-permute-start | bytes 786440 | tf_op jit(solution)/shard_map/ppermute | solution.py:214
  52.1 0.6 convolution_add_fusion.1
  52.7 1.2 %collective-permute-start.17 = (f32[512,128]{1,0:T(8,128)S(1)}, f32[512,128]{1,0:T(8,128)S(1)}, u32[]{:S(2)}, u32[]{:S(2)}) collective-permute-start(f32[512,128]{1,0:T(8,128)S(1)} %slice_add_fusion.2), channel_id=1, source_target_pairs={{0,1},{1,0},{2,3},{3,2},{4,5},{5,4},{6,7},{7,6},{8,9},{9,8},{10,11... | collective-permute-start | bytes 786440 | tf_op jit(solution)/shard_map/ppermute | solution.py:214
  54.0 6.4 %collective-permute-done.21 = f32[512,128]{1,0:T(8,128)S(1)} collective-permute-done((f32[512,128]{1,0:T(8,128)S(1)}, f32[512,128]{1,0:T(8,128)S(1)}, u32[]{:S(2)}, u32[]{:S(2)}) %collective-permute-start.21) | collective-permute-done | bytes 262176 | tf_op jit(solution)/shard_map/ppermute | solution.py:214
  60.7 4.3 %collective-permute-done.17 = f32[512,128]{1,0:T(8,128)S(1)} collective-permute-done((f32[512,128]{1,0:T(8,128)S(1)}, f32[512,128]{1,0:T(8,128)S(1)}, u32[]{:S(2)}, u32[]{:S(2)}) %collective-permute-start.17) | collective-permute-done | bytes 262176 | tf_op jit(solution)/shard_map/ppermute | solution.py:214
  65.1 1.2 %fusion.1 = f32[512,256]{1,0:T(8,128)} fusion(f32[512,256]{1,0:T(8,128)S(1)} %fusion.4, f32[512,256]{1,0:T(8,128)S(1)} %convolution_add_fusion.1, f32[512,128]{1,0:T(8,128)S(1)} %get-tuple-element.59, f32[512,128]{1,0:T(8,128)S(1)} %collective-permute-done.17, f32[1024,128]{1,0:T(8,128)S(1)} %collective-permute-done.16, ...), kind=kOutput, calls=%fused_computation.2 | convolution fusion | flops 101253120 | bytes 2752512 | tf_op jit(solution)/shard_map/dot_general | solution.py:313
  (76 shorter events, 2.8 us)
Async XLA Ops:
  0.0 52.1 %copy-start = (f32[256,256]{1,0:T(8,128)S(1)}, f32[256,256]{1,0:T(8,128)}, u32[]{:S(2)}) copy-start(f32[256,256]{1,0:T(8,128)} %param.14) | copy-start | bytes 786436
  0.0 4.3 %copy-start.5 = (s32[1,8,16,256]{3,2,1,0:T(8,128)S(1)}, s32[1,8,16,256]{3,2,1,0:T(8,128)}, u32[]{:S(2)}) copy-start(s32[1,8,16,256]{3,2,1,0:T(8,128)} %param.20) | copy-start | bytes 393220
  0.0 4.3 %copy-start.11 = (s32[1,8]{1,0:T(1,128)S(1)}, s32[1,8]{1,0:T(1,128)}, u32[]{:S(2)}) copy-start(s32[1,8]{1,0:T(1,128)} %param.19) | copy-start | bytes 100
  1.2 4.0 %copy-start.6 = (s32[1,8,16,256]{3,2,1,0:T(8,128)S(1)}, s32[1,8,16,256]{3,2,1,0:T(8,128)}, u32[]{:S(2)}) copy-start(s32[1,8,16,256]{3,2,1,0:T(8,128)} %param.22) | copy-start | bytes 393220
  1.2 4.0 %copy-start.7 = (s32[1,8,16,256]{3,2,1,0:T(8,128)S(1)}, s32[1,8,16,256]{3,2,1,0:T(8,128)}, u32[]{:S(2)}) copy-start(s32[1,8,16,256]{3,2,1,0:T(8,128)} %param.21) | copy-start | bytes 393220
  1.2 9.8 %collective-permute-start.6 = (f32[512,128]{1,0:T(8,128)S(1)}, f32[512,128]{1,0:T(8,128)S(1)}, u32[]{:S(2)}, u32[]{:S(2)}) collective-permute-start(f32[512,128]{1,0:T(8,128)S(1)} %shard_map.118.refs_4_), channel_id=1, source_target_pairs={{0,8},{2,10},{8,16},{10,18},{16,24},{18,26},{24,28},{26,30},{28,20... | collective-permute-start | bytes 786440 | tf_op jit(solution)/shard_map/ppermute | solution.py:208
  4.3 8.3 %collective-permute-start.7 = (f32[512,128]{1,0:T(8,128)S(1)}, f32[512,128]{1,0:T(8,128)S(1)}, u32[]{:S(2)}, u32[]{:S(2)}) collective-permute-start(f32[512,128]{1,0:T(8,128)S(1)} %shard_map.118.refs_4_), channel_id=1, source_target_pairs={{0,4},{2,6},{8,0},{10,2},{16,8},{18,10},{24,16},{26,18},{28,24},{3... | collective-permute-start | bytes 786440 | tf_op jit(solution)/shard_map/ppermute | solution.py:208
  5.3 1.6 %collective-permute-start = (s32[4,56,256]{2,1,0:T(8,128)S(1)}, s32[4,56,256]{2,1,0:T(8,128)S(1)}, u32[]{:S(2)}, u32[]{:S(2)}) collective-permute-start(s32[4,56,256]{2,1,0:T(8,128)S(1)} %pad_add_fusion.2), channel_id=1, source_target_pairs={{0,2},{2,0},{4,6},{6,4},{8,10},{10,8},{12,14},{14,12},{16,18},{18,... | collective-permute-start | bytes 688136 | tf_op jit(solution)/shard_map/ppermute | solution.py:211
  5.7 1.1 %copy-start.2 = (s32[4,8,256]{2,1,0:T(8,128)}, s32[4,8,256]{2,1,0:T(8,128)S(1)}, u32[]{:S(2)}) copy-start(s32[4,8,256]{2,1,0:T(8,128)S(1)} %pad.15) | copy-start | bytes 98308
  6.9 9.4 %collective-permute-start.1 = (f32[512,128]{1,0:T(8,128)S(1)}, f32[512,128]{1,0:T(8,128)S(1)}, u32[]{:S(2)}, u32[]{:S(2)}) collective-permute-start(f32[512,128]{1,0:T(8,128)S(1)} %get-tuple-element.39.refs_3_), channel_id=1, source_target_pairs={{0,8},{2,10},{8,16},{10,18},{16,24},{18,26},{24,28},{26,30},{28,20... | collective-permute-start | bytes 786440 | tf_op jit(solution)/shard_map/ppermute | solution.py:208
  9.0 9.9 %collective-permute-start.4 = (f32[512,128]{1,0:T(8,128)S(1)}, f32[512,128]{1,0:T(8,128)S(1)}, u32[]{:S(2)}, u32[]{:S(2)}) collective-permute-start(f32[512,128]{1,0:T(8,128)S(1)} %get-tuple-element.39.refs_3_), channel_id=1, source_target_pairs={{0,4},{2,6},{8,0},{10,2},{16,8},{18,10},{24,16},{26,18},{28,24},{3... | collective-permute-start | bytes 786440 | tf_op jit(solution)/shard_map/ppermute | solution.py:208
  9.0 16.6 %collective-permute-start.2 = (s32[8,56,256]{2,1,0:T(8,128)S(1)}, s32[8,56,256]{2,1,0:T(8,128)}, u32[]{:S(2)}, u32[]{:S(2)}) collective-permute-start(s32[8,56,256]{2,1,0:T(8,128)S(1)} %pad_add_fusion.1.refs_2_), channel_id=1, source_target_pairs={{0,1},{1,0},{2,3},{3,2},{4,5},{5,4},{6,7},{7,6},{8,9},{9,8},{10,11... | collective-permute-start | bytes 1376264 | tf_op jit(solution)/shard_map/ppermute | solution.py:214
  10.9 11.0 %collective-permute-start.10 = (f32[512,128]{1,0:T(8,128)S(1)}, f32[512,128]{1,0:T(8,128)S(1)}, u32[]{:S(2)}, u32[]{:S(2)}) collective-permute-start(f32[512,128]{1,0:T(8,128)S(1)} %collective-permute-done.6.refs_6_), channel_id=1, source_target_pairs={{0,8},{2,10},{8,16},{10,18},{16,24},{18,26},{24,28},{26,30},{28,20... | collective-permute-start | bytes 786440 | tf_op jit(solution)/shard_map/ppermute | solution.py:208
  12.5 13.1 %collective-permute-start.11 = (f32[512,128]{1,0:T(8,128)S(1)}, f32[512,128]{1,0:T(8,128)S(1)}, u32[]{:S(2)}, u32[]{:S(2)}) collective-permute-start(f32[512,128]{1,0:T(8,128)S(1)} %collective-permute-done.7.refs_8_), channel_id=1, source_target_pairs={{0,4},{2,6},{8,0},{10,2},{16,8},{18,10},{24,16},{26,18},{28,24},{3... | collective-permute-start | bytes 786440 | tf_op jit(solution)/shard_map/ppermute | solution.py:208
  16.3 14.4 %collective-permute-start.3 = (f32[512,128]{1,0:T(8,128)S(1)}, f32[512,128]{1,0:T(8,128)S(1)}, u32[]{:S(2)}, u32[]{:S(2)}) collective-permute-start(f32[512,128]{1,0:T(8,128)S(1)} %collective-permute-done.1.refs_5_), channel_id=1, source_target_pairs={{0,8},{2,10},{8,16},{10,18},{16,24},{18,26},{24,28},{26,30},{28,20... | collective-permute-start | bytes 786440 | tf_op jit(solution)/shard_map/ppermute | solution.py:208
  18.8 11.9 %collective-permute-start.5 = (f32[512,128]{1,0:T(8,128)S(1)}, f32[512,128]{1,0:T(8,128)S(1)}, u32[]{:S(2)}, u32[]{:S(2)}) collective-permute-start(f32[512,128]{1,0:T(8,128)S(1)} %collective-permute-done.4.refs_7_), channel_id=1, source_target_pairs={{0,4},{2,6},{8,0},{10,2},{16,8},{18,10},{24,16},{26,18},{28,24},{3... | collective-permute-start | bytes 786440 | tf_op jit(solution)/shard_map/ppermute | solution.py:208
  19.0 6.6 %copy-start.3 = (s32[4,8,256]{2,1,0:T(8,128)S(1)}, s32[4,8,256]{2,1,0:T(8,128)}, u32[]{:S(2)}) copy-start(s32[4,8,256]{2,1,0:T(8,128)} %copy-done.2) | copy-start | bytes 98308
  21.9 14.6 %collective-permute-start.14 = (f32[512,128]{1,0:T(8,128)S(1)}, f32[512,128]{1,0:T(8,128)S(1)}, u32[]{:S(2)}, u32[]{:S(2)}) collective-permute-start(f32[512,128]{1,0:T(8,128)S(1)} %collective-permute-done.10.refs_4_), channel_id=1, source_target_pairs={{0,8},{2,10},{8,16},{10,18},{16,24},{18,26},{24,28},{26,30},{28,20... | collective-permute-start | bytes 786440 | tf_op jit(solution)/shard_map/ppermute | solution.py:208
  25.6 11.1 %collective-permute-start.15 = (f32[512,128]{1,0:T(8,128)S(1)}, f32[512,128]{1,0:T(8,128)S(1)}, u32[]{:S(2)}, u32[]{:S(2)}) collective-permute-start(f32[512,128]{1,0:T(8,128)S(1)} %collective-permute-done.11.refs_6_), channel_id=1, source_target_pairs={{0,4},{2,6},{8,0},{10,2},{16,8},{18,10},{24,16},{26,18},{28,24},{3... | collective-permute-start | bytes 786440 | tf_op jit(solution)/shard_map/ppermute | solution.py:208
  30.7 9.3 %collective-permute-start.8 = (f32[512,128]{1,0:T(8,128)S(1)}, f32[512,128]{1,0:T(8,128)S(1)}, u32[]{:S(2)}, u32[]{:S(2)}) collective-permute-start(f32[512,128]{1,0:T(8,128)S(1)} %collective-permute-done.3.refs_3_), channel_id=1, source_target_pairs={{0,8},{2,10},{8,16},{10,18},{16,24},{18,26},{24,28},{26,30},{28,20... | collective-permute-start | bytes 786440 | tf_op jit(solution)/shard_map/ppermute | solution.py:208
  31.5 9.2 %collective-permute-start.9 = (f32[512,128]{1,0:T(8,128)S(1)}, f32[512,128]{1,0:T(8,128)S(1)}, u32[]{:S(2)}, u32[]{:S(2)}) collective-permute-start(f32[512,128]{1,0:T(8,128)S(1)} %collective-permute-done.5.refs_5_), channel_id=1, source_target_pairs={{0,4},{2,6},{8,0},{10,2},{16,8},{18,10},{24,16},{26,18},{28,24},{3... | collective-permute-start | bytes 786440 | tf_op jit(solution)/shard_map/ppermute | solution.py:208
  36.6 9.4 %collective-permute-start.18 = (f32[256,128]{1,0:T(8,128)S(1)}, f32[256,128]{1,0:T(8,128)S(1)}, u32[]{:S(2)}, u32[]{:S(2)}) collective-permute-start(f32[256,128]{1,0:T(8,128)S(1)} %slice.116), channel_id=1, source_target_pairs={{0,8},{2,10},{8,16},{10,18},{16,24},{18,26},{24,28},{26,30},{28,20... | collective-permute-start | bytes 393224 | tf_op jit(solution)/shard_map/ppermute | solution.py:208
  36.7 9.3 %collective-permute-start.19 = (f32[256,128]{1,0:T(8,128)S(1)}, f32[256,128]{1,0:T(8,128)S(1)}, u32[]{:S(2)}, u32[]{:S(2)}) collective-permute-start(f32[256,128]{1,0:T(8,128)S(1)} %slice.117), channel_id=1, source_target_pairs={{0,4},{2,6},{8,0},{10,2},{16,8},{18,10},{24,16},{26,18},{28,24},{3... | collective-permute-start | bytes 393224 | tf_op jit(solution)/shard_map/ppermute | solution.py:208
  40.7 7.3 %collective-permute-start.12 = (f32[256,128]{1,0:T(8,128)S(1)}, f32[256,128]{1,0:T(8,128)S(1)}, u32[]{:S(2)}, u32[]{:S(2)}) collective-permute-start(f32[256,128]{1,0:T(8,128)S(1)} %slice.98), channel_id=1, source_target_pairs={{0,8},{2,10},{8,16},{10,18},{16,24},{18,26},{24,28},{26,30},{28,20... | collective-permute-start | bytes 393224 | tf_op jit(solution)/shard_map/ppermute | solution.py:208
  42.2 5.8 %collective-permute-start.13 = (f32[256,128]{1,0:T(8,128)S(1)}, f32[256,128]{1,0:T(8,128)S(1)}, u32[]{:S(2)}, u32[]{:S(2)}) collective-permute-start(f32[256,128]{1,0:T(8,128)S(1)} %slice.99), channel_id=1, source_target_pairs={{0,4},{2,6},{8,0},{10,2},{16,8},{18,10},{24,16},{26,18},{28,24},{3... | collective-permute-start | bytes 393224 | tf_op jit(solution)/shard_map/ppermute | solution.py:208
  48.0 3.1 %collective-permute-start.20 = (f32[1024,128]{1,0:T(8,128)S(1)}, f32[1024,128]{1,0:T(8,128)S(1)}, u32[]{:S(2)}, u32[]{:S(2)}) collective-permute-start(f32[1024,128]{1,0:T(8,128)S(1)} %get-tuple-element.62), channel_id=1, source_target_pairs={{0,2},{2,0},{4,6},{6,4},{8,10},{10,8},{12,14},{14,12},{16,18},{18,... | collective-permute-start | bytes 1572872 | tf_op jit(solution)/shard_map/ppermute | solution.py:211
  50.0 2.0 %copy-start.1 = (f32[512,256]{1,0:T(8,128)S(1)}, f32[512,256]{1,0:T(8,128)}, u32[]{:S(2)}) copy-start(f32[512,256]{1,0:T(8,128)} %features.2) | copy-start | bytes 1572868
  50.1 2.6 %collective-permute-start.16 = (f32[1024,128]{1,0:T(8,128)S(1)}, f32[1024,128]{1,0:T(8,128)S(1)}, u32[]{:S(2)}, u32[]{:S(2)}) collective-permute-start(f32[1024,128]{1,0:T(8,128)S(1)} %get-tuple-element.58), channel_id=1, source_target_pairs={{0,2},{2,0},{4,6},{6,4},{8,10},{10,8},{12,14},{14,12},{16,18},{18,... | collective-permute-start | bytes 1572872 | tf_op jit(solution)/shard_map/ppermute | solution.py:211
  51.1 1.0 %copy-start.10 = (f32[256]{0:T(256)S(1)}, f32[256]{0:T(256)}, u32[]{:S(2)}) copy-start(f32[256]{0:T(256)} %param.16) | copy-start | bytes 3076
  51.1 9.2 %collective-permute-start.21 = (f32[512,128]{1,0:T(8,128)S(1)}, f32[512,128]{1,0:T(8,128)S(1)}, u32[]{:S(2)}, u32[]{:S(2)}) collective-permute-start(f32[512,128]{1,0:T(8,128)S(1)} %slice_add_fusion), channel_id=1, source_target_pairs={{0,1},{1,0},{2,3},{3,2},{4,5},{5,4},{6,7},{7,6},{8,9},{9,8},{10,11... | collective-permute-start | bytes 786440 | tf_op jit(solution)/shard_map/ppermute | solution.py:214
  52.7 7.7 %copy-start.4 = (f32[256,256]{1,0:T(8,128)S(1)}, f32[256,256]{1,0:T(8,128)}, u32[]{:S(2)}) copy-start(f32[256,256]{1,0:T(8,128)} %param.15) | copy-start | bytes 786436
  52.7 12.3 %collective-permute-start.17 = (f32[512,128]{1,0:T(8,128)S(1)}, f32[512,128]{1,0:T(8,128)S(1)}, u32[]{:S(2)}, u32[]{:S(2)}) collective-permute-start(f32[512,128]{1,0:T(8,128)S(1)} %slice_add_fusion.2), channel_id=1, source_target_pairs={{0,1},{1,0},{2,3},{3,2},{4,5},{5,4},{6,7},{7,6},{8,9},{9,8},{10,11... | collective-permute-start | bytes 786440 | tf_op jit(solution)/shard_map/ppermute | solution.py:214
  (2 other events, 1.4 us)

commit v7 on v6

--- a/solution.py
+++ b/solution.py
@@ -269,6 +269,8 @@
     table = np.array(
         [numbers_of(b // 2, b % 2, r) for b in range(blocks) for r in range(groups)], dtype=np.int32
     )
+    numbers = lax.dynamic_index_in_dim(jnp.asarray(table), block * groups + replica, keepdims=False)
+
     def base_of(step):
         return 14 + 4 * (step - 2)
 
@@ -288,8 +290,6 @@
         parts = [[[v] for v in side] for side in hops[step - 1]]
         if step == 1:
             early = parts[:1]
-            index, _ = lax.optimization_barrier((block * groups + replica, hops[-1][0][0]))
-            numbers = lax.dynamic_index_in_dim(jnp.asarray(table), index, keepdims=False)
         elif step == 2:
             early = early + parts
             totals = add(2, numbers, near_meta, lists, early, None)

time: 66.8 us -> 66.7 us (level)
  waiting for transfers between devices: 17 us -> 19.4 us
  starting transfers between devices: 24.5 us -> 22.9 us
  other arithmetic: 1.38 us -> 0.34 us
    ppermute x16, waiting for transfers between devices: 6.21 us -> 9.05 us  [ring(): return lax.ppermute(value, 'blk', pairs)]
    ppermute x16, starting transfers between devices: 19.2 us -> 17.5 us  [ring(): return lax.ppermute(value, 'blk', pairs)]
    concatenate x1, other arithmetic: 1.09 us -> 0.07 us  [on_device(): edges = jnp.concatenate([lists, rep_swap(lists)], axis=0)]
    ppermute x3, starting transfers between devices: 4.12 us -> 5.12 us  [rep_swap(): return lax.ppermute(value, 'rep', [(0, 1), (1, 0)])]
    ppermute x3, starting transfers between devices: 1.18 us -> 0.21 us  [core_swap(): return lax.ppermute(value, 'blk', [(b, b ^ 1) for b in range(blocks)])]
  transfers between devices with their start and end apart: 22 -> 22, of which waited for: 6 -> 7; matrix products, arithmetic and copies ran while one was open for 5% -> 4% of each run, Pallas kernels for 27% -> 27%
where the time goes in v7:
time: 66.7 us; the launch traced here: 66.3 us
  starting transfers between devices  22.9 us (34%)
  Pallas kernels  19.4 us (29%)
  waiting for transfers between devices  19.4 us (29%)
  matrix products  2.11 us (3%)
  local copies, waits for them, and re-layouts  1.88 us (3%)
    ppermute x16, starting transfers between devices, ring(): return lax.ppermute(value, 'blk', pairs)  17.5 us
    pallas_call x6, Pallas kernels, add_sources(): pl.pallas_call(functools.partial(sum_kernel, base, sources, chunks, piece...  17.1 us
    ppermute x3, waiting for transfers between devices, rep_swap(): return lax.ppermute(value, 'rep', [(0, 1), (1, 0)])  10.3 us
    ppermute x16, waiting for transfers between devices, ring(): return lax.ppermute(value, 'blk', pairs)  9.05 us
    ppermute x3, starting transfers between devices, rep_swap(): return lax.ppermute(value, 'rep', [(0, 1), (1, 0)])  5.12 us
    pallas_call x2, Pallas kernels, scaled_chunk(): pl.pallas_call(scale_kernel, grid=(1,), in_specs=[pl.BlockSpec((tiles, TI...  2.26 us
    dot_general x2, matrix products, on_device(): jnp.dot(mixed, neighbor_weight[f * TILE:(f + 1) * TILE], precision=final)  1.53 us
  transfers between devices with their start and end apart: 22, of which 7 were waited for; matrix products, arithmetic and copies ran while one was open for 4% of the time, Pallas kernels for 27%

profile of v7, /device:TPU:0, one launch (start us, length us, event | category | flops | bytes accessed | tf_op | source)
XLA Modules:
  0.0 66.3 jit_solution(8055510580468928061)
XLA Ops:
  0.0 1.2 %shard_map.118.refs_4_ = f32[512,128]{1,0:T(8,128)S(1)} custom-call(s32[4,128]{1,0:T(4,128)} %bitcast.37, f32[512,256]{1,0:T(8,128)} %features.2), custom_call_target="tpu_custom_call" | custom-call | flops 3000000000 | bytes 1048576 | tf_op jit(solution)/shard_map/pallas_call | solution.py:37
  1.2 3.1 %collective-permute-start.6 = (f32[512,128]{1,0:T(8,128)S(1)}, f32[512,128]{1,0:T(8,128)S(1)}, u32[]{:S(2)}, u32[]{:S(2)}) collective-permute-start(f32[512,128]{1,0:T(8,128)S(1)} %shard_map.118.refs_4_), channel_id=1, source_target_pairs={{0,8},{2,10},{8,16},{10,18},{16,24},{18,26},{24,28},{26,30},{28,20... | collective-permute-start | bytes 786440 | tf_op jit(solution)/shard_map/ppermute | solution.py:208
  4.5 0.5 copy-done.6
  5.7 1.1 %shard_map.119 = (f32[512,128]{1,0:T(8,128)S(1)}, f32[512,128]{1,0:T(8,128)S(1)}) custom-call(s32[4,128]{1,0:T(4,128)} %bitcast.38, f32[512,256]{1,0:T(8,128)} %features.2), custom_call_target="tpu_custom_call" | custom-call | flops 3000000000 | bytes 1048576 | tf_op jit(solution)/shard_map/pallas_call | solution.py:37
  6.9 2.1 %collective-permute-start.2 = (f32[512,128]{1,0:T(8,128)S(1)}, f32[512,128]{1,0:T(8,128)S(1)}, u32[]{:S(2)}, u32[]{:S(2)}) collective-permute-start(f32[512,128]{1,0:T(8,128)S(1)} %get-tuple-element.38.refs_3_), channel_id=1, source_target_pairs={{0,8},{2,10},{8,16},{10,18},{16,24},{18,26},{24,28},{26,30},{28,20... | collective-permute-start | bytes 786440 | tf_op jit(solution)/shard_map/ppermute | solution.py:208
  9.0 0.7 %dynamic-slice_bitcast_fusion.refs_0_ = s32[24]{0:T(128)S(1)} fusion(s32[32,24]{1,0:T(8,128)} %constant.22.clone, s32[]{:T(128)S(6)} %select_n.4), kind=kLoop, calls=%fused_computation.28 | loop fusion | bytes 196 | tf_op jit(solution)/shard_map/jit(dynamic_index_in_dim)/squeeze | solution.py:272
  9.7 2.0 %collective-permute-start.1 = (s32[8,56,256]{2,1,0:T(8,128)S(1)}, s32[8,56,256]{2,1,0:T(8,128)S(1)}, u32[]{:S(2)}, u32[]{:S(2)}) collective-permute-start(s32[8,56,256]{2,1,0:T(8,128)S(1)} %pad_add_fusion.1.refs_2_), channel_id=1, source_target_pairs={{0,1},{1,0},{2,3},{3,2},{4,5},{5,4},{6,7},{7,6},{8,9},{9,8},{10,11... | collective-permute-start | bytes 1376264 | tf_op jit(solution)/shard_map/ppermute | solution.py:214
  11.6 1.6 %collective-permute-start.10 = (f32[512,128]{1,0:T(8,128)S(1)}, f32[512,128]{1,0:T(8,128)S(1)}, u32[]{:S(2)}, u32[]{:S(2)}) collective-permute-start(f32[512,128]{1,0:T(8,128)S(1)} %collective-permute-done.6.refs_6_), channel_id=1, source_target_pairs={{0,8},{2,10},{8,16},{10,18},{16,24},{18,26},{24,28},{26,30},{28,20... | collective-permute-start | bytes 786440 | tf_op jit(solution)/shard_map/ppermute | solution.py:208
  13.7 2.7 %collective-permute-done.2.refs_5_ = f32[512,128]{1,0:T(8,128)S(1)} collective-permute-done((f32[512,128]{1,0:T(8,128)S(1)}, f32[512,128]{1,0:T(8,128)S(1)}, u32[]{:S(2)}, u32[]{:S(2)}) %collective-permute-start.2) | collective-permute-done | bytes 262176 | tf_op jit(solution)/shard_map/ppermute | solution.py:208
  16.3 1.8 %collective-permute-start.3 = (f32[512,128]{1,0:T(8,128)S(1)}, f32[512,128]{1,0:T(8,128)S(1)}, u32[]{:S(2)}, u32[]{:S(2)}) collective-permute-start(f32[512,128]{1,0:T(8,128)S(1)} %collective-permute-done.2.refs_5_), channel_id=1, source_target_pairs={{0,8},{2,10},{8,16},{10,18},{16,24},{18,26},{24,28},{26,30},{28,20... | collective-permute-start | bytes 786440 | tf_op jit(solution)/shard_map/ppermute | solution.py:208
  18.4 2.0 %shard_map.120 = (f32[2,1024,128]{2,1,0:T(8,128)S(1)}, f32[2,1024,128]{2,1,0:T(8,128)S(1)}) custom-call(s32[24]{0:T(128)S(1)} %dynamic-slice_bitcast_fusion.refs_0_, s32[8,128]{1,0:T(8,128)S(1)} %bitcast.30, s32[8,56,256]{2,1,0:T(8,128)S(1)} %pad_add_fusion.1.refs_2_, f32[512,128]{1,0:T(8,128)S(1)} %get-tuple-element.38.refs_3_, ...), custom_call_target="tpu_custom_call" | custom-call | flops 7000000000 | bytes 1048576 | tf_op jit(solution)/shard_map/pallas_call | solution.py:165
  20.4 1.6 %collective-permute-done.10.refs_4_ = f32[512,128]{1,0:T(8,128)S(1)} collective-permute-done((f32[512,128]{1,0:T(8,128)S(1)}, f32[512,128]{1,0:T(8,128)S(1)}, u32[]{:S(2)}, u32[]{:S(2)}) %collective-permute-start.10) | collective-permute-done | bytes 262176 | tf_op jit(solution)/shard_map/ppermute | solution.py:208
  22.0 1.8 %collective-permute-start.14 = (f32[512,128]{1,0:T(8,128)S(1)}, f32[512,128]{1,0:T(8,128)S(1)}, u32[]{:S(2)}, u32[]{:S(2)}) collective-permute-start(f32[512,128]{1,0:T(8,128)S(1)} %collective-permute-done.10.refs_4_), channel_id=1, source_target_pairs={{0,8},{2,10},{8,16},{10,18},{16,24},{18,26},{24,28},{26,30},{28,20... | collective-permute-start | bytes 786440 | tf_op jit(solution)/shard_map/ppermute | solution.py:208
  24.1 3.9 %shard_map.121 = (f32[2,1024,128]{2,1,0:T(8,128)S(1)}, f32[2,1024,128]{2,1,0:T(8,128)S(1)}) custom-call(s32[24]{0:T(128)S(1)} %dynamic-slice_bitcast_fusion.refs_0_, s32[16,128]{1,0:T(8,128)S(1)} %bitcast.25, s32[16,56,256]{2,1,0:T(8,128)S(1)} %pad_add_fusion.refs_2_, ...), custom_call_target="tpu_custom_call", output_to_operand_aliasing={{0}: (9, {}), {1}: (10, {})} | custom-call | flops 7000000000 | bytes 1048576 | tf_op jit(solution)/shard_map/pallas_call | solution.py:165
  28.0 1.4 %collective-permute-done.5.refs_5_ = f32[512,128]{1,0:T(8,128)S(1)} collective-permute-done((f32[512,128]{1,0:T(8,128)S(1)}, f32[512,128]{1,0:T(8,128)S(1)}, u32[]{:S(2)}, u32[]{:S(2)}) %collective-permute-start.5) | collective-permute-done | bytes 262176 | tf_op jit(solution)/shard_map/ppermute | solution.py:208
  29.3 1.6 %collective-permute-start.8 = (f32[512,128]{1,0:T(8,128)S(1)}, f32[512,128]{1,0:T(8,128)S(1)}, u32[]{:S(2)}, u32[]{:S(2)}) collective-permute-start(f32[512,128]{1,0:T(8,128)S(1)} %collective-permute-done.3.refs_3_), channel_id=1, source_target_pairs={{0,8},{2,10},{8,16},{10,18},{16,24},{18,26},{24,28},{26,30},{28,20... | collective-permute-start | bytes 786440 | tf_op jit(solution)/shard_map/ppermute | solution.py:208
  31.4 3.6 %shard_map.122 = (f32[2,1024,128]{2,1,0:T(8,128)S(1)}, f32[2,1024,128]{2,1,0:T(8,128)S(1)}) custom-call(s32[24]{0:T(128)S(1)} %dynamic-slice_bitcast_fusion.refs_0_, s32[16,128]{1,0:T(8,128)S(1)} %bitcast.26, s32[16,56,256]{2,1,0:T(8,128)S(1)} %pad_add_fusion.refs_2_, ...), custom_call_target="tpu_custom_call", output_to_operand_aliasing={{0}: (7, {}), {1}: (8, {})} | custom-call | flops 5000000000 | bytes 1048576 | tf_op jit(solution)/shard_map/pallas_call | solution.py:165
  35.0 1.0 %collective-permute-start.18 = (f32[256,128]{1,0:T(8,128)S(1)}, f32[256,128]{1,0:T(8,128)S(1)}, u32[]{:S(2)}, u32[]{:S(2)}) collective-permute-start(f32[256,128]{1,0:T(8,128)S(1)} %slice.116), channel_id=1, source_target_pairs={{0,8},{2,10},{8,16},{10,18},{16,24},{18,26},{24,28},{26,30},{28,20... | collective-permute-start | bytes 393224 | tf_op jit(solution)/shard_map/ppermute | solution.py:208
  36.1 1.1 %collective-permute-start.19 = (f32[256,128]{1,0:T(8,128)S(1)}, f32[256,128]{1,0:T(8,128)S(1)}, u32[]{:S(2)}, u32[]{:S(2)}) collective-permute-start(f32[256,128]{1,0:T(8,128)S(1)} %slice.117), channel_id=1, source_target_pairs={{0,4},{2,6},{8,0},{10,2},{16,8},{18,10},{24,16},{26,18},{28,24},{3... | collective-permute-start | bytes 393224 | tf_op jit(solution)/shard_map/ppermute | solution.py:208
  37.2 1.6 %collective-permute-done.8.refs_3_ = f32[512,128]{1,0:T(8,128)S(1)} collective-permute-done((f32[512,128]{1,0:T(8,128)S(1)}, f32[512,128]{1,0:T(8,128)S(1)}, u32[]{:S(2)}, u32[]{:S(2)}) %collective-permute-start.8) | collective-permute-done | bytes 262176 | tf_op jit(solution)/shard_map/ppermute | solution.py:208
  38.8 1.8 %collective-permute-done.9.refs_5_ = f32[512,128]{1,0:T(8,128)S(1)} collective-permute-done((f32[512,128]{1,0:T(8,128)S(1)}, f32[512,128]{1,0:T(8,128)S(1)}, u32[]{:S(2)}, u32[]{:S(2)}) %collective-permute-start.9) | collective-permute-done | bytes 262176 | tf_op jit(solution)/shard_map/ppermute | solution.py:208
  40.6 1.6 %collective-permute-start.12 = (f32[256,128]{1,0:T(8,128)S(1)}, f32[256,128]{1,0:T(8,128)S(1)}, u32[]{:S(2)}, u32[]{:S(2)}) collective-permute-start(f32[256,128]{1,0:T(8,128)S(1)} %slice.98), channel_id=1, source_target_pairs={{0,8},{2,10},{8,16},{10,18},{16,24},{18,26},{24,28},{26,30},{28,20... | collective-permute-start | bytes 393224 | tf_op jit(solution)/shard_map/ppermute | solution.py:208
  42.2 0.5 collective-permute-start.13
  42.7 3.6 %shard_map.123 = (f32[2,1024,128]{2,1,0:T(8,128)S(1)}, f32[2,1024,128]{2,1,0:T(8,128)S(1)}) custom-call(s32[24]{0:T(128)S(1)} %dynamic-slice_bitcast_fusion.refs_0_, s32[16,128]{1,0:T(8,128)S(1)} %bitcast.27, s32[16,56,256]{2,1,0:T(8,128)S(1)} %pad_add_fusion.refs_2_, ...), custom_call_target="tpu_custom_call", output_to_operand_aliasing={{0}: (7, {}), {1}: (8, {})} | custom-call | flops 5000000000 | bytes 1048576 | tf_op jit(solution)/shard_map/pallas_call | solution.py:165
  46.4 2.0 %shard_map.125 = (f32[1024,128]{1,0:T(8,128)S(1)}, f32[1024,128]{1,0:T(8,128)S(1)}) custom-call(s32[24]{0:T(128)S(1)} %dynamic-slice_bitcast_fusion.refs_0_, s32[16,128]{1,0:T(8,128)S(1)} %bitcast.28, s32[16,56,256]{2,1,0:T(8,128)S(1)} %pad_add_fusion.refs_2_, f32[256,128]{1,0:T(8,128)S(1)} %collective-permute-done.18.refs_3_, ...), custom_call_target="tpu_custom_call" | custom-call | flops 4000000000 | bytes 1048576 | tf_op jit(solution)/shard_map/pallas_call | solution.py:165
  48.5 2.0 %shard_map.124 = (f32[1024,128]{1,0:T(8,128)S(1)}, f32[1024,128]{1,0:T(8,128)S(1)}) custom-call(s32[24]{0:T(128)S(1)} %dynamic-slice_bitcast_fusion.refs_0_, s32[16,128]{1,0:T(8,128)S(1)} %bitcast.29, s32[16,56,256]{2,1,0:T(8,128)S(1)} %pad_add_fusion.refs_2_, f32[256,128]{1,0:T(8,128)S(1)} %collective-permute-done.12.refs_3_, ...), custom_call_target="tpu_custom_call" | custom-call | flops 4000000000 | bytes 1048576 | tf_op jit(solution)/shard_map/pallas_call | solution.py:165
  50.6 1.9 %collective-permute-start.21 = (f32[512,128]{1,0:T(8,128)S(1)}, f32[512,128]{1,0:T(8,128)S(1)}, u32[]{:S(2)}, u32[]{:S(2)}) collective-permute-start(f32[512,128]{1,0:T(8,128)S(1)} %slice_add_fusion), channel_id=1, source_target_pairs={{0,1},{1,0},{2,3},{3,2},{4,5},{5,4},{6,7},{7,6},{8,9},{9,8},{10,11... | collective-permute-start | bytes 786440 | tf_op jit(solution)/shard_map/ppermute | solution.py:214
  52.6 0.6 convolution_add_fusion.1
  53.2 1.2 %collective-permute-start.17 = (f32[512,128]{1,0:T(8,128)S(1)}, f32[512,128]{1,0:T(8,128)S(1)}, u32[]{:S(2)}, u32[]{:S(2)}) collective-permute-start(f32[512,128]{1,0:T(8,128)S(1)} %slice_add_fusion.2), channel_id=1, source_target_pairs={{0,1},{1,0},{2,3},{3,2},{4,5},{5,4},{6,7},{7,6},{8,9},{9,8},{10,11... | collective-permute-start | bytes 786440 | tf_op jit(solution)/shard_map/ppermute | solution.py:214
  54.4 5.3 %collective-permute-done.21 = f32[512,128]{1,0:T(8,128)S(1)} collective-permute-done((f32[512,128]{1,0:T(8,128)S(1)}, f32[512,128]{1,0:T(8,128)S(1)}, u32[]{:S(2)}, u32[]{:S(2)}) %collective-permute-start.21) | collective-permute-done | bytes 262176 | tf_op jit(solution)/shard_map/ppermute | solution.py:214
  60.1 5.0 %collective-permute-done.17 = f32[512,128]{1,0:T(8,128)S(1)} collective-permute-done((f32[512,128]{1,0:T(8,128)S(1)}, f32[512,128]{1,0:T(8,128)S(1)}, u32[]{:S(2)}, u32[]{:S(2)}) %collective-permute-start.17) | collective-permute-done | bytes 262176 | tf_op jit(solution)/shard_map/ppermute | solution.py:214
  65.1 1.2 %fusion.1 = f32[512,256]{1,0:T(8,128)} fusion(f32[512,256]{1,0:T(8,128)S(1)} %fusion.4, f32[512,256]{1,0:T(8,128)S(1)} %convolution_add_fusion.1, f32[512,128]{1,0:T(8,128)S(1)} %get-tuple-element.57, f32[512,128]{1,0:T(8,128)S(1)} %collective-permute-done.17, f32[1024,128]{1,0:T(8,128)S(1)} %collective-permute-done.16, ...), kind=kOutput, calls=%fused_computation.2 | convolution fusion | flops 101253120 | bytes 2752512 | tf_op jit(solution)/shard_map/dot_general | solution.py:313
  (72 shorter events, 3.0 us)
Async XLA Ops:
  0.0 52.5 %copy-start = (f32[256,256]{1,0:T(8,128)S(1)}, f32[256,256]{1,0:T(8,128)}, u32[]{:S(2)}) copy-start(f32[256,256]{1,0:T(8,128)} %param.14) | copy-start | bytes 786436
  0.0 4.3 %copy-start.3 = (s32[1,8,16,256]{3,2,1,0:T(8,128)S(1)}, s32[1,8,16,256]{3,2,1,0:T(8,128)}, u32[]{:S(2)}) copy-start(s32[1,8,16,256]{3,2,1,0:T(8,128)} %param.20) | copy-start | bytes 393220
  0.0 4.3 %copy-start.9 = (s32[1,8]{1,0:T(1,128)S(1)}, s32[1,8]{1,0:T(1,128)}, u32[]{:S(2)}) copy-start(s32[1,8]{1,0:T(1,128)} %param.19) | copy-start | bytes 100
  1.2 4.0 %copy-start.4 = (s32[1,8,16,256]{3,2,1,0:T(8,128)S(1)}, s32[1,8,16,256]{3,2,1,0:T(8,128)}, u32[]{:S(2)}) copy-start(s32[1,8,16,256]{3,2,1,0:T(8,128)} %param.22) | copy-start | bytes 393220
  1.2 4.0 %copy-start.5 = (s32[1,8,16,256]{3,2,1,0:T(8,128)S(1)}, s32[1,8,16,256]{3,2,1,0:T(8,128)}, u32[]{:S(2)}) copy-start(s32[1,8,16,256]{3,2,1,0:T(8,128)} %param.21) | copy-start | bytes 393220
  1.2 10.4 %collective-permute-start.6 = (f32[512,128]{1,0:T(8,128)S(1)}, f32[512,128]{1,0:T(8,128)S(1)}, u32[]{:S(2)}, u32[]{:S(2)}) collective-permute-start(f32[512,128]{1,0:T(8,128)S(1)} %shard_map.118.refs_4_), channel_id=1, source_target_pairs={{0,8},{2,10},{8,16},{10,18},{16,24},{18,26},{24,28},{26,30},{28,20... | collective-permute-start | bytes 786440 | tf_op jit(solution)/shard_map/ppermute | solution.py:208
  4.3 8.9 %collective-permute-start.7 = (f32[512,128]{1,0:T(8,128)S(1)}, f32[512,128]{1,0:T(8,128)S(1)}, u32[]{:S(2)}, u32[]{:S(2)}) collective-permute-start(f32[512,128]{1,0:T(8,128)S(1)} %shard_map.118.refs_4_), channel_id=1, source_target_pairs={{0,4},{2,6},{8,0},{10,2},{16,8},{18,10},{24,16},{26,18},{28,24},{3... | collective-permute-start | bytes 786440 | tf_op jit(solution)/shard_map/ppermute | solution.py:208
  4.3 0.7 %copy-start.6 = (s32[1,8,16]{2,1,0:T(8,128)S(1)}, s32[1,8,16]{2,1,0:T(8,128)}, u32[]{:S(2)}) copy-start(s32[1,8,16]{2,1,0:T(8,128)} %param.17) | copy-start | bytes 1540
  4.4 0.7 %copy-start.7 = (s32[1,8,16]{2,1,0:T(8,128)S(1)}, s32[1,8,16]{2,1,0:T(8,128)}, u32[]{:S(2)}) copy-start(s32[1,8,16]{2,1,0:T(8,128)} %param.18) | copy-start | bytes 1540
  5.3 1.6 %collective-permute-start = (s32[4,56,256]{2,1,0:T(8,128)S(1)}, s32[4,56,256]{2,1,0:T(8,128)S(1)}, u32[]{:S(2)}, u32[]{:S(2)}) collective-permute-start(s32[4,56,256]{2,1,0:T(8,128)S(1)} %pad_add_fusion.2), channel_id=1, source_target_pairs={{0,2},{2,0},{4,6},{6,4},{8,10},{10,8},{12,14},{14,12},{16,18},{18,... | collective-permute-start | bytes 688136 | tf_op jit(solution)/shard_map/ppermute | solution.py:211
  6.9 9.5 %collective-permute-start.2 = (f32[512,128]{1,0:T(8,128)S(1)}, f32[512,128]{1,0:T(8,128)S(1)}, u32[]{:S(2)}, u32[]{:S(2)}) collective-permute-start(f32[512,128]{1,0:T(8,128)S(1)} %get-tuple-element.38.refs_3_), channel_id=1, source_target_pairs={{0,8},{2,10},{8,16},{10,18},{16,24},{18,26},{24,28},{26,30},{28,20... | collective-permute-start | bytes 786440 | tf_op jit(solution)/shard_map/ppermute | solution.py:208
  9.0 9.2 %collective-permute-start.4 = (f32[512,128]{1,0:T(8,128)S(1)}, f32[512,128]{1,0:T(8,128)S(1)}, u32[]{:S(2)}, u32[]{:S(2)}) collective-permute-start(f32[512,128]{1,0:T(8,128)S(1)} %get-tuple-element.38.refs_3_), channel_id=1, source_target_pairs={{0,4},{2,6},{8,0},{10,2},{16,8},{18,10},{24,16},{26,18},{28,24},{3... | collective-permute-start | bytes 786440 | tf_op jit(solution)/shard_map/ppermute | solution.py:208
  9.7 14.3 %collective-permute-start.1 = (s32[8,56,256]{2,1,0:T(8,128)S(1)}, s32[8,56,256]{2,1,0:T(8,128)S(1)}, u32[]{:S(2)}, u32[]{:S(2)}) collective-permute-start(s32[8,56,256]{2,1,0:T(8,128)S(1)} %pad_add_fusion.1.refs_2_), channel_id=1, source_target_pairs={{0,1},{1,0},{2,3},{3,2},{4,5},{5,4},{6,7},{7,6},{8,9},{9,8},{10,11... | collective-permute-start | bytes 1376264 | tf_op jit(solution)/shard_map/ppermute | solution.py:214
  11.6 10.3 %collective-permute-start.10 = (f32[512,128]{1,0:T(8,128)S(1)}, f32[512,128]{1,0:T(8,128)S(1)}, u32[]{:S(2)}, u32[]{:S(2)}) collective-permute-start(f32[512,128]{1,0:T(8,128)S(1)} %collective-permute-done.6.refs_6_), channel_id=1, source_target_pairs={{0,8},{2,10},{8,16},{10,18},{16,24},{18,26},{24,28},{26,30},{28,20... | collective-permute-start | bytes 786440 | tf_op jit(solution)/shard_map/ppermute | solution.py:208
  13.2 10.6 %collective-permute-start.11 = (f32[512,128]{1,0:T(8,128)S(1)}, f32[512,128]{1,0:T(8,128)S(1)}, u32[]{:S(2)}, u32[]{:S(2)}) collective-permute-start(f32[512,128]{1,0:T(8,128)S(1)} %collective-permute-done.7.refs_8_), channel_id=1, source_target_pairs={{0,4},{2,6},{8,0},{10,2},{16,8},{18,10},{24,16},{26,18},{28,24},{3... | collective-permute-start | bytes 786440 | tf_op jit(solution)/shard_map/ppermute | solution.py:208
  16.3 11.6 %collective-permute-start.3 = (f32[512,128]{1,0:T(8,128)S(1)}, f32[512,128]{1,0:T(8,128)S(1)}, u32[]{:S(2)}, u32[]{:S(2)}) collective-permute-start(f32[512,128]{1,0:T(8,128)S(1)} %collective-permute-done.2.refs_5_), channel_id=1, source_target_pairs={{0,8},{2,10},{8,16},{10,18},{16,24},{18,26},{24,28},{26,30},{28,20... | collective-permute-start | bytes 786440 | tf_op jit(solution)/shard_map/ppermute | solution.py:208
  18.2 11.2 %collective-permute-start.5 = (f32[512,128]{1,0:T(8,128)S(1)}, f32[512,128]{1,0:T(8,128)S(1)}, u32[]{:S(2)}, u32[]{:S(2)}) collective-permute-start(f32[512,128]{1,0:T(8,128)S(1)} %collective-permute-done.4.refs_7_), channel_id=1, source_target_pairs={{0,4},{2,6},{8,0},{10,2},{16,8},{18,10},{24,16},{26,18},{28,24},{3... | collective-permute-start | bytes 786440 | tf_op jit(solution)/shard_map/ppermute | solution.py:208
  22.0 13.1 %collective-permute-start.14 = (f32[512,128]{1,0:T(8,128)S(1)}, f32[512,128]{1,0:T(8,128)S(1)}, u32[]{:S(2)}, u32[]{:S(2)}) collective-permute-start(f32[512,128]{1,0:T(8,128)S(1)} %collective-permute-done.10.refs_4_), channel_id=1, source_target_pairs={{0,8},{2,10},{8,16},{10,18},{16,24},{18,26},{24,28},{26,30},{28,20... | collective-permute-start | bytes 786440 | tf_op jit(solution)/shard_map/ppermute | solution.py:208
  23.8 12.3 %collective-permute-start.15 = (f32[512,128]{1,0:T(8,128)S(1)}, f32[512,128]{1,0:T(8,128)S(1)}, u32[]{:S(2)}, u32[]{:S(2)}) collective-permute-start(f32[512,128]{1,0:T(8,128)S(1)} %collective-permute-done.11.refs_6_), channel_id=1, source_target_pairs={{0,4},{2,6},{8,0},{10,2},{16,8},{18,10},{24,16},{26,18},{28,24},{3... | collective-permute-start | bytes 786440 | tf_op jit(solution)/shard_map/ppermute | solution.py:208
  29.3 9.5 %collective-permute-start.8 = (f32[512,128]{1,0:T(8,128)S(1)}, f32[512,128]{1,0:T(8,128)S(1)}, u32[]{:S(2)}, u32[]{:S(2)}) collective-permute-start(f32[512,128]{1,0:T(8,128)S(1)} %collective-permute-done.3.refs_3_), channel_id=1, source_target_pairs={{0,8},{2,10},{8,16},{10,18},{16,24},{18,26},{24,28},{26,30},{28,20... | collective-permute-start | bytes 786440 | tf_op jit(solution)/shard_map/ppermute | solution.py:208
  30.9 9.7 %collective-permute-start.9 = (f32[512,128]{1,0:T(8,128)S(1)}, f32[512,128]{1,0:T(8,128)S(1)}, u32[]{:S(2)}, u32[]{:S(2)}) collective-permute-start(f32[512,128]{1,0:T(8,128)S(1)} %collective-permute-done.5.refs_5_), channel_id=1, source_target_pairs={{0,4},{2,6},{8,0},{10,2},{16,8},{18,10},{24,16},{26,18},{28,24},{3... | collective-permute-start | bytes 786440 | tf_op jit(solution)/shard_map/ppermute | solution.py:208
  35.0 11.3 %collective-permute-start.18 = (f32[256,128]{1,0:T(8,128)S(1)}, f32[256,128]{1,0:T(8,128)S(1)}, u32[]{:S(2)}, u32[]{:S(2)}) collective-permute-start(f32[256,128]{1,0:T(8,128)S(1)} %slice.116), channel_id=1, source_target_pairs={{0,8},{2,10},{8,16},{10,18},{16,24},{18,26},{24,28},{26,30},{28,20... | collective-permute-start | bytes 393224 | tf_op jit(solution)/shard_map/ppermute | solution.py:208
  36.1 10.3 %collective-permute-start.19 = (f32[256,128]{1,0:T(8,128)S(1)}, f32[256,128]{1,0:T(8,128)S(1)}, u32[]{:S(2)}, u32[]{:S(2)}) collective-permute-start(f32[256,128]{1,0:T(8,128)S(1)} %slice.117), channel_id=1, source_target_pairs={{0,4},{2,6},{8,0},{10,2},{16,8},{18,10},{24,16},{26,18},{28,24},{3... | collective-permute-start | bytes 393224 | tf_op jit(solution)/shard_map/ppermute | solution.py:208
  40.6 7.9 %collective-permute-start.12 = (f32[256,128]{1,0:T(8,128)S(1)}, f32[256,128]{1,0:T(8,128)S(1)}, u32[]{:S(2)}, u32[]{:S(2)}) collective-permute-start(f32[256,128]{1,0:T(8,128)S(1)} %slice.98), channel_id=1, source_target_pairs={{0,8},{2,10},{8,16},{10,18},{16,24},{18,26},{24,28},{26,30},{28,20... | collective-permute-start | bytes 393224 | tf_op jit(solution)/shard_map/ppermute | solution.py:208
  42.2 6.2 %collective-permute-start.13 = (f32[256,128]{1,0:T(8,128)S(1)}, f32[256,128]{1,0:T(8,128)S(1)}, u32[]{:S(2)}, u32[]{:S(2)}) collective-permute-start(f32[256,128]{1,0:T(8,128)S(1)} %slice.99), channel_id=1, source_target_pairs={{0,4},{2,6},{8,0},{10,2},{16,8},{18,10},{24,16},{26,18},{28,24},{3... | collective-permute-start | bytes 393224 | tf_op jit(solution)/shard_map/ppermute | solution.py:208
  48.4 2.2 %collective-permute-start.20 = (f32[1024,128]{1,0:T(8,128)S(1)}, f32[1024,128]{1,0:T(8,128)S(1)}, u32[]{:S(2)}, u32[]{:S(2)}) collective-permute-start(f32[1024,128]{1,0:T(8,128)S(1)} %get-tuple-element.60), channel_id=1, source_target_pairs={{0,2},{2,0},{4,6},{6,4},{8,10},{10,8},{12,14},{14,12},{16,18},{18,... | collective-permute-start | bytes 1572872 | tf_op jit(solution)/shard_map/ppermute | solution.py:211
  50.5 2.1 %copy-start.1 = (f32[512,256]{1,0:T(8,128)S(1)}, f32[512,256]{1,0:T(8,128)}, u32[]{:S(2)}) copy-start(f32[512,256]{1,0:T(8,128)} %features.2) | copy-start | bytes 1572868
  50.5 2.7 %collective-permute-start.16 = (f32[1024,128]{1,0:T(8,128)S(1)}, f32[1024,128]{1,0:T(8,128)S(1)}, u32[]{:S(2)}, u32[]{:S(2)}) collective-permute-start(f32[1024,128]{1,0:T(8,128)S(1)} %get-tuple-element.56), channel_id=1, source_target_pairs={{0,2},{2,0},{4,6},{6,4},{8,10},{10,8},{12,14},{14,12},{16,18},{18,... | collective-permute-start | bytes 1572872 | tf_op jit(solution)/shard_map/ppermute | solution.py:211
  50.6 2.0 %copy-start.8 = (f32[256]{0:T(256)S(1)}, f32[256]{0:T(256)}, u32[]{:S(2)}) copy-start(f32[256]{0:T(256)} %param.16) | copy-start | bytes 3076
  50.6 9.1 %collective-permute-start.21 = (f32[512,128]{1,0:T(8,128)S(1)}, f32[512,128]{1,0:T(8,128)S(1)}, u32[]{:S(2)}, u32[]{:S(2)}) collective-permute-start(f32[512,128]{1,0:T(8,128)S(1)} %slice_add_fusion), channel_id=1, source_target_pairs={{0,1},{1,0},{2,3},{3,2},{4,5},{5,4},{6,7},{7,6},{8,9},{9,8},{10,11... | collective-permute-start | bytes 786440 | tf_op jit(solution)/shard_map/ppermute | solution.py:214
  53.2 6.6 %copy-start.2 = (f32[256,256]{1,0:T(8,128)S(1)}, f32[256,256]{1,0:T(8,128)}, u32[]{:S(2)}) copy-start(f32[256,256]{1,0:T(8,128)} %param.15) | copy-start | bytes 786436
  53.2 11.9 %collective-permute-start.17 = (f32[512,128]{1,0:T(8,128)S(1)}, f32[512,128]{1,0:T(8,128)S(1)}, u32[]{:S(2)}, u32[]{:S(2)}) collective-permute-start(f32[512,128]{1,0:T(8,128)S(1)} %slice_add_fusion.2), channel_id=1, source_target_pairs={{0,1},{1,0},{2,3},{3,2},{4,5},{5,4},{6,7},{7,6},{8,9},{9,8},{10,11... | collective-permute-start | bytes 786440 | tf_op jit(solution)/shard_map/ppermute | solution.py:214

commit v8 on v7

--- a/solution.py
+++ b/solution.py
@@ -276,7 +276,7 @@
 
     add = functools.partial(add_sources, rows=rows, slots=slots)
 
-    root = jnp.dot(features, root_weight, precision=highest) + bias
+    root = jnp.dot(features, root_weight, precision=final) + bias
 
     half = shard // 2
     later = [lax.optimization_barrier((v, lists))[0] for v in own[:-1]] + own[-1:]

time: 66.7 us -> 67 us (level)
  waiting for transfers between devices: 19.4 us -> 18 us
  Pallas kernels: 19.4 us -> 20.6 us
  starting transfers between devices: 22.9 us -> 23.9 us
    ppermute x16, waiting for transfers between devices: 9.05 us -> 7.61 us  [ring(): return lax.ppermute(value, 'blk', pairs)]
    pallas_call x6, Pallas kernels: 17.1 us -> 18.4 us  [add_sources(): pl.pallas_call(functools.partial(sum_kernel, base, sources, chunks, piece...]
    ppermute x16, starting transfers between devices: 17.5 us -> 18.3 us  [ring(): return lax.ppermute(value, 'blk', pairs)]
  transfers between devices with their start and end apart: 22 -> 22, of which waited for: 7 -> 7; matrix products, arithmetic and copies ran while one was open for 4% -> 3% of each run, Pallas kernels for 27% -> 29%
where the time goes in v8:
time: 67 us; the launch traced here: 66.9 us
  starting transfers between devices  23.9 us (36%)
  Pallas kernels  20.6 us (31%)
  waiting for transfers between devices  18 us (27%)
  matrix products  1.91 us (3%)
  local copies, waits for them, and re-layouts  1.88 us (3%)
    pallas_call x6, Pallas kernels, add_sources(): pl.pallas_call(functools.partial(sum_kernel, base, sources, chunks, piece...  18.4 us
    ppermute x16, starting transfers between devices, ring(): return lax.ppermute(value, 'blk', pairs)  18.3 us
    ppermute x3, waiting for transfers between devices, rep_swap(): return lax.ppermute(value, 'rep', [(0, 1), (1, 0)])  10.3 us
    ppermute x16, waiting for transfers between devices, ring(): return lax.ppermute(value, 'blk', pairs)  7.61 us
    ppermute x3, starting transfers between devices, rep_swap(): return lax.ppermute(value, 'rep', [(0, 1), (1, 0)])  4.88 us
    pallas_call x2, Pallas kernels, scaled_chunk(): pl.pallas_call(scale_kernel, grid=(1,), in_specs=[pl.BlockSpec((tiles, TI...  2.26 us
    dot_general x2, matrix products, on_device(): jnp.dot(mixed, neighbor_weight[f * TILE:(f + 1) * TILE], precision=final)  1.53 us
  transfers between devices with their start and end apart: 22, of which 7 were waited for; matrix products, arithmetic and copies ran while one was open for 3% of the time, Pallas kernels for 29%

profile of v8, /device:TPU:0, one launch (start us, length us, event | category | flops | bytes accessed | tf_op | source)
XLA Modules:
  0.0 66.9 jit_solution(6403297384203288209)
XLA Ops:
  0.0 1.2 %shard_map.118.refs_4_ = f32[512,128]{1,0:T(8,128)S(1)} custom-call(s32[4,128]{1,0:T(4,128)} %bitcast.37, f32[512,256]{1,0:T(8,128)} %features.2), custom_call_target="tpu_custom_call" | custom-call | flops 3000000000 | bytes 1048576 | tf_op jit(solution)/shard_map/pallas_call | solution.py:37
  1.2 3.1 %collective-permute-start.6 = (f32[512,128]{1,0:T(8,128)S(1)}, f32[512,128]{1,0:T(8,128)S(1)}, u32[]{:S(2)}, u32[]{:S(2)}) collective-permute-start(f32[512,128]{1,0:T(8,128)S(1)} %shard_map.118.refs_4_), channel_id=1, source_target_pairs={{0,8},{2,10},{8,16},{10,18},{16,24},{18,26},{24,28},{26,30},{28,20... | collective-permute-start | bytes 786440 | tf_op jit(solution)/shard_map/ppermute | solution.py:208
  4.5 0.5 copy-done.6
  5.7 1.1 %shard_map.119 = (f32[512,128]{1,0:T(8,128)S(1)}, f32[512,128]{1,0:T(8,128)S(1)}) custom-call(s32[4,128]{1,0:T(4,128)} %bitcast.38, f32[512,256]{1,0:T(8,128)} %features.2), custom_call_target="tpu_custom_call" | custom-call | flops 3000000000 | bytes 1048576 | tf_op jit(solution)/shard_map/pallas_call | solution.py:37
  6.9 2.1 %collective-permute-start.2 = (f32[512,128]{1,0:T(8,128)S(1)}, f32[512,128]{1,0:T(8,128)S(1)}, u32[]{:S(2)}, u32[]{:S(2)}) collective-permute-start(f32[512,128]{1,0:T(8,128)S(1)} %get-tuple-element.38.refs_3_), channel_id=1, source_target_pairs={{0,8},{2,10},{8,16},{10,18},{16,24},{18,26},{24,28},{26,30},{28,20... | collective-permute-start | bytes 786440 | tf_op jit(solution)/shard_map/ppermute | solution.py:208
  9.0 0.7 %dynamic-slice_bitcast_fusion.refs_0_ = s32[24]{0:T(128)S(1)} fusion(s32[32,24]{1,0:T(8,128)} %constant.22.clone, s32[]{:T(128)S(6)} %select_n.4), kind=kLoop, calls=%fused_computation.28 | loop fusion | bytes 196 | tf_op jit(solution)/shard_map/jit(dynamic_index_in_dim)/squeeze | solution.py:272
  9.7 2.0 %collective-permute-start.1 = (s32[8,56,256]{2,1,0:T(8,128)S(1)}, s32[8,56,256]{2,1,0:T(8,128)S(1)}, u32[]{:S(2)}, u32[]{:S(2)}) collective-permute-start(s32[8,56,256]{2,1,0:T(8,128)S(1)} %pad_add_fusion.1.refs_2_), channel_id=1, source_target_pairs={{0,1},{1,0},{2,3},{3,2},{4,5},{5,4},{6,7},{7,6},{8,9},{9,8},{10,11... | collective-permute-start | bytes 1376264 | tf_op jit(solution)/shard_map/ppermute | solution.py:214
  11.6 1.6 %collective-permute-start.10 = (f32[512,128]{1,0:T(8,128)S(1)}, f32[512,128]{1,0:T(8,128)S(1)}, u32[]{:S(2)}, u32[]{:S(2)}) collective-permute-start(f32[512,128]{1,0:T(8,128)S(1)} %collective-permute-done.6.refs_6_), channel_id=1, source_target_pairs={{0,8},{2,10},{8,16},{10,18},{16,24},{18,26},{24,28},{26,30},{28,20... | collective-permute-start | bytes 786440 | tf_op jit(solution)/shard_map/ppermute | solution.py:208
  13.7 2.7 %collective-permute-done.2.refs_5_ = f32[512,128]{1,0:T(8,128)S(1)} collective-permute-done((f32[512,128]{1,0:T(8,128)S(1)}, f32[512,128]{1,0:T(8,128)S(1)}, u32[]{:S(2)}, u32[]{:S(2)}) %collective-permute-start.2) | collective-permute-done | bytes 262176 | tf_op jit(solution)/shard_map/ppermute | solution.py:208
  16.3 1.8 %collective-permute-start.3 = (f32[512,128]{1,0:T(8,128)S(1)}, f32[512,128]{1,0:T(8,128)S(1)}, u32[]{:S(2)}, u32[]{:S(2)}) collective-permute-start(f32[512,128]{1,0:T(8,128)S(1)} %collective-permute-done.2.refs_5_), channel_id=1, source_target_pairs={{0,8},{2,10},{8,16},{10,18},{16,24},{18,26},{24,28},{26,30},{28,20... | collective-permute-start | bytes 786440 | tf_op jit(solution)/shard_map/ppermute | solution.py:208
  18.4 3.3 %shard_map.120 = (f32[2,1024,128]{2,1,0:T(8,128)S(1)}, f32[2,1024,128]{2,1,0:T(8,128)S(1)}) custom-call(s32[24]{0:T(128)S(1)} %dynamic-slice_bitcast_fusion.refs_0_, s32[8,128]{1,0:T(8,128)S(1)} %bitcast.30, s32[8,56,256]{2,1,0:T(8,128)S(1)} %pad_add_fusion.1.refs_2_, f32[512,128]{1,0:T(8,128)S(1)} %get-tuple-element.38.refs_3_, ...), custom_call_target="tpu_custom_call" | custom-call | flops 7000000000 | bytes 1048576 | tf_op jit(solution)/shard_map/pallas_call | solution.py:165
  22.0 2.2 %collective-permute-start.14 = (f32[512,128]{1,0:T(8,128)S(1)}, f32[512,128]{1,0:T(8,128)S(1)}, u32[]{:S(2)}, u32[]{:S(2)}) collective-permute-start(f32[512,128]{1,0:T(8,128)S(1)} %collective-permute-done.10.refs_4_), channel_id=1, source_target_pairs={{0,8},{2,10},{8,16},{10,18},{16,24},{18,26},{24,28},{26,30},{28,20... | collective-permute-start | bytes 786440 | tf_op jit(solution)/shard_map/ppermute | solution.py:208
  24.2 0.6 collective-permute-start.15
  24.9 3.2 %shard_map.121 = (f32[2,1024,128]{2,1,0:T(8,128)S(1)}, f32[2,1024,128]{2,1,0:T(8,128)S(1)}) custom-call(s32[24]{0:T(128)S(1)} %dynamic-slice_bitcast_fusion.refs_0_, s32[16,128]{1,0:T(8,128)S(1)} %bitcast.25, s32[16,56,256]{2,1,0:T(8,128)S(1)} %pad_add_fusion.refs_2_, ...), custom_call_target="tpu_custom_call", output_to_operand_aliasing={{0}: (9, {}), {1}: (10, {})} | custom-call | flops 7000000000 | bytes 1048576 | tf_op jit(solution)/shard_map/pallas_call | solution.py:165
  28.1 1.2 %collective-permute-done.5.refs_5_ = f32[512,128]{1,0:T(8,128)S(1)} collective-permute-done((f32[512,128]{1,0:T(8,128)S(1)}, f32[512,128]{1,0:T(8,128)S(1)}, u32[]{:S(2)}, u32[]{:S(2)}) %collective-permute-start.5) | collective-permute-done | bytes 262176 | tf_op jit(solution)/shard_map/ppermute | solution.py:208
  29.3 1.6 %collective-permute-start.8 = (f32[512,128]{1,0:T(8,128)S(1)}, f32[512,128]{1,0:T(8,128)S(1)}, u32[]{:S(2)}, u32[]{:S(2)}) collective-permute-start(f32[512,128]{1,0:T(8,128)S(1)} %collective-permute-done.3.refs_3_), channel_id=1, source_target_pairs={{0,8},{2,10},{8,16},{10,18},{16,24},{18,26},{24,28},{26,30},{28,20... | collective-permute-start | bytes 786440 | tf_op jit(solution)/shard_map/ppermute | solution.py:208
  31.4 3.6 %shard_map.122 = (f32[2,1024,128]{2,1,0:T(8,128)S(1)}, f32[2,1024,128]{2,1,0:T(8,128)S(1)}) custom-call(s32[24]{0:T(128)S(1)} %dynamic-slice_bitcast_fusion.refs_0_, s32[16,128]{1,0:T(8,128)S(1)} %bitcast.26, s32[16,56,256]{2,1,0:T(8,128)S(1)} %pad_add_fusion.refs_2_, ...), custom_call_target="tpu_custom_call", output_to_operand_aliasing={{0}: (7, {}), {1}: (8, {})} | custom-call | flops 5000000000 | bytes 1048576 | tf_op jit(solution)/shard_map/pallas_call | solution.py:165
  35.0 1.6 %collective-permute-start.18 = (f32[256,128]{1,0:T(8,128)S(1)}, f32[256,128]{1,0:T(8,128)S(1)}, u32[]{:S(2)}, u32[]{:S(2)}) collective-permute-start(f32[256,128]{1,0:T(8,128)S(1)} %slice.116), channel_id=1, source_target_pairs={{0,8},{2,10},{8,16},{10,18},{16,24},{18,26},{24,28},{26,30},{28,20... | collective-permute-start | bytes 393224 | tf_op jit(solution)/shard_map/ppermute | solution.py:208
  36.7 0.5 collective-permute-start.19
  37.2 1.6 %collective-permute-done.8.refs_3_ = f32[512,128]{1,0:T(8,128)S(1)} collective-permute-done((f32[512,128]{1,0:T(8,128)S(1)}, f32[512,128]{1,0:T(8,128)S(1)}, u32[]{:S(2)}, u32[]{:S(2)}) %collective-permute-start.8) | collective-permute-done | bytes 262176 | tf_op jit(solution)/shard_map/ppermute | solution.py:208
  38.8 1.8 %collective-permute-done.9.refs_5_ = f32[512,128]{1,0:T(8,128)S(1)} collective-permute-done((f32[512,128]{1,0:T(8,128)S(1)}, f32[512,128]{1,0:T(8,128)S(1)}, u32[]{:S(2)}, u32[]{:S(2)}) %collective-permute-start.9) | collective-permute-done | bytes 262176 | tf_op jit(solution)/shard_map/ppermute | solution.py:208
  40.6 1.6 %collective-permute-start.12 = (f32[256,128]{1,0:T(8,128)S(1)}, f32[256,128]{1,0:T(8,128)S(1)}, u32[]{:S(2)}, u32[]{:S(2)}) collective-permute-start(f32[256,128]{1,0:T(8,128)S(1)} %slice.98), channel_id=1, source_target_pairs={{0,8},{2,10},{8,16},{10,18},{16,24},{18,26},{24,28},{26,30},{28,20... | collective-permute-start | bytes 393224 | tf_op jit(solution)/shard_map/ppermute | solution.py:208
  42.2 0.5 collective-permute-start.13
  42.7 4.3 %shard_map.123 = (f32[2,1024,128]{2,1,0:T(8,128)S(1)}, f32[2,1024,128]{2,1,0:T(8,128)S(1)}) custom-call(s32[24]{0:T(128)S(1)} %dynamic-slice_bitcast_fusion.refs_0_, s32[16,128]{1,0:T(8,128)S(1)} %bitcast.27, s32[16,56,256]{2,1,0:T(8,128)S(1)} %pad_add_fusion.refs_2_, ...), custom_call_target="tpu_custom_call", output_to_operand_aliasing={{0}: (7, {}), {1}: (8, {})} | custom-call | flops 5000000000 | bytes 1048576 | tf_op jit(solution)/shard_map/pallas_call | solution.py:165
  47.0 2.0 %shard_map.125 = (f32[1024,128]{1,0:T(8,128)S(1)}, f32[1024,128]{1,0:T(8,128)S(1)}) custom-call(s32[24]{0:T(128)S(1)} %dynamic-slice_bitcast_fusion.refs_0_, s32[16,128]{1,0:T(8,128)S(1)} %bitcast.28, s32[16,56,256]{2,1,0:T(8,128)S(1)} %pad_add_fusion.refs_2_, f32[256,128]{1,0:T(8,128)S(1)} %collective-permute-done.18.refs_3_, ...), custom_call_target="tpu_custom_call" | custom-call | flops 4000000000 | bytes 1048576 | tf_op jit(solution)/shard_map/pallas_call | solution.py:165
  49.1 2.0 %shard_map.124 = (f32[1024,128]{1,0:T(8,128)S(1)}, f32[1024,128]{1,0:T(8,128)S(1)}) custom-call(s32[24]{0:T(128)S(1)} %dynamic-slice_bitcast_fusion.refs_0_, s32[16,128]{1,0:T(8,128)S(1)} %bitcast.29, s32[16,56,256]{2,1,0:T(8,128)S(1)} %pad_add_fusion.refs_2_, f32[256,128]{1,0:T(8,128)S(1)} %collective-permute-done.12.refs_3_, ...), custom_call_target="tpu_custom_call" | custom-call | flops 4000000000 | bytes 1048576 | tf_op jit(solution)/shard_map/pallas_call | solution.py:165
  51.1 0.5 collective-permute-start.16
  51.7 1.5 %collective-permute-start.21 = (f32[512,128]{1,0:T(8,128)S(1)}, f32[512,128]{1,0:T(8,128)S(1)}, u32[]{:S(2)}, u32[]{:S(2)}) collective-permute-start(f32[512,128]{1,0:T(8,128)S(1)} %slice_add_fusion), channel_id=1, source_target_pairs={{0,1},{1,0},{2,3},{3,2},{4,5},{5,4},{6,7},{7,6},{8,9},{9,8},{10,11... | collective-permute-start | bytes 786440 | tf_op jit(solution)/shard_map/ppermute | solution.py:214
  53.6 1.4 %collective-permute-start.17 = (f32[512,128]{1,0:T(8,128)S(1)}, f32[512,128]{1,0:T(8,128)S(1)}, u32[]{:S(2)}, u32[]{:S(2)}) collective-permute-start(f32[512,128]{1,0:T(8,128)S(1)} %slice_add_fusion.2), channel_id=1, source_target_pairs={{0,1},{1,0},{2,3},{3,2},{4,5},{5,4},{6,7},{7,6},{8,9},{9,8},{10,11... | collective-permute-start | bytes 786440 | tf_op jit(solution)/shard_map/ppermute | solution.py:214
  55.1 5.8 %collective-permute-done.21 = f32[512,128]{1,0:T(8,128)S(1)} collective-permute-done((f32[512,128]{1,0:T(8,128)S(1)}, f32[512,128]{1,0:T(8,128)S(1)}, u32[]{:S(2)}, u32[]{:S(2)}) %collective-permute-start.21) | collective-permute-done | bytes 262176 | tf_op jit(solution)/shard_map/ppermute | solution.py:214
  61.3 4.5 %collective-permute-done.17 = f32[512,128]{1,0:T(8,128)S(1)} collective-permute-done((f32[512,128]{1,0:T(8,128)S(1)}, f32[512,128]{1,0:T(8,128)S(1)}, u32[]{:S(2)}, u32[]{:S(2)}) %collective-permute-start.17) | collective-permute-done | bytes 262176 | tf_op jit(solution)/shard_map/ppermute | solution.py:214
  65.7 1.2 %fusion.1 = f32[512,256]{1,0:T(8,128)} fusion(f32[512,256]{1,0:T(8,128)S(1)} %fusion.4, f32[512,256]{1,0:T(8,128)S(1)} %convolution_add_fusion.1, f32[512,128]{1,0:T(8,128)S(1)} %get-tuple-element.57, f32[512,128]{1,0:T(8,128)S(1)} %collective-permute-done.17, f32[1024,128]{1,0:T(8,128)S(1)} %collective-permute-done.16, ...), kind=kOutput, calls=%fused_computation.2 | convolution fusion | flops 101253120 | bytes 2752512 | tf_op jit(solution)/shard_map/dot_general | solution.py:313
  (72 shorter events, 3.4 us)
Async XLA Ops:
  0.0 53.2 %copy-start = (f32[256,256]{1,0:T(8,128)S(1)}, f32[256,256]{1,0:T(8,128)}, u32[]{:S(2)}) copy-start(f32[256,256]{1,0:T(8,128)} %param.14) | copy-start | bytes 786436
  0.0 4.3 %copy-start.3 = (s32[1,8,16,256]{3,2,1,0:T(8,128)S(1)}, s32[1,8,16,256]{3,2,1,0:T(8,128)}, u32[]{:S(2)}) copy-start(s32[1,8,16,256]{3,2,1,0:T(8,128)} %param.20) | copy-start | bytes 393220
  0.0 4.3 %copy-start.9 = (s32[1,8]{1,0:T(1,128)S(1)}, s32[1,8]{1,0:T(1,128)}, u32[]{:S(2)}) copy-start(s32[1,8]{1,0:T(1,128)} %param.19) | copy-start | bytes 100
  1.2 4.0 %copy-start.4 = (s32[1,8,16,256]{3,2,1,0:T(8,128)S(1)}, s32[1,8,16,256]{3,2,1,0:T(8,128)}, u32[]{:S(2)}) copy-start(s32[1,8,16,256]{3,2,1,0:T(8,128)} %param.22) | copy-start | bytes 393220
  1.2 4.0 %copy-start.5 = (s32[1,8,16,256]{3,2,1,0:T(8,128)S(1)}, s32[1,8,16,256]{3,2,1,0:T(8,128)}, u32[]{:S(2)}) copy-start(s32[1,8,16,256]{3,2,1,0:T(8,128)} %param.21) | copy-start | bytes 393220
  1.2 10.4 %collective-permute-start.6 = (f32[512,128]{1,0:T(8,128)S(1)}, f32[512,128]{1,0:T(8,128)S(1)}, u32[]{:S(2)}, u32[]{:S(2)}) collective-permute-start(f32[512,128]{1,0:T(8,128)S(1)} %shard_map.118.refs_4_), channel_id=1, source_target_pairs={{0,8},{2,10},{8,16},{10,18},{16,24},{18,26},{24,28},{26,30},{28,20... | collective-permute-start | bytes 786440 | tf_op jit(solution)/shard_map/ppermute | solution.py:208
  4.3 8.9 %collective-permute-start.7 = (f32[512,128]{1,0:T(8,128)S(1)}, f32[512,128]{1,0:T(8,128)S(1)}, u32[]{:S(2)}, u32[]{:S(2)}) collective-permute-start(f32[512,128]{1,0:T(8,128)S(1)} %shard_map.118.refs_4_), channel_id=1, source_target_pairs={{0,4},{2,6},{8,0},{10,2},{16,8},{18,10},{24,16},{26,18},{28,24},{3... | collective-permute-start | bytes 786440 | tf_op jit(solution)/shard_map/ppermute | solution.py:208
  4.3 0.7 %copy-start.6 = (s32[1,8,16]{2,1,0:T(8,128)S(1)}, s32[1,8,16]{2,1,0:T(8,128)}, u32[]{:S(2)}) copy-start(s32[1,8,16]{2,1,0:T(8,128)} %param.17) | copy-start | bytes 1540
  4.4 0.7 %copy-start.7 = (s32[1,8,16]{2,1,0:T(8,128)S(1)}, s32[1,8,16]{2,1,0:T(8,128)}, u32[]{:S(2)}) copy-start(s32[1,8,16]{2,1,0:T(8,128)} %param.18) | copy-start | bytes 1540
  5.3 1.6 %collective-permute-start = (s32[4,56,256]{2,1,0:T(8,128)S(1)}, s32[4,56,256]{2,1,0:T(8,128)S(1)}, u32[]{:S(2)}, u32[]{:S(2)}) collective-permute-start(s32[4,56,256]{2,1,0:T(8,128)S(1)} %pad_add_fusion.2), channel_id=1, source_target_pairs={{0,2},{2,0},{4,6},{6,4},{8,10},{10,8},{12,14},{14,12},{16,18},{18,... | collective-permute-start | bytes 688136 | tf_op jit(solution)/shard_map/ppermute | solution.py:211
  6.9 9.5 %collective-permute-start.2 = (f32[512,128]{1,0:T(8,128)S(1)}, f32[512,128]{1,0:T(8,128)S(1)}, u32[]{:S(2)}, u32[]{:S(2)}) collective-permute-start(f32[512,128]{1,0:T(8,128)S(1)} %get-tuple-element.38.refs_3_), channel_id=1, source_target_pairs={{0,8},{2,10},{8,16},{10,18},{16,24},{18,26},{24,28},{26,30},{28,20... | collective-permute-start | bytes 786440 | tf_op jit(solution)/shard_map/ppermute | solution.py:208
  9.0 9.2 %collective-permute-start.4 = (f32[512,128]{1,0:T(8,128)S(1)}, f32[512,128]{1,0:T(8,128)S(1)}, u32[]{:S(2)}, u32[]{:S(2)}) collective-permute-start(f32[512,128]{1,0:T(8,128)S(1)} %get-tuple-element.38.refs_3_), channel_id=1, source_target_pairs={{0,4},{2,6},{8,0},{10,2},{16,8},{18,10},{24,16},{26,18},{28,24},{3... | collective-permute-start | bytes 786440 | tf_op jit(solution)/shard_map/ppermute | solution.py:208
  9.7 15.1 %collective-permute-start.1 = (s32[8,56,256]{2,1,0:T(8,128)S(1)}, s32[8,56,256]{2,1,0:T(8,128)S(1)}, u32[]{:S(2)}, u32[]{:S(2)}) collective-permute-start(s32[8,56,256]{2,1,0:T(8,128)S(1)} %pad_add_fusion.1.refs_2_), channel_id=1, source_target_pairs={{0,1},{1,0},{2,3},{3,2},{4,5},{5,4},{6,7},{7,6},{8,9},{9,8},{10,11... | collective-permute-start | bytes 1376264 | tf_op jit(solution)/shard_map/ppermute | solution.py:214
  11.6 10.3 %collective-permute-start.10 = (f32[512,128]{1,0:T(8,128)S(1)}, f32[512,128]{1,0:T(8,128)S(1)}, u32[]{:S(2)}, u32[]{:S(2)}) collective-permute-start(f32[512,128]{1,0:T(8,128)S(1)} %collective-permute-done.6.refs_6_), channel_id=1, source_target_pairs={{0,8},{2,10},{8,16},{10,18},{16,24},{18,26},{24,28},{26,30},{28,20... | collective-permute-start | bytes 786440 | tf_op jit(solution)/shard_map/ppermute | solution.py:208
  13.2 11.0 %collective-permute-start.11 = (f32[512,128]{1,0:T(8,128)S(1)}, f32[512,128]{1,0:T(8,128)S(1)}, u32[]{:S(2)}, u32[]{:S(2)}) collective-permute-start(f32[512,128]{1,0:T(8,128)S(1)} %collective-permute-done.7.refs_8_), channel_id=1, source_target_pairs={{0,4},{2,6},{8,0},{10,2},{16,8},{18,10},{24,16},{26,18},{28,24},{3... | collective-permute-start | bytes 786440 | tf_op jit(solution)/shard_map/ppermute | solution.py:208
  16.3 11.8 %collective-permute-start.3 = (f32[512,128]{1,0:T(8,128)S(1)}, f32[512,128]{1,0:T(8,128)S(1)}, u32[]{:S(2)}, u32[]{:S(2)}) collective-permute-start(f32[512,128]{1,0:T(8,128)S(1)} %collective-permute-done.2.refs_5_), channel_id=1, source_target_pairs={{0,8},{2,10},{8,16},{10,18},{16,24},{18,26},{24,28},{26,30},{28,20... | collective-permute-start | bytes 786440 | tf_op jit(solution)/shard_map/ppermute | solution.py:208
  18.2 11.2 %collective-permute-start.5 = (f32[512,128]{1,0:T(8,128)S(1)}, f32[512,128]{1,0:T(8,128)S(1)}, u32[]{:S(2)}, u32[]{:S(2)}) collective-permute-start(f32[512,128]{1,0:T(8,128)S(1)} %collective-permute-done.4.refs_7_), channel_id=1, source_target_pairs={{0,4},{2,6},{8,0},{10,2},{16,8},{18,10},{24,16},{26,18},{28,24},{3... | collective-permute-start | bytes 786440 | tf_op jit(solution)/shard_map/ppermute | solution.py:208
  22.0 13.1 %collective-permute-start.14 = (f32[512,128]{1,0:T(8,128)S(1)}, f32[512,128]{1,0:T(8,128)S(1)}, u32[]{:S(2)}, u32[]{:S(2)}) collective-permute-start(f32[512,128]{1,0:T(8,128)S(1)} %collective-permute-done.10.refs_4_), channel_id=1, source_target_pairs={{0,8},{2,10},{8,16},{10,18},{16,24},{18,26},{24,28},{26,30},{28,20... | collective-permute-start | bytes 786440 | tf_op jit(solution)/shard_map/ppermute | solution.py:208
  24.2 12.5 %collective-permute-start.15 = (f32[512,128]{1,0:T(8,128)S(1)}, f32[512,128]{1,0:T(8,128)S(1)}, u32[]{:S(2)}, u32[]{:S(2)}) collective-permute-start(f32[512,128]{1,0:T(8,128)S(1)} %collective-permute-done.11.refs_6_), channel_id=1, source_target_pairs={{0,4},{2,6},{8,0},{10,2},{16,8},{18,10},{24,16},{26,18},{28,24},{3... | collective-permute-start | bytes 786440 | tf_op jit(solution)/shard_map/ppermute | solution.py:208
  29.3 9.5 %collective-permute-start.8 = (f32[512,128]{1,0:T(8,128)S(1)}, f32[512,128]{1,0:T(8,128)S(1)}, u32[]{:S(2)}, u32[]{:S(2)}) collective-permute-start(f32[512,128]{1,0:T(8,128)S(1)} %collective-permute-done.3.refs_3_), channel_id=1, source_target_pairs={{0,8},{2,10},{8,16},{10,18},{16,24},{18,26},{24,28},{26,30},{28,20... | collective-permute-start | bytes 786440 | tf_op jit(solution)/shard_map/ppermute | solution.py:208
  30.9 9.7 %collective-permute-start.9 = (f32[512,128]{1,0:T(8,128)S(1)}, f32[512,128]{1,0:T(8,128)S(1)}, u32[]{:S(2)}, u32[]{:S(2)}) collective-permute-start(f32[512,128]{1,0:T(8,128)S(1)} %collective-permute-done.5.refs_5_), channel_id=1, source_target_pairs={{0,4},{2,6},{8,0},{10,2},{16,8},{18,10},{24,16},{26,18},{28,24},{3... | collective-permute-start | bytes 786440 | tf_op jit(solution)/shard_map/ppermute | solution.py:208
  35.0 12.0 %collective-permute-start.18 = (f32[256,128]{1,0:T(8,128)S(1)}, f32[256,128]{1,0:T(8,128)S(1)}, u32[]{:S(2)}, u32[]{:S(2)}) collective-permute-start(f32[256,128]{1,0:T(8,128)S(1)} %slice.116), channel_id=1, source_target_pairs={{0,8},{2,10},{8,16},{10,18},{16,24},{18,26},{24,28},{26,30},{28,20... | collective-permute-start | bytes 393224 | tf_op jit(solution)/shard_map/ppermute | solution.py:208
  36.7 10.3 %collective-permute-start.19 = (f32[256,128]{1,0:T(8,128)S(1)}, f32[256,128]{1,0:T(8,128)S(1)}, u32[]{:S(2)}, u32[]{:S(2)}) collective-permute-start(f32[256,128]{1,0:T(8,128)S(1)} %slice.117), channel_id=1, source_target_pairs={{0,4},{2,6},{8,0},{10,2},{16,8},{18,10},{24,16},{26,18},{28,24},{3... | collective-permute-start | bytes 393224 | tf_op jit(solution)/shard_map/ppermute | solution.py:208
  40.6 8.5 %collective-permute-start.12 = (f32[256,128]{1,0:T(8,128)S(1)}, f32[256,128]{1,0:T(8,128)S(1)}, u32[]{:S(2)}, u32[]{:S(2)}) collective-permute-start(f32[256,128]{1,0:T(8,128)S(1)} %slice.98), channel_id=1, source_target_pairs={{0,8},{2,10},{8,16},{10,18},{16,24},{18,26},{24,28},{26,30},{28,20... | collective-permute-start | bytes 393224 | tf_op jit(solution)/shard_map/ppermute | solution.py:208
  42.2 6.9 %collective-permute-start.13 = (f32[256,128]{1,0:T(8,128)S(1)}, f32[256,128]{1,0:T(8,128)S(1)}, u32[]{:S(2)}, u32[]{:S(2)}) collective-permute-start(f32[256,128]{1,0:T(8,128)S(1)} %slice.99), channel_id=1, source_target_pairs={{0,4},{2,6},{8,0},{10,2},{16,8},{18,10},{24,16},{26,18},{28,24},{3... | collective-permute-start | bytes 393224 | tf_op jit(solution)/shard_map/ppermute | solution.py:208
  49.0 2.6 %collective-permute-start.20 = (f32[1024,128]{1,0:T(8,128)S(1)}, f32[1024,128]{1,0:T(8,128)S(1)}, u32[]{:S(2)}, u32[]{:S(2)}) collective-permute-start(f32[1024,128]{1,0:T(8,128)S(1)} %get-tuple-element.60), channel_id=1, source_target_pairs={{0,2},{2,0},{4,6},{6,4},{8,10},{10,8},{12,14},{14,12},{16,18},{18,... | collective-permute-start | bytes 1572872 | tf_op jit(solution)/shard_map/ppermute | solution.py:211
  51.1 2.1 %copy-start.1 = (f32[512,256]{1,0:T(8,128)S(1)}, f32[512,256]{1,0:T(8,128)}, u32[]{:S(2)}) copy-start(f32[512,256]{1,0:T(8,128)} %features.2) | copy-start | bytes 1572868
  51.1 2.5 %collective-permute-start.16 = (f32[1024,128]{1,0:T(8,128)S(1)}, f32[1024,128]{1,0:T(8,128)S(1)}, u32[]{:S(2)}, u32[]{:S(2)}) collective-permute-start(f32[1024,128]{1,0:T(8,128)S(1)} %get-tuple-element.56), channel_id=1, source_target_pairs={{0,2},{2,0},{4,6},{6,4},{8,10},{10,8},{12,14},{14,12},{16,18},{18,... | collective-permute-start | bytes 1572872 | tf_op jit(solution)/shard_map/ppermute | solution.py:211
  51.6 1.5 %copy-start.8 = (f32[256]{0:T(256)S(1)}, f32[256]{0:T(256)}, u32[]{:S(2)}) copy-start(f32[256]{0:T(256)} %param.16) | copy-start | bytes 3076
  51.7 9.2 %collective-permute-start.21 = (f32[512,128]{1,0:T(8,128)S(1)}, f32[512,128]{1,0:T(8,128)S(1)}, u32[]{:S(2)}, u32[]{:S(2)}) collective-permute-start(f32[512,128]{1,0:T(8,128)S(1)} %slice_add_fusion), channel_id=1, source_target_pairs={{0,1},{1,0},{2,3},{3,2},{4,5},{5,4},{6,7},{7,6},{8,9},{9,8},{10,11... | collective-permute-start | bytes 786440 | tf_op jit(solution)/shard_map/ppermute | solution.py:214
  53.6 7.3 %copy-start.2 = (f32[256,256]{1,0:T(8,128)S(1)}, f32[256,256]{1,0:T(8,128)}, u32[]{:S(2)}) copy-start(f32[256,256]{1,0:T(8,128)} %param.15) | copy-start | bytes 786436
  53.6 12.1 %collective-permute-start.17 = (f32[512,128]{1,0:T(8,128)S(1)}, f32[512,128]{1,0:T(8,128)S(1)}, u32[]{:S(2)}, u32[]{:S(2)}) collective-permute-start(f32[512,128]{1,0:T(8,128)S(1)} %slice_add_fusion.2), channel_id=1, source_target_pairs={{0,1},{1,0},{2,3},{3,2},{4,5},{5,4},{6,7},{7,6},{8,9},{9,8},{10,11... | collective-permute-start | bytes 786440 | tf_op jit(solution)/shard_map/ppermute | solution.py:214
